TPU v7x, 512 devices: a whole 4x8x8 slice. The times are simulated.
512 devices in a mesh: cells: 32 (over y, z_hi), bands: 16 (over x, z_lo, core).
Axes of the slice: x: 4, y: 8, z: 8 (z_hi: 4, z_lo: 2; z = z_hi * 2 + z_lo), core: 2. Of those that a mesh axis runs over, the one named last changes fastest.
Arguments:
- cur_block: bfloat16 [32, 1048576], P(None, ('cells', 'bands')), may hold values from -6 to 6
- stored_blocks: bfloat16 [64, 1048576], P('bands', 'cells'), may hold values from -6 to 6
- cell_potential: float32 [125, 16384], P(None, ('cells', 'bands')), may hold values from 0.1 to 2
- connectivity: int32 [125, 16384], P(None, ('cells', 'bands')), may hold values from 0 to 2311, as said below
Outputs:
- filtered_block: bfloat16 [32, 1048576], P(None, ('cells', 'bands'))
- correlation: float32 [64, 32], P('bands', 'cells')
Inputs may be any that keep to these rules, and one draw needn't show every extreme that they name: `connectivity`: column e of device d (columns d * 32 to (d + 1) * 32 - 1) lists one of the device's 32 cells, each cell once, in an order drawn from the seed; for the cell at cell position (i, j, l), 0 <= i < 2, 0 <= j < 4, 0 <= l < 4, row k = 25 a + 5 b + c holds (((4 i + a) mod 8) (17) + 4 j + b) (17) + 4 l + c.
All inputs are finite; a program needn't handle non-finite values.
Results may differ from a plain program's by a relative error of at most 0.012.
The roundings to bfloat16 on the way count: a program that leaves them out, or rounds other values in their place, can miss the bound.
Values may be sent and summed in bfloat16 or wider, within the bound.
No kernel may reach another device: no remote copies, remote signals or barrier semaphores. Data moves between devices by JAX's collectives and lax.ppermute only.
A program may use at most 64 MiB of HBM per device.

v0:
```python
import math

import jax
import jax.numpy as jnp
import numpy as np
from jax import lax
from jax.sharding import PartitionSpec as P

NWF = 32
DEGREE = 4
STEPS = 2
NXL = 8
NYL = 16
NZL = 16
CELLS_DEV = 32
NODES_DEV = 2048
NE = 2312


def passed_along(block, axis, distance):
    devices = range(lax.axis_size(axis))
    route = [((i - distance) % len(devices), i) for i in devices]
    return lax.ppermute(block, axis, route)


def kinetic_table():
    points = [-1.0, -math.sqrt(3.0 / 7.0), 0.0, math.sqrt(3.0 / 7.0), 1.0]
    weights = [0.1, 49.0 / 90.0, 32.0 / 45.0, 49.0 / 90.0, 0.1]
    scales = []
    for row in range(5):
        prod_val = 1.0
        for other in range(5):
            if other != row:
                prod_val = prod_val * (points[row] - points[other])
        scales.append(prod_val)
    deriv = [[0.0] * 5 for row in range(5)]
    for row in range(5):
        for col in range(5):
            if row != col:
                deriv[row][col] = scales[row] / scales[col] / (points[row] - points[col])
            else:
                total = 0.0
                for other in range(5):
                    if other != row:
                        total = total + 1.0 / (points[row] - points[other])
                deriv[row][col] = total
    stiff_one = [
        [sum((deriv[i][a] * weights[i] * deriv[i][b] for i in range(5))) for b in range(5)]
        for a in range(5)
    ]
    mass_one = [[weights[a] if a == b else 0.0 for b in range(5)] for a in range(5)]
    table = [[0.0] * 125 for row in range(125)]
    for k in range(125):
        ka, kb, kc = (k // 25, k // 5 % 5, k % 5)
        for j in range(125):
            ja, jb, jc = (j // 25, j // 5 % 5, j % 5)
            table[k][j] = 0.5 * (
                stiff_one[ka][ja] * mass_one[kb][jb] * mass_one[kc][jc]
                + mass_one[ka][ja] * stiff_one[kb][jb] * mass_one[kc][jc]
                + mass_one[ka][ja] * mass_one[kb][jb] * stiff_one[kc][jc]
            )
    assembled = [dict() for row in range(512)]
    for cell_x in range(2):
        for cell_y in range(2):
            for cell_z in range(2):
                global_ids = []
                for k in range(125):
                    node_x = (4 * cell_x + k // 25) % 8
                    node_y = (4 * cell_y + k // 5 % 5) % 8
                    node_z = (4 * cell_z + k % 5) % 8
                    global_ids.append((node_x * 8 + node_y) * 8 + node_z)
                for k in range(125):
                    row_map = assembled[global_ids[k]]
                    for j in range(125):
                        target = global_ids[j]
                        row_map[target] = row_map.get(target, 0.0) + table[k][j]
    largest = 0.0
    for row_map in assembled:
        total = sum((abs(value) for value in row_map.values()))
        largest = max(largest, total)
    bound = largest + 8.0 * 2.0
    return (np.array(table), float(0.55 * bound), float(0.45 * bound))


def apply_op(values, flat_idx, potential, kinetic):
    upper_z = passed_along(values[:, :, :, 0], "cells", -1)
    extended = jnp.concatenate([values, upper_z[..., None]], axis=3)
    upper_y = passed_along(extended[:, :, 0, :], "bands", -1)
    extended = jnp.concatenate([extended, upper_y[:, :, None, :]], axis=2)
    flat_vals = extended.reshape(NWF, NE)
    cell_vals = jnp.take(flat_vals, flat_idx, axis=1).reshape(NWF, 125, CELLS_DEV)
    product = jnp.einsum("kj,wjc->wkc", kinetic, cell_vals, preferred_element_type=jnp.float32)
    product = product + potential[None] * cell_vals.astype(jnp.float32)
    summed = jnp.zeros((NWF, NE), jnp.float32).at[:, flat_idx].add(product.reshape(NWF, -1))
    summed = summed.reshape(NWF, NXL, NYL + 1, NZL + 1)
    back_y = passed_along(summed[:, :, NYL, :], "bands", 1)
    summed = summed[:, :, :NYL, :].at[:, :, 0, :].add(back_y)
    back_z = passed_along(summed[:, :, :, NZL], "cells", 1)
    return summed[:, :, :, :NZL].at[:, :, :, 0].add(back_z)


def shards(cur_block, stored_blocks, cell_potential, connectivity):
    table, centre, half = kinetic_table()
    kinetic = jnp.asarray(table, jnp.float32).astype(jnp.bfloat16)
    flat_idx = connectivity.reshape(-1)
    block = cur_block.reshape(NWF, NXL, NYL, NZL)
    for pass_idx in range(STEPS):
        previous = block
        applied = apply_op(previous, flat_idx, cell_potential, kinetic)
        current = ((applied - centre * previous.astype(jnp.float32)) / half).astype(jnp.bfloat16)
        for order_idx in range(1, DEGREE):
            applied = apply_op(current, flat_idx, cell_potential, kinetic)
            following = 2.0 * (
                (applied - centre * current.astype(jnp.float32)) / half
            ) - previous.astype(jnp.float32)
            previous, current = (current, following.astype(jnp.bfloat16))
        block = current
    filtered = block.reshape(NWF, NODES_DEV)
    nodes_total = NODES_DEV * lax.axis_size("cells") * lax.axis_size("bands")
    factor = 1.0 / math.sqrt(nodes_total)
    contract = (((1,), (1,)), ((), ()))
    partial_sum = lax.dot_general(
        stored_blocks,
        lax.all_gather(filtered, "bands", axis=1, tiled=True),
        contract,
        preferred_element_type=jnp.float32,
    )
    correlation = lax.psum_scatter(partial_sum * factor, "cells", scatter_dimension=1, tiled=True)
    return (filtered, correlation)


def solution(mesh):
    in_specs = (
        P(None, ("cells", "bands")),
        P("bands", "cells"),
        P(None, ("cells", "bands")),
        P(None, ("cells", "bands")),
    )
    out_specs = (P(None, ("cells", "bands")), P("bands", "cells"))
    return jax.shard_map(shards, mesh=mesh, in_specs=in_specs, out_specs=out_specs, check_vma=False)
```

profile of v0, /device:TPU:2, one launch (start us, length us, event | category | flops | bytes accessed | tf_op | source)
XLA Modules:
  0.0 834.5 jit_solution(13871634325130141281)
XLA Ops:
  8.5 13.8 %collective-permute-start = (bf16[32,8,16]{0,2,1:T(8,128)(2,1)S(1)}, bf16[32,8,16]{0,2,1:T(8,128)(2,1)S(1)}, u32[]{:S(2)}, u32[]{:S(2)}) collective-permute-start(bf16[32,8,16]{0,2,1:T(8,128)(2,1)S(1)} %bitcast.322), channel_id=1, source_target_pairs={{16,0},{32,16},{48,32},{64,48},{80,64},{96,80},{112,96},{128,112},... | collective-permute-start | bytes 24584 | tf_op jit(solution)/shard_map/ppermute | solution.py:23
  28.3 12.3 %gather_fusion = bf16[4000,32]{1,0:T(8,128)(2,1)S(1)} fusion(bf16[32,2312]{0,1:T(8,128)(2,1)S(1)} %reshape.696, s32[4096]{0:T(1024)S(1)} %pad_clamp_fusion), kind=kCustom, calls=%fused_computation.clone | custom fusion | bytes 528000 | tf_op jit(solution)/shard_map/jit(_take)/gather | solution.py:91
  46.7 23.8 %scatter_custom_fusion = f32[32,2312]{0,1:T(8,128)} fusion(s32[4000]{0:T(1024)S(1)} %bitcast.338, f32[4000,32]{1,0:T(8,128)S(1)} %copy.277, f32[]{:T(128)} %constant.364.clone.1), kind=kCustom, calls=%fused_computation.96 | custom fusion | flops 128000 | bytes 295940 | tf_op jit(solution)/shard_map/scatter-add | solution.py:94
  84.8 8.0 collective-permute-done.3
  94.5 4.8 collective-permute-start.4
  105.7 14.9 %gather_fusion.1 = bf16[4000,32]{1,0:T(8,128)(2,1)} fusion(bf16[32,2312]{0,1:T(8,128)(2,1)S(1)} %reshape.703, s32[4096]{0:T(1024)S(1)} %pad_clamp_fusion), kind=kCustom, calls=%fused_computation.1.clone | custom fusion | bytes 528000 | tf_op jit(solution)/shard_map/jit(_take)/gather | solution.py:91
  132.1 23.8 %scatter_custom_fusion.1 = f32[32,2312]{0,1:T(8,128)} fusion(s32[4000]{0:T(1024)} %bitcast.339, f32[4000,32]{1,0:T(8,128)} %copy.289, f32[]{:T(128)} %constant.364.clone.1), kind=kCustom, calls=%fused_computation.94 | custom fusion | flops 128000 | bytes 296448 | tf_op jit(solution)/shard_map/scatter-add | solution.py:94
  170.2 7.7 collective-permute-done.7
  190.7 14.9 %gather_fusion.2 = bf16[4000,32]{1,0:T(8,128)(2,1)} fusion(bf16[32,2312]{0,1:T(8,128)(2,1)S(1)} %reshape.709, s32[4096]{0:T(1024)S(1)} %pad_clamp_fusion), kind=kCustom, calls=%fused_computation.2.clone | custom fusion | bytes 528000 | tf_op jit(solution)/shard_map/jit(_take)/gather | solution.py:91
  217.0 23.8 %scatter_custom_fusion.2 = f32[32,2312]{0,1:T(8,128)} fusion(s32[4000]{0:T(1024)} %bitcast.340, f32[4000,32]{1,0:T(8,128)} %copy.301, f32[]{:T(128)} %constant.364.clone.1), kind=kCustom, calls=%fused_computation.92 | custom fusion | flops 128000 | bytes 296448 | tf_op jit(solution)/shard_map/scatter-add | solution.py:94
  255.1 7.7 collective-permute-done.11
  275.6 12.3 %gather_fusion.3 = bf16[4000,32]{1,0:T(8,128)(2,1)S(1)} fusion(bf16[32,2312]{0,1:T(8,128)(2,1)S(1)} %reshape.715, s32[4096]{0:T(1024)S(1)} %pad_clamp_fusion), kind=kCustom, calls=%fused_computation.3.clone | custom fusion | bytes 528000 | tf_op jit(solution)/shard_map/jit(_take)/gather | solution.py:91
  297.6 23.9 %scatter_custom_fusion.3 = f32[32,2312]{0,1:T(8,128)} fusion(s32[4000]{0:T(1024)} %bitcast.341, f32[4000,32]{1,0:T(8,128)S(1)} %copy.313, f32[]{:T(128)} %constant.364.clone.1), kind=kCustom, calls=%fused_computation.90 | custom fusion | flops 128000 | bytes 296448 | tf_op jit(solution)/shard_map/scatter-add | solution.py:94
  335.8 7.7 collective-permute-done.15
  356.3 12.3 %gather_fusion.4 = bf16[4000,32]{1,0:T(8,128)(2,1)S(1)} fusion(bf16[32,2312]{0,1:T(8,128)(2,1)S(1)} %reshape.721, s32[4096]{0:T(1024)S(1)} %pad_clamp_fusion), kind=kCustom, calls=%fused_computation.4.clone | custom fusion | bytes 528000 | tf_op jit(solution)/shard_map/jit(_take)/gather | solution.py:91
  378.9 23.8 %scatter_custom_fusion.4 = f32[32,2312]{0,1:T(8,128)} fusion(s32[4000]{0:T(1024)} %bitcast.342, f32[4000,32]{1,0:T(8,128)} %copy.325, f32[]{:T(128)} %constant.364.clone.1), kind=kCustom, calls=%fused_computation.88 | custom fusion | flops 128000 | bytes 296448 | tf_op jit(solution)/shard_map/scatter-add | solution.py:94
  417.4 7.7 collective-permute-done.19
  437.9 14.9 %gather_fusion.5 = bf16[4000,32]{1,0:T(8,128)(2,1)} fusion(bf16[32,2312]{0,1:T(8,128)(2,1)S(1)} %reshape.727, s32[4096]{0:T(1024)S(1)} %pad_clamp_fusion), kind=kCustom, calls=%fused_computation.5.clone | custom fusion | bytes 528000 | tf_op jit(solution)/shard_map/jit(_take)/gather | solution.py:91
  464.2 23.8 %scatter_custom_fusion.5 = f32[32,2312]{0,1:T(8,128)} fusion(s32[4000]{0:T(1024)} %bitcast.343, f32[4000,32]{1,0:T(8,128)} %copy.337, f32[]{:T(128)} %constant.364.clone.1), kind=kCustom, calls=%fused_computation.86 | custom fusion | flops 128000 | bytes 296448 | tf_op jit(solution)/shard_map/scatter-add | solution.py:94
  491.7 5.5 collective-permute-done.22
  503.5 7.7 collective-permute-done.23
  524.0 12.3 %gather_fusion.6 = bf16[4000,32]{1,0:T(8,128)(2,1)S(1)} fusion(bf16[32,2312]{0,1:T(8,128)(2,1)S(1)} %reshape.733, s32[4096]{0:T(1024)S(1)} %pad_clamp_fusion), kind=kCustom, calls=%fused_computation.6.clone | custom fusion | bytes 528000 | tf_op jit(solution)/shard_map/jit(_take)/gather | solution.py:91
  546.0 23.9 %scatter_custom_fusion.6 = f32[32,2312]{0,1:T(8,128)} fusion(s32[4000]{0:T(1024)} %bitcast.344, f32[4000,32]{1,0:T(8,128)S(1)} %copy.349, f32[]{:T(128)} %constant.364.clone.1), kind=kCustom, calls=%fused_computation.84 | custom fusion | flops 128000 | bytes 296448 | tf_op jit(solution)/shard_map/scatter-add | solution.py:94
  573.6 5.5 collective-permute-done.26
  585.5 7.7 collective-permute-done.27
  595.0 4.8 collective-permute-start.28
  605.9 14.9 %gather_fusion.7 = bf16[4000,32]{1,0:T(8,128)(2,1)} fusion(bf16[32,2312]{0,1:T(8,128)(2,1)S(1)} %reshape.739, s32[4096]{0:T(1024)S(1)} %pad_clamp_fusion), kind=kCustom, calls=%fused_computation.7.clone | custom fusion | bytes 528000 | tf_op jit(solution)/shard_map/jit(_take)/gather | solution.py:91
  632.3 23.8 %scatter_custom_fusion.7 = f32[32,2312]{0,1:T(8,128)} fusion(s32[4000]{0:T(1024)} %bitcast.345, f32[4000,32]{1,0:T(8,128)} %copy.361, f32[]{:T(128)} %constant.364.clone.1), kind=kCustom, calls=%fused_computation.82 | custom fusion | flops 128000 | bytes 296448 | tf_op jit(solution)/shard_map/scatter-add | solution.py:94
  659.7 6.4 collective-permute-done.30
  672.5 7.7 collective-permute-done.31
  685.9 51.7 %all-gather.2.cloned.1.call-done = bf16[32,32768]{0,1:T(8,128)(2,1)} async-done(((bf16[32,2048]{0,1:T(8,128)(2,1)}), bf16[32,32768]{0,1:T(8,128)(2,1)}) %all-gather.2.cloned.1.call-update) | async-done | bytes 2097168 | tf_op jit(solution)/shard_map/all_gather | solution.py:124
  742.2 83.8 %all-reduce = f32[4,32]{1,0:T(4,128)S(1)} all-reduce(f32[4,32]{1,0:T(4,128)S(1)} %fusion.8), channel_id=2, replica_groups=mesh['cells'=32,'bands'=16] {'cells'}, use_global_device_ids=true, to_apply=%region_8.10.clone | all-reduce | flops 128 | bytes 1024
  (291 shorter events, 280.3 us)
Async XLA Ops:
  7.2 730.4 %all-gather.2.cloned.1.call-start = ((), (), s32[]{:S(2)}) async-start(), calls=%async_computation | async-start | bytes 8912896 | tf_op jit(solution)/shard_map/all_gather | solution.py:124
  8.5 15.4 %collective-permute-start = (bf16[32,8,16]{0,2,1:T(8,128)(2,1)S(1)}, bf16[32,8,16]{0,2,1:T(8,128)(2,1)S(1)}, u32[]{:S(2)}, u32[]{:S(2)}) collective-permute-start(bf16[32,8,16]{0,2,1:T(8,128)(2,1)S(1)} %bitcast.322), channel_id=1, source_target_pairs={{16,0},{32,16},{48,32},{64,48},{80,64},{96,80},{112,96},{128,112},... | collective-permute-start | bytes 24584 | tf_op jit(solution)/shard_map/ppermute | solution.py:23
  24.0 3.8 collective-permute-start.1
  71.9 6.6 collective-permute-start.2
  82.1 10.7 %collective-permute-start.3 = (f32[32,8,16]{0,2,1:T(8,128)S(1)}, f32[32,8,16]{0,2,1:T(8,128)S(1)}, u32[]{:S(2)}, u32[]{:S(2)}) collective-permute-start(f32[32,8,16]{0,2,1:T(8,128)S(1)} %get-tuple-element.233), channel_id=1, source_target_pairs={{496,0},{0,16},{16,32},{32,48},{48,64},{64,80},{80,96},{96,112},{1... | collective-permute-start | bytes 49160 | tf_op jit(solution)/shard_map/ppermute | solution.py:23
  94.5 6.9 collective-permute-start.4
  101.5 3.7 collective-permute-start.5
  157.3 6.6 collective-permute-start.6
  167.5 10.4 %collective-permute-start.7 = (f32[32,8,16]{0,2,1:T(8,128)S(1)}, f32[32,8,16]{0,2,1:T(8,128)S(1)}, u32[]{:S(2)}, u32[]{:S(2)}) collective-permute-start(f32[32,8,16]{0,2,1:T(8,128)S(1)} %get-tuple-element.231), channel_id=1, source_target_pairs={{496,0},{0,16},{16,32},{32,48},{48,64},{64,80},{80,96},{96,112},{1... | collective-permute-start | bytes 49160 | tf_op jit(solution)/shard_map/ppermute | solution.py:23
  179.7 6.7 collective-permute-start.8
  186.5 3.7 collective-permute-start.9
  242.2 6.6 collective-permute-start.10
  252.5 10.4 %collective-permute-start.11 = (f32[32,8,16]{0,2,1:T(8,128)S(1)}, f32[32,8,16]{0,2,1:T(8,128)S(1)}, u32[]{:S(2)}, u32[]{:S(2)}) collective-permute-start(f32[32,8,16]{0,2,1:T(8,128)S(1)} %get-tuple-element.229), channel_id=1, source_target_pairs={{496,0},{0,16},{16,32},{32,48},{48,64},{64,80},{80,96},{96,112},{1... | collective-permute-start | bytes 49160 | tf_op jit(solution)/shard_map/ppermute | solution.py:23
  264.6 6.7 collective-permute-start.12
  271.4 3.7 collective-permute-start.13
  322.9 6.6 collective-permute-start.14
  333.2 10.4 %collective-permute-start.15 = (f32[32,8,16]{0,2,1:T(8,128)S(1)}, f32[32,8,16]{0,2,1:T(8,128)S(1)}, u32[]{:S(2)}, u32[]{:S(2)}) collective-permute-start(f32[32,8,16]{0,2,1:T(8,128)S(1)} %get-tuple-element.227), channel_id=1, source_target_pairs={{496,0},{0,16},{16,32},{32,48},{48,64},{64,80},{80,96},{96,112},{1... | collective-permute-start | bytes 49160 | tf_op jit(solution)/shard_map/ppermute | solution.py:23
  345.3 6.7 collective-permute-start.16
  352.1 3.7 collective-permute-start.17
  404.0 7.0 collective-permute-start.18
  414.8 10.4 %collective-permute-start.19 = (f32[32,8,16]{0,2,1:T(8,128)S(1)}, f32[32,8,16]{0,2,1:T(8,128)S(1)}, u32[]{:S(2)}, u32[]{:S(2)}) collective-permute-start(f32[32,8,16]{0,2,1:T(8,128)S(1)} %get-tuple-element.225), channel_id=1, source_target_pairs={{496,0},{0,16},{16,32},{32,48},{48,64},{64,80},{80,96},{96,112},{1... | collective-permute-start | bytes 49160 | tf_op jit(solution)/shard_map/ppermute | solution.py:23
  426.9 6.7 collective-permute-start.20
  433.7 3.7 collective-permute-start.21
  489.4 7.8 collective-permute-start.22
  500.9 10.4 %collective-permute-start.23 = (f32[32,8,16]{0,2,1:T(8,128)S(1)}, f32[32,8,16]{0,2,1:T(8,128)S(1)}, u32[]{:S(2)}, u32[]{:S(2)}) collective-permute-start(f32[32,8,16]{0,2,1:T(8,128)S(1)} %get-tuple-element.223), channel_id=1, source_target_pairs={{496,0},{0,16},{16,32},{32,48},{48,64},{64,80},{80,96},{96,112},{1... | collective-permute-start | bytes 49160 | tf_op jit(solution)/shard_map/ppermute | solution.py:23
  513.1 6.7 collective-permute-start.24
  519.8 3.7 collective-permute-start.25
  571.3 7.8 collective-permute-start.26
  582.8 10.4 %collective-permute-start.27 = (f32[32,8,16]{0,2,1:T(8,128)S(1)}, f32[32,8,16]{0,2,1:T(8,128)S(1)}, u32[]{:S(2)}, u32[]{:S(2)}) collective-permute-start(f32[32,8,16]{0,2,1:T(8,128)S(1)} %get-tuple-element.221), channel_id=1, source_target_pairs={{496,0},{0,16},{16,32},{32,48},{48,64},{64,80},{80,96},{96,112},{1... | collective-permute-start | bytes 49160 | tf_op jit(solution)/shard_map/ppermute | solution.py:23
  595.0 6.7 collective-permute-start.28
  657.5 8.6 %collective-permute-start.30 = (f32[32,8,17]{0,1,2:T(8,128)S(1)}, f32[32,8,17]{0,1,2:T(8,128)S(1)}, u32[]{:S(2)}, u32[]{:S(2)}) collective-permute-start(f32[32,8,17]{0,1,2:T(8,128)S(1)} %bitcast.305), channel_id=1, source_target_pairs={{15,0},{0,1},{1,2},{2,3},{3,4},{4,5},{5,6},{6,7},{7,8},{8,9},{9,10... | collective-permute-start | bytes 52232 | tf_op jit(solution)/shard_map/ppermute | solution.py:23
  669.8 10.4 %collective-permute-start.31 = (f32[32,8,16]{0,2,1:T(8,128)S(1)}, f32[32,8,16]{0,2,1:T(8,128)S(1)}, u32[]{:S(2)}, u32[]{:S(2)}) collective-permute-start(f32[32,8,16]{0,2,1:T(8,128)S(1)} %get-tuple-element.219), channel_id=1, source_target_pairs={{496,0},{0,16},{16,32},{32,48},{48,64},{64,80},{80,96},{96,112},{1... | collective-permute-start | bytes 49160 | tf_op jit(solution)/shard_map/ppermute | solution.py:23
  (14 other events, 933.6 us)
Sparse Core Ops, SparseCore 0:
  682.9 54.6 all-gather.1
where the time goes:
time: 844 us; the launch traced here: 835 us
  local copies, waits for them, and re-layouts  233 us (28%)
  other arithmetic  218 us (26%)
  waiting for transfers between devices  177 us (21%)
  starting transfers between devices  97.6 us (12%)
  blocking collectives  83.8 us (10%)
  between operations  16.2 us (2%)
    scatter-add x8, other arithmetic, apply_op(): jnp.zeros((NWF, NE), jnp.float32).at[:, flat_idx]  191 us
    ppermute x32, waiting for transfers between devices, passed_along(): return lax.ppermute(block, axis, route)  125 us
    gather x8, local copies, waits for them, and re-layouts, apply_op(): jnp.take(flat_vals, flat_idx, axis=1).reshape(NWF, 125, CELLS_DEV)  109 us
    ppermute x32, starting transfers between devices, passed_along(): return lax.ppermute(block, axis, route)  97.5 us
    unnamed x1, blocking collectives  83.8 us
    all_gather x1, waiting for transfers between devices, shards(): lax.all_gather(filtered, 'bands', axis=1, tiled=True)  51.7 us
    reshape x16, local copies, waits for them, and re-layouts, apply_op(): product.reshape(NWF, -1)  30.8 us
    scatter-add x8, local copies, waits for them, and re-layouts, apply_op(): summed = summed[:, :, :NYL, :].at[:, :, 0, :].add(back_y)  28.6 us
  transfers between devices with their start and end apart: 33, of which 33 were waited for; matrix products, arithmetic and copies ran while one was open for 1% of the time, Pallas kernels for 0%

commit v1 on v0

v1 whole, which is shorter than its diff:
```python
import functools
import math

import jax
import jax.numpy as jnp
import ml_dtypes
import numpy as np
from jax import lax
from jax.experimental import pallas as pl
from jax.experimental.pallas import tpu as pltpu
from jax.sharding import PartitionSpec as P

NWF = 32
DEGREE = 4
STEPS = 2
NXL = 8
NODES_DEV = 2048
PLANE = 256
GHOST = 128
V_AT = NODES_DEV
G_AT = 2 * NODES_DEV
S_AT = G_AT + NXL * GHOST
PAYLOAD = S_AT + 2 * NODES_DEV
LANES_V = PLANE + GHOST
X_ORDER = (0, 4, 1, 3, 5, 7, 2, 6)
CLASS_ROWS = ((0, 2), (2, 6), (6, 8))
VMEM = 48 * 1024 * 1024


def kinetic_table():
    points = [-1.0, -math.sqrt(3.0 / 7.0), 0.0, math.sqrt(3.0 / 7.0), 1.0]
    weights = [0.1, 49.0 / 90.0, 32.0 / 45.0, 49.0 / 90.0, 0.1]
    scales = []
    for row in range(5):
        prod_val = 1.0
        for other in range(5):
            if other != row:
                prod_val = prod_val * (points[row] - points[other])
        scales.append(prod_val)
    deriv = [[0.0] * 5 for row in range(5)]
    for row in range(5):
        for col in range(5):
            if row != col:
                deriv[row][col] = scales[row] / scales[col] / (points[row] - points[col])
            else:
                total = 0.0
                for other in range(5):
                    if other != row:
                        total = total + 1.0 / (points[row] - points[other])
                deriv[row][col] = total
    stiff_one = [
        [sum((deriv[i][a] * weights[i] * deriv[i][b] for i in range(5))) for b in range(5)]
        for a in range(5)
    ]
    mass_one = [[weights[a] if a == b else 0.0 for b in range(5)] for a in range(5)]
    table = [[0.0] * 125 for row in range(125)]
    for k in range(125):
        ka, kb, kc = (k // 25, k // 5 % 5, k % 5)
        for j in range(125):
            ja, jb, jc = (j // 25, j // 5 % 5, j % 5)
            table[k][j] = 0.5 * (
                stiff_one[ka][ja] * mass_one[kb][jb] * mass_one[kc][jc]
                + mass_one[ka][ja] * stiff_one[kb][jb] * mass_one[kc][jc]
                + mass_one[ka][ja] * mass_one[kb][jb] * stiff_one[kc][jc]
            )
    assembled = [dict() for row in range(512)]
    for cell_x in range(2):
        for cell_y in range(2):
            for cell_z in range(2):
                global_ids = []
                for k in range(125):
                    node_x = (4 * cell_x + k // 25) % 8
                    node_y = (4 * cell_y + k // 5 % 5) % 8
                    node_z = (4 * cell_z + k % 5) % 8
                    global_ids.append((node_x * 8 + node_y) * 8 + node_z)
                for k in range(125):
                    row_map = assembled[global_ids[k]]
                    for j in range(125):
                        target = global_ids[j]
                        row_map[target] = row_map.get(target, 0.0) + table[k][j]
    largest = 0.0
    for row_map in assembled:
        total = sum((abs(value) for value in row_map.values()))
        largest = max(largest, total)
    bound = largest + 8.0 * 2.0
    return (np.array(table), float(0.55 * bound), float(0.45 * bound))


@functools.lru_cache(maxsize=None)
def tables():
    table, centre, half = kinetic_table()
    kin = table.astype(np.float32).astype(ml_dtypes.bfloat16).astype(np.float64)
    kin = kin.reshape(5, 5, 5, 5, 5, 5)
    planes = np.zeros((3, 3, PLANE, PLANE))
    lines = np.zeros((5, 5, PLANE))
    for j in range(-1, 5):
        for l in range(-1, 5):
            for b in range(5):
                for c in range(5):
                    y, z = 4 * j + b, 4 * l + c
                    if not (0 <= y < 16 and 0 <= z < 16):
                        continue
                    at = 16 * y + z
                    for a in range(5):
                        for other in range(5):
                            if other != a:
                                lines[a, other, at] += kin[a, b, c, other, b, c]
                    for b2 in range(5):
                        for c2 in range(5):
                            y2, z2 = 4 * j + b2, 4 * l + c2
                            far_y, far_z = y2 // 16, z2 // 16
                            source = 16 * (y2 % 16) + z2 % 16
                            for kind, locals_a in enumerate(((0, 4), (1,), (2,))):
                                value = sum(kin[a, b, c, a, b2, c2] for a in locals_a)
                                if value == 0.0:
                                    continue
                                assert far_y == 0 or far_z == 0
                                part = 1 if far_y else 2 if far_z else 0
                                planes[kind, part, source, at] += value
    line_rows = np.stack(
        [lines[0, 1], lines[0, 2], lines[0, 3], 2.0 * lines[0, 4], lines[1, 2], lines[1, 3]]
    )
    codes = np.full((LANES_V, 8), -7, np.int32)
    mask = np.zeros((128, LANES_V), np.float32)
    kinds = np.zeros((128, 8), np.float32)
    to_x = np.zeros((2, 8, 128), np.float32)
    spread = np.zeros((3, GHOST, PLANE), np.float32)
    for lane in range(LANES_V):
        ghost = lane - PLANE
        if ghost < 0:
            y, z = lane // 16, lane % 16
        elif ghost < 16:
            y, z = 16, ghost
            spread[0, ghost, z] = 1.0
        elif ghost < 32:
            y, z = ghost - 16, 16
            spread[1, ghost, 16 * y] = 1.0
        elif ghost == 32:
            y, z = 16, 16
            spread[2, ghost, 0] = 1.0
        else:
            continue
        for i in range(2):
            for kind in range(4):
                j, l = y // 4 - kind // 2, z // 4 - kind % 2
                if 0 <= j < 4 and 0 <= l < 4:
                    codes[lane, 4 * i + kind] = (4 * i * 17 + 4 * j) * 17 + 4 * l
        for k in range(125):
            b, c = k // 5 % 5, k % 5
            mask[k, lane] = float(y % 4 == b % 4 and z % 4 == c % 4)
    for k in range(125):
        a, b, c = k // 25, k // 5 % 5, k % 5
        kinds[k, 2 * (b == 4) + (c == 4)] = 1.0
        for i in range(2):
            to_x[i, (4 * i + a) % 8, k] = 1.0
    pairs = np.zeros((32, 4, 32), np.float32)
    for row in range(32):
        for other in range(32):
            if row // 2 == other // 2:
                pairs[row, 0::2, other] = 1.0
            if (row // 2 - 1) % 16 == other // 2:
                pairs[row, 1::2, other] = 1.0
    bf = ml_dtypes.bfloat16
    weights = planes.reshape(3, 3 * PLANE, PLANE)
    return dict(
        centre=centre,
        half=half,
        weights=weights.astype(np.float32).astype(bf),
        lines=line_rows.astype(np.float32),
        codes=codes,
        mask=mask,
        kinds=kinds,
        to_x=to_x,
        spread=spread.astype(bf),
        pairs=pairs.reshape(32, 128).astype(bf),
    )


def pack_kernel(v_ref, st_ref, pot_ref, conn_ref, codes_ref, mask_ref, kinds_ref, to_x_ref, out_ref, pot, conn):
    out_ref[:, :V_AT] = v_ref[...]
    out_ref[:, S_AT:] = st_ref[...]
    pot[...] = jnp.zeros_like(pot)
    pot[:125, :32] = pot_ref[...]
    conn[...] = jnp.full_like(conn, -1)
    conn[0:1, :32] = conn_ref[0:1, :]
    first = conn[0:1, :]
    exact = lax.Precision.HIGHEST
    total = jnp.zeros((8, LANES_V), jnp.float32)
    for i in range(2):
        spread = jnp.zeros((128, LANES_V), jnp.float32)
        for kind in range(4):
            column = 4 * i + kind
            placed = jnp.where(codes_ref[:, column : column + 1] == first, 1.0, 0.0)
            spread += lax.dot_general(
                pot[...] * kinds_ref[:, kind : kind + 1],
                placed,
                (((1,), (1,)), ((), ())),
                precision=exact,
                preferred_element_type=jnp.float32,
            )
        total += jnp.dot(
            to_x_ref[i], spread * mask_ref[...], precision=exact, preferred_element_type=jnp.float32
        )
    high = total.astype(jnp.bfloat16).astype(jnp.float32)
    low = total - high
    even = lax.broadcasted_iota(jnp.int32, (32, PLANE), 0) % 2 == 0
    for x in range(NXL):
        main = jnp.where(even, high[x : x + 1, :PLANE], low[x : x + 1, :PLANE])
        out_ref[:, V_AT + PLANE * x : V_AT + PLANE * (x + 1)] = main.astype(jnp.bfloat16)
        ghost = jnp.where(even[:, :GHOST], high[x : x + 1, PLANE:], low[x : x + 1, PLANE:])
        out_ref[:, G_AT + GHOST * x : G_AT + GHOST * (x + 1)] = ghost.astype(jnp.bfloat16)


def diagonal(slabs, pairs_ref, spread_ref, g_ref, centre):
    for x in range(NXL):
        ghosts = []
        for slab in slabs:
            raw = slab[:, G_AT + GHOST * x : G_AT + GHOST * (x + 1)]
            ghosts.append(
                [
                    jnp.dot(raw, spread_ref[part], preferred_element_type=jnp.float32).astype(jnp.bfloat16)
                    for part in range(3)
                ]
            )
        for s, slab in enumerate(slabs):
            own = slab[:, V_AT + PLANE * x : V_AT + PLANE * (x + 1)]
            if s == 0:
                stack = jnp.concatenate([own, ghosts[0][0]], axis=0)
                pairs = pairs_ref[:, :64]
            else:
                stack = jnp.concatenate([own, ghosts[s][0], ghosts[s - 1][1], ghosts[s - 1][2]], axis=0)
                pairs = pairs_ref[...]
            g_ref[x, s] = jnp.dot(pairs, stack, preferred_element_type=jnp.float32) - centre


def filter_step(slabs, w_ref, lines_ref, g_ref, out_ref, cur, prev, acc, half):
    place = {x: at for at, x in enumerate(X_ORDER)}
    right_lanes = lax.broadcasted_iota(jnp.int32, (32, PLANE), 1) % 16 < 8
    for s, slab in enumerate(slabs):
        for x in range(NXL):
            block = slab[:, PLANE * x : PLANE * (x + 1)]
            cur[place[x], s, :, :PLANE] = block
            turn(cur, place[x], s, 0, block[:, :128].astype(jnp.float32))
            turn(cur, place[x], s, 1, block[:, 128:].astype(jnp.float32))
    prev[...] = jnp.zeros_like(prev)

    def sides():
        for at in range(NXL):
            left, middle, right = (cur[at, s, :, :PLANE].astype(jnp.float32) for s in range(3))
            zero = jnp.zeros_like(left)
            cur[at, 0, :, 2 * PLANE :] = jnp.where(right_lanes, middle, zero).astype(jnp.bfloat16)
            cur[at, 1, :, 2 * PLANE :] = jnp.where(right_lanes, right, left).astype(jnp.bfloat16)
            cur[at, 2, :, 2 * PLANE :] = jnp.where(right_lanes, zero, middle).astype(jnp.bfloat16)

    def apply(which, alpha, beta, store):
        first, last = which[0], which[-1] + 1
        for kind, (low, high) in enumerate(CLASS_ROWS):
            rows = cur[low:high, first:last]
            count = (high - low) * (last - first) * 32
            result = jnp.dot(
                rows.reshape(count, 3 * PLANE), w_ref[kind], preferred_element_type=jnp.float32
            )
            acc[low:high, first:last] = result.reshape(high - low, last - first, 32, PLANE)
        for s in which:
            for part in range(2):
                lanes = slice(128 * part, 128 * (part + 1))
                v = [cur[place[x], s, :, lanes].astype(jnp.float32) for x in range(NXL)]
                c01, c02, c03, c04, c12, c13 = (lines_ref[row : row + 1, lanes] for row in range(6))
                s17, s26, s35 = v[1] + v[7], v[2] + v[6], v[3] + v[5]
                s04 = c02 * (v[0] + v[4])
                extra = {
                    0: c01 * s17 + c02 * s26 + c03 * s35 + c04 * v[4],
                    4: c01 * s35 + c02 * s26 + c03 * s17 + c04 * v[0],
                    1: c01 * v[0] + c12 * v[2] + c13 * v[3] + c03 * v[4],
                    3: c01 * v[4] + c12 * v[2] + c13 * v[1] + c03 * v[0],
                    5: c01 * v[4] + c12 * v[6] + c13 * v[7] + c03 * v[0],
                    7: c01 * v[0] + c12 * v[6] + c13 * v[5] + c03 * v[4],
                    2: s04 + c12 * (v[1] + v[3]),
                    6: s04 + c12 * (v[5] + v[7]),
                }
                for x in range(NXL):
                    at = place[x]
                    applied = acc[at, s, :, lanes] + extra[x] + g_ref[x, s, :, lanes] * v[x]
                    store(x, at, s, part, alpha * applied - beta * prev[at, s, :, lanes].astype(jnp.float32))

    def keep(x, at, s, part, new):
        lanes = slice(128 * part, 128 * (part + 1))
        prev[at, s, :, lanes] = cur[at, s, :, lanes]
        new = new.astype(jnp.bfloat16)
        cur[at, s, :, lanes] = new
        turn(cur, at, s, part, new.astype(jnp.float32))

    def emit(x, at, s, part, new):
        out_ref[:, PLANE * x + 128 * part : PLANE * x + 128 * (part + 1)] = new.astype(jnp.bfloat16)

    def order(k, carry):
        sides()
        alpha = jnp.where(k == 0, jnp.float32(1.0 / half), jnp.float32(2.0 / half))
        beta = jnp.where(k == 0, jnp.float32(0.0), jnp.float32(1.0))
        apply((0, 1, 2), alpha, beta, keep)
        return carry

    lax.fori_loop(0, DEGREE - 1, order, 0)
    sides()
    apply((1,), jnp.float32(2.0 / half), jnp.float32(1.0), emit)


def turn(cur, at, s, part, value):
    shift = 30 if part == 0 else 2
    lanes = slice(PLANE + 128 * part, PLANE + 128 * (part + 1))
    cur[at, s, :, lanes] = pltpu.roll(value, shift, 0).astype(jnp.bfloat16)


def first_kernel(centre, half, c_ref, l_ref, r_ref, w_ref, lines_ref, pairs_ref, spread_ref, out_ref, g_ref, cur, prev, acc):
    slabs = (l_ref, c_ref, r_ref)
    diagonal(slabs, pairs_ref, spread_ref, g_ref, centre)
    filter_step(slabs, w_ref, lines_ref, g_ref, out_ref, cur, prev, acc, half)


def later_kernel(half, c_ref, l_ref, r_ref, w_ref, lines_ref, g_ref, out_ref, cur, prev, acc):
    filter_step((l_ref, c_ref, r_ref), w_ref, lines_ref, g_ref, out_ref, cur, prev, acc, half)


def corr_kernel(factor, st_ref, f_ref, out_ref):
    for part in range(2):
        out_ref[part] = factor * lax.dot_general(
            st_ref[:, NODES_DEV * part : NODES_DEV * (part + 1)],
            f_ref[...],
            (((1,), (1,)), ((), ())),
            preferred_element_type=jnp.float32,
        )


def full(shape):
    return pl.BlockSpec(shape, lambda *_: (0,) * len(shape))


def call(kernel, args, specs, outs, scratch=()):
    return pl.pallas_call(
        kernel,
        grid=(1,),
        in_specs=specs,
        out_specs=[full(o.shape) for o in outs],
        out_shape=list(outs),
        scratch_shapes=list(scratch),
        compiler_params=pltpu.CompilerParams(vmem_limit_bytes=VMEM),
    )(*args)


def passed_along(block, axis, distance):
    devices = range(lax.axis_size(axis))
    route = [((i - distance) % len(devices), i) for i in devices]
    return lax.ppermute(block, axis, route)


def shards(cur_block, stored_blocks, cell_potential, connectivity):
    t = tables()
    bf, f32 = jnp.bfloat16, jnp.float32
    n_cells, n_bands = lax.axis_size("cells"), lax.axis_size("bands")
    const = {k: jnp.asarray(v) for k, v in t.items() if isinstance(v, np.ndarray)}
    stored = stored_blocks.reshape(2, 2, n_bands, NODES_DEV).transpose(2, 1, 0, 3).reshape(NWF, 2 * NODES_DEV)
    pack_args = (cur_block, stored, cell_potential, connectivity) + tuple(
        const[k] for k in ("codes", "mask", "kinds", "to_x")
    )
    (payload,) = call(
        pack_kernel,
        pack_args,
        [full(a.shape) for a in pack_args],
        [jax.ShapeDtypeStruct((NWF, PAYLOAD), bf)],
        [pltpu.VMEM((128, 128), f32), pltpu.VMEM((8, 128), jnp.int32)],
    )
    got = lax.all_to_all(payload, "bands", 0, 0, tiled=True)
    near = got[:, :S_AT]
    left = passed_along(near, "cells", 1)
    right = passed_along(near, "cells", -1)
    scratch = [
        pltpu.VMEM((NXL, 3, NWF, 3 * PLANE), bf),
        pltpu.VMEM((NXL, 3, NWF, PLANE), bf),
        pltpu.VMEM((NXL, 3, NWF, PLANE), f32),
    ]
    args = (near, left, right) + tuple(const[k] for k in ("weights", "lines", "pairs", "spread"))
    block, diag = call(
        functools.partial(first_kernel, t["centre"], t["half"]),
        args,
        [full(a.shape) for a in args],
        [
            jax.ShapeDtypeStruct((NWF, NODES_DEV), bf),
            jax.ShapeDtypeStruct((NXL, 3, NWF, PLANE), f32),
        ],
        scratch,
    )
    for step in range(1, STEPS):
        left = passed_along(block, "cells", 1)
        right = passed_along(block, "cells", -1)
        args = (block, left, right, const["weights"], const["lines"], diag)
        (block,) = call(
            functools.partial(later_kernel, t["half"]),
            args,
            [full(a.shape) for a in args],
            [jax.ShapeDtypeStruct((NWF, NODES_DEV), bf)],
            scratch,
        )
    filtered = lax.all_to_all(block, "bands", 0, 0, tiled=True)
    factor = 1.0 / math.sqrt(NODES_DEV * n_cells * n_bands)
    args = (got[:, S_AT:], filtered)
    (partial,) = call(
        functools.partial(corr_kernel, factor),
        args,
        [full(a.shape) for a in args],
        [jax.ShapeDtypeStruct((2, NWF, NWF), f32)],
    )
    partial = partial.reshape(2, n_bands, 2, NWF).transpose(1, 3, 0, 2).reshape(n_bands, NWF, 4)
    partial = lax.all_to_all(partial, "bands", 0, 0, tiled=True).sum(axis=0)
    per_cell = NWF // n_cells
    partial = partial.reshape(n_cells, per_cell, 4)
    total = lax.all_to_all(partial, "cells", 0, 0, tiled=True).sum(axis=0)
    return (filtered, total.T)


def solution(mesh):
    in_specs = (
        P(None, ("cells", "bands")),
        P("bands", "cells"),
        P(None, ("cells", "bands")),
        P(None, ("cells", "bands")),
    )
    out_specs = (P(None, ("cells", "bands")), P("bands", "cells"))
    return jax.shard_map(shards, mesh=mesh, in_specs=in_specs, out_specs=out_specs, check_vma=False)
```

time: 844 us -> 120 us (0.14)
  the two profiles are of different devices: /device:TPU:2 before, /device:TPU:1 now
where the time goes in v1:
time: 120 us; the launch traced here: 119 us
  blocking collectives  44.1 us (37%)
  waiting for transfers between devices  31.2 us (26%)
  starting transfers between devices  26.2 us (22%)
  Pallas kernels  9.92 us (8%)
  local copies, waits for them, and re-layouts  5.34 us (4%)
  other arithmetic  1.25 us (1%)
    ppermute x4, waiting for transfers between devices, passed_along(): return lax.ppermute(block, axis, route)  25 us
    all_to_all x1, blocking collectives, shards(): got = lax.all_to_all(payload, 'bands', 0, 0, tiled=True)  20.6 us
    ppermute x4, starting transfers between devices, passed_along(): return lax.ppermute(block, axis, route)  19 us
    all_to_all x1, blocking collectives, shards(): total = lax.all_to_all(partial, 'cells', 0, 0, tiled=True).sum(axis=0)  14.9 us
    pallas_call x4, Pallas kernels, call(): pl.pallas_call(kernel, grid=(1,), in_specs=specs, out_specs=[full(o.shape...  9.92 us
    all_to_all x1, blocking collectives, shards(): partial = lax.all_to_all(partial, 'bands', 0, 0, tiled=True).sum(axis=0)  8.62 us
    all_to_all x1, starting transfers between devices, shards(): filtered = lax.all_to_all(block, 'bands', 0, 0, tiled=True)  7.24 us
    all_to_all x1, waiting for transfers between devices, shards(): filtered = lax.all_to_all(block, 'bands', 0, 0, tiled=True)  6.21 us
  transfers between devices with their start and end apart: 5, of which 5 were waited for; matrix products, arithmetic and copies ran while one was open for 0% of the time, Pallas kernels for 0%

profile of v1, /device:TPU:1, one launch (start us, length us, event | category | flops | bytes accessed | tf_op | source)
XLA Modules:
  0.0 119.0 jit_solution(17163064568629322624)
XLA Ops:
  0.7 0.9 copy.22.pot_ref
  1.6 0.8 copy.23.conn_ref
  2.4 1.1 copy.27
  3.5 0.3 copy.21
  3.8 0.1 copy.28
  3.9 2.4 %shard_map.131 = bf16[32,9216]{1,0:T(8,128)(2,1)S(1)} custom-call(bf16[32,2048]{1,0:T(8,128)(2,1)S(1)} %copy-done.5, bf16[32,4096]{1,0:T(8,128)(2,1)S(1)} %bitcast.18, f32[125,32]{1,0:T(8,128)S(1)} %copy.22.pot_ref, s32[125,32]{1,0:T(8,128)S(1)} %copy.23.conn_ref, s32[384,8]{1,0:T(8,128)S(1)} %copy-done.4, f32[128,384]{1,0:T(8,128)S(1)} %copy-done.3, ...), custom_call_target="tpu_custom_call" | custom-call | tf_op jit(solution)/shard_map/pallas_call | solution.py:339
  6.4 0.2 all_to_all.21
  6.6 20.6 %all_to_all.33 = bf16[16,2,9216]{2,1,0:T(2,128)(2,1)S(1)} all-to-all(bf16[16,2,9216]{2,1,0:T(2,128)(2,1)S(1)} %all_to_all.21), channel_id=1, replica_groups=mesh['cells'=32,'bands'=16] {'bands'}, dimensions={0} | all-to-all | bytes 1179648 | tf_op jit(solution)/shard_map/all_to_all | solution.py:372
  27.2 0.2 all_to_all.23
  27.5 10.9 %collective-permute-start.1 = (bf16[32,5120]{1,0:T(8,128)(2,1)S(1)}, bf16[32,5120]{1,0:T(8,128)(2,1)S(1)}, u32[]{:S(2)}, u32[]{:S(2)}) collective-permute-start(bf16[32,5120]{1,0:T(8,128)(2,1)S(1)} %slice.8.c_ref), channel_id=1, source_target_pairs={{16,0},{32,16},{48,32},{64,48},{80,64},{96,80},{112,96},{128,112},... | collective-permute-start | bytes 983048 | tf_op jit(solution)/shard_map/ppermute | solution.py:353
  38.4 1.9 %collective-permute-start = (bf16[32,5120]{1,0:T(8,128)(2,1)S(1)}, bf16[32,5120]{1,0:T(8,128)(2,1)S(1)}, u32[]{:S(2)}, u32[]{:S(2)}) collective-permute-start(bf16[32,5120]{1,0:T(8,128)(2,1)S(1)} %slice.8.c_ref), channel_id=1, source_target_pairs={{496,0},{0,16},{16,32},{32,48},{48,64},{64,80},{80,96},{96,112},{1... | collective-permute-start | bytes 983048 | tf_op jit(solution)/shard_map/ppermute | solution.py:353
  40.3 11.3 %collective-permute-done.1.r_ref = bf16[32,5120]{1,0:T(8,128)(2,1)S(1)} collective-permute-done((bf16[32,5120]{1,0:T(8,128)(2,1)S(1)}, bf16[32,5120]{1,0:T(8,128)(2,1)S(1)}, u32[]{:S(2)}, u32[]{:S(2)}) %collective-permute-start.1) | collective-permute-done | bytes 327712 | tf_op jit(solution)/shard_map/ppermute | solution.py:353
  51.6 7.3 %collective-permute-done.l_ref = bf16[32,5120]{1,0:T(8,128)(2,1)S(1)} collective-permute-done((bf16[32,5120]{1,0:T(8,128)(2,1)S(1)}, bf16[32,5120]{1,0:T(8,128)(2,1)S(1)}, u32[]{:S(2)}, u32[]{:S(2)}) %collective-permute-start) | collective-permute-done | bytes 327712 | tf_op jit(solution)/shard_map/ppermute | solution.py:353
  58.9 4.4 %shard_map.132 = (bf16[32,2048]{1,0:T(8,128)(2,1)S(1)}, f32[8,3,32,256]{3,2,1,0:T(8,128)S(1)}) custom-call(bf16[32,5120]{1,0:T(8,128)(2,1)S(1)} %slice.8.c_ref, bf16[32,5120]{1,0:T(8,128)(2,1)S(1)} %collective-permute-done.l_ref, bf16[32,5120]{1,0:T(8,128)(2,1)S(1)} %collective-permute-done.1.r_ref, bf16[3,768,256]{2,1,0:T(8,128)(2,1)S(1)} %copy-done, ...), custom_call_target="tpu_custom_call" | custom-call | tf_op jit(solution)/shard_map/pallas_call | solution.py:339
  63.3 1.9 %collective-permute-start.3 = (bf16[32,2048]{1,0:T(8,128)(2,1)S(1)}, bf16[32,2048]{1,0:T(8,128)(2,1)S(1)}, u32[]{:S(2)}, u32[]{:S(2)}) collective-permute-start(bf16[32,2048]{1,0:T(8,128)(2,1)S(1)} %get-tuple-element.4.c_ref), channel_id=1, source_target_pairs={{16,0},{32,16},{48,32},{64,48},{80,64},{96,80},{112,96},{128,112},... | collective-permute-start | bytes 393224 | tf_op jit(solution)/shard_map/ppermute | solution.py:353
  65.2 4.3 %collective-permute-start.2 = (bf16[32,2048]{1,0:T(8,128)(2,1)S(1)}, bf16[32,2048]{1,0:T(8,128)(2,1)S(1)}, u32[]{:S(2)}, u32[]{:S(2)}) collective-permute-start(bf16[32,2048]{1,0:T(8,128)(2,1)S(1)} %get-tuple-element.4.c_ref), channel_id=1, source_target_pairs={{496,0},{0,16},{16,32},{32,48},{48,64},{64,80},{80,96},{96,112},{1... | collective-permute-start | bytes 393224 | tf_op jit(solution)/shard_map/ppermute | solution.py:353
  69.5 1.9 %collective-permute-done.3.r_ref = bf16[32,2048]{1,0:T(8,128)(2,1)S(1)} collective-permute-done((bf16[32,2048]{1,0:T(8,128)(2,1)S(1)}, bf16[32,2048]{1,0:T(8,128)(2,1)S(1)}, u32[]{:S(2)}, u32[]{:S(2)}) %collective-permute-start.3) | collective-permute-done | bytes 131104 | tf_op jit(solution)/shard_map/ppermute | solution.py:353
  71.4 4.6 %collective-permute-done.2.l_ref = bf16[32,2048]{1,0:T(8,128)(2,1)S(1)} collective-permute-done((bf16[32,2048]{1,0:T(8,128)(2,1)S(1)}, bf16[32,2048]{1,0:T(8,128)(2,1)S(1)}, u32[]{:S(2)}, u32[]{:S(2)}) %collective-permute-start.2) | collective-permute-done | bytes 131104 | tf_op jit(solution)/shard_map/ppermute | solution.py:353
  76.0 2.9 %shard_map.133 = bf16[32,2048]{1,0:T(8,128)(2,1)S(1)} custom-call(bf16[32,2048]{1,0:T(8,128)(2,1)S(1)} %get-tuple-element.4.c_ref, bf16[32,2048]{1,0:T(8,128)(2,1)S(1)} %collective-permute-done.2.l_ref, bf16[32,2048]{1,0:T(8,128)(2,1)S(1)} %collective-permute-done.3.r_ref, bf16[3,768,256]{2,1,0:T(8,128)(2,1)S(1)} %copy-done, f32[6,256]{1,0:T(8,128)S(1)} %copy-done.7, ...), custom_call_target="tpu_custom_call" | custom-call | tf_op jit(solution)/shard_map/pallas_call | solution.py:339
  78.8 0.8 all_to_all.24
  79.6 7.2 %all-to-all-start.1 = ((bf16[16,2,2048]{2,1,0:T(2,128)(2,1)}), bf16[16,2,2048]{2,1,0:T(2,128)(2,1)S(1)}, u32[]{:S(2)}, u32[]{:S(2)}) async-start(bf16[16,2,2048]{2,1,0:T(2,128)(2,1)} %all_to_all.24), calls=%async_computation.1 | async-start | bytes 262144 | tf_op jit(solution)/shard_map/all_to_all | solution.py:403
  86.9 6.2 %all-to-all-done.1 = bf16[16,2,2048]{2,1,0:T(2,128)(2,1)S(1)} async-done(((bf16[16,2,2048]{2,1,0:T(2,128)(2,1)}), bf16[16,2,2048]{2,1,0:T(2,128)(2,1)S(1)}, u32[]{:S(2)}, u32[]{:S(2)}) %all-to-all-start.1) | async-done | bytes 131104 | tf_op jit(solution)/shard_map/all_to_all | solution.py:403
  93.1 0.1 all_to_all.26.f_ref
  93.1 0.2 shard_map.134
  93.4 0.1 reshape.30
  93.5 8.6 %all_to_all.34 = f32[16,1,128]{2,1,0:T(1,128)S(1)} all-to-all(f32[16,1,128]{2,1,0:T(1,128)S(1)} %reshape.30), channel_id=1, replica_groups=mesh['cells'=32,'bands'=16] {'bands'}, dimensions={0} | all-to-all | bytes 16384 | tf_op jit(solution)/shard_map/all_to_all | solution.py:413
  102.1 0.5 broadcast
  102.6 0.7 reduce.1
  103.3 0.1 reshape.31
  103.4 0.1 copy.26
  103.5 14.9 %all_to_all.35 = f32[32,1,4]{2,1,0:T(1,128)S(1)} all-to-all(f32[32,1,4]{2,1,0:T(1,128)S(1)} %copy.26), channel_id=1, replica_groups=mesh['cells'=32,'bands'=16] {'cells'}, dimensions={0} | all-to-all | bytes 1024 | tf_op jit(solution)/shard_map/all_to_all | solution.py:416
  118.4 0.6 reduce_sum.19
  (25 shorter events, 0.2 us)
Async XLA Ops:
  0.6 3.3 %copy-start.9 = (f32[2,8,128]{2,1,0:T(8,128)S(1)}, f32[2,8,128]{2,1,0:T(8,128)}, u32[]{:S(2)}) copy-start(f32[2,8,128]{2,1,0:T(8,128)} %constant.23.clone.to_x_ref) | copy-start | bytes 24580
  0.6 3.3 %copy-start.6 = (f32[128,8]{1,0:T(8,128)S(1)}, f32[128,8]{1,0:T(8,128)}, u32[]{:S(2)}) copy-start(f32[128,8]{1,0:T(8,128)} %constant.22.clone.kinds_ref) | copy-start | bytes 12292
  0.7 3.3 %copy-start.3 = (f32[128,384]{1,0:T(8,128)S(1)}, f32[128,384]{1,0:T(8,128)}, u32[]{:S(2)}) copy-start(f32[128,384]{1,0:T(8,128)} %constant.21.clone.mask_ref) | copy-start | bytes 589828
  0.7 3.2 %copy-start.4 = (s32[384,8]{1,0:T(8,128)S(1)}, s32[384,8]{1,0:T(8,128)}, u32[]{:S(2)}) copy-start(s32[384,8]{1,0:T(8,128)} %constant.20.clone.codes_ref) | copy-start | bytes 36868
  0.7 3.2 %copy-start.5 = (bf16[32,2048]{1,0:T(8,128)(2,1)S(1)}, bf16[32,2048]{1,0:T(8,128)(2,1)}, u32[]{:S(2)}) copy-start(bf16[32,2048]{1,0:T(8,128)(2,1)} %v_ref.1) | copy-start | bytes 393220
  27.2 31.7 %copy-start = (bf16[3,768,256]{2,1,0:T(8,128)(2,1)S(1)}, bf16[3,768,256]{2,1,0:T(8,128)(2,1)}, u32[]{:S(2)}) copy-start(bf16[3,768,256]{2,1,0:T(8,128)(2,1)} %constant.18.clone.w_ref) | copy-start | bytes 3538948
  27.2 31.7 %copy-start.2 = (bf16[3,128,256]{2,1,0:T(8,128)(2,1)S(1)}, bf16[3,128,256]{2,1,0:T(8,128)(2,1)}, u32[]{:S(2)}) copy-start(bf16[3,128,256]{2,1,0:T(8,128)(2,1)} %constant.24.clone.spread_ref) | copy-start | bytes 589828
  27.2 31.7 %copy-start.7 = (f32[6,256]{1,0:T(8,128)S(1)}, f32[6,256]{1,0:T(8,128)}, u32[]{:S(2)}) copy-start(f32[6,256]{1,0:T(8,128)} %constant.19.clone.lines_ref) | copy-start | bytes 18436
  27.2 31.7 %copy-start.8 = (bf16[32,128]{1,0:T(8,128)(2,1)S(1)}, bf16[32,128]{1,0:T(8,128)(2,1)}, u32[]{:S(2)}) copy-start(bf16[32,128]{1,0:T(8,128)(2,1)} %constant.25.clone.pairs_ref) | copy-start | bytes 24580
  27.5 24.1 %collective-permute-start.1 = (bf16[32,5120]{1,0:T(8,128)(2,1)S(1)}, bf16[32,5120]{1,0:T(8,128)(2,1)S(1)}, u32[]{:S(2)}, u32[]{:S(2)}) collective-permute-start(bf16[32,5120]{1,0:T(8,128)(2,1)S(1)} %slice.8.c_ref), channel_id=1, source_target_pairs={{16,0},{32,16},{48,32},{64,48},{80,64},{96,80},{112,96},{128,112},... | collective-permute-start | bytes 983048 | tf_op jit(solution)/shard_map/ppermute | solution.py:353
  38.4 20.5 %collective-permute-start = (bf16[32,5120]{1,0:T(8,128)(2,1)S(1)}, bf16[32,5120]{1,0:T(8,128)(2,1)S(1)}, u32[]{:S(2)}, u32[]{:S(2)}) collective-permute-start(bf16[32,5120]{1,0:T(8,128)(2,1)S(1)} %slice.8.c_ref), channel_id=1, source_target_pairs={{496,0},{0,16},{16,32},{32,48},{48,64},{64,80},{80,96},{96,112},{1... | collective-permute-start | bytes 983048 | tf_op jit(solution)/shard_map/ppermute | solution.py:353
  63.3 8.1 %collective-permute-start.3 = (bf16[32,2048]{1,0:T(8,128)(2,1)S(1)}, bf16[32,2048]{1,0:T(8,128)(2,1)S(1)}, u32[]{:S(2)}, u32[]{:S(2)}) collective-permute-start(bf16[32,2048]{1,0:T(8,128)(2,1)S(1)} %get-tuple-element.4.c_ref), channel_id=1, source_target_pairs={{16,0},{32,16},{48,32},{64,48},{80,64},{96,80},{112,96},{128,112},... | collective-permute-start | bytes 393224 | tf_op jit(solution)/shard_map/ppermute | solution.py:353
  65.2 10.7 %collective-permute-start.2 = (bf16[32,2048]{1,0:T(8,128)(2,1)S(1)}, bf16[32,2048]{1,0:T(8,128)(2,1)S(1)}, u32[]{:S(2)}, u32[]{:S(2)}) collective-permute-start(bf16[32,2048]{1,0:T(8,128)(2,1)S(1)} %get-tuple-element.4.c_ref), channel_id=1, source_target_pairs={{496,0},{0,16},{16,32},{32,48},{48,64},{64,80},{80,96},{96,112},{1... | collective-permute-start | bytes 393224 | tf_op jit(solution)/shard_map/ppermute | solution.py:353
  79.6 13.5 %all-to-all-start.1 = ((bf16[16,2,2048]{2,1,0:T(2,128)(2,1)}), bf16[16,2,2048]{2,1,0:T(2,128)(2,1)S(1)}, u32[]{:S(2)}, u32[]{:S(2)}) async-start(bf16[16,2,2048]{2,1,0:T(2,128)(2,1)} %all_to_all.24), calls=%async_computation.1 | async-start | bytes 262144 | tf_op jit(solution)/shard_map/all_to_all | solution.py:403
  93.1 25.8 %copy-start.1 = (bf16[32,2048]{1,0:T(8,128)(2,1)}, bf16[32,2048]{1,0:T(8,128)(2,1)S(1)}, u32[]{:S(2)}) copy-start(bf16[32,2048]{1,0:T(8,128)(2,1)S(1)} %all_to_all.26.f_ref) | copy-start | bytes 393220

commit v2 on v1

--- a/solution.py
+++ b/solution.py
@@ -16,12 +16,11 @@
 NXL = 8
 NODES_DEV = 2048
 PLANE = 256
-GHOST = 128
-V_AT = NODES_DEV
-G_AT = 2 * NODES_DEV
-S_AT = G_AT + NXL * GHOST
-PAYLOAD = S_AT + 2 * NODES_DEV
-LANES_V = PLANE + GHOST
+LANES_V = 384
+MESSAGE = NODES_DEV + 256
+V_AT = 3 * NODES_DEV
+G_AT = 6 * NODES_DEV
+PAYLOAD = G_AT + 3 * 128
 X_ORDER = (0, 4, 1, 3, 5, 7, 2, 6)
 CLASS_ROWS = ((0, 2), (2, 6), (6, 8))
 VMEM = 48 * 1024 * 1024
@@ -120,46 +119,46 @@
     line_rows = np.stack(
         [lines[0, 1], lines[0, 2], lines[0, 3], 2.0 * lines[0, 4], lines[1, 2], lines[1, 3]]
     )
-    codes = np.full((LANES_V, 8), -7, np.int32)
+    cell_codes = np.full((1, 128), -1, np.int32)
+    for cell in range(32):
+        i, j, l = cell // 16, cell // 4 % 4, cell % 4
+        cell_codes[0, cell] = (4 * i * 17 + 4 * j) * 17 + 4 * l
+    places = np.full((2, 6, LANES_V), -1.0, np.float32)
     mask = np.zeros((128, LANES_V), np.float32)
-    kinds = np.zeros((128, 8), np.float32)
+    kinds = np.zeros((6, 128), np.float32)
     to_x = np.zeros((2, 8, 128), np.float32)
-    spread = np.zeros((3, GHOST, PLANE), np.float32)
-    for lane in range(LANES_V):
-        ghost = lane - PLANE
-        if ghost < 0:
-            y, z = lane // 16, lane % 16
-        elif ghost < 16:
-            y, z = 16, ghost
-            spread[0, ghost, z] = 1.0
-        elif ghost < 32:
-            y, z = ghost - 16, 16
-            spread[1, ghost, 16 * y] = 1.0
-        elif ghost == 32:
-            y, z = 16, 16
-            spread[2, ghost, 0] = 1.0
-        else:
-            continue
+    spread = np.zeros((128, NXL, 128), np.float32)
+    for lane in range(PLANE + 16):
+        y, z = (lane // 16, lane % 16) if lane < PLANE else (16, lane - PLANE)
         for i in range(2):
             for kind in range(4):
                 j, l = y // 4 - kind // 2, z // 4 - kind % 2
                 if 0 <= j < 4 and 0 <= l < 4:
-                    codes[lane, 4 * i + kind] = (4 * i * 17 + 4 * j) * 17 + 4 * l
+                    places[i, kind, lane] = 16 * i + 4 * j + l
+            for kind in range(2):
+                j = y // 4 - kind
+                if 0 <= j < 4 and z == 0:
+                    places[i, 4 + kind, lane] = 16 * i + 4 * j + 3
         for k in range(125):
             b, c = k // 5 % 5, k % 5
             mask[k, lane] = float(y % 4 == b % 4 and z % 4 == c % 4)
     for k in range(125):
         a, b, c = k // 25, k // 5 % 5, k % 5
-        kinds[k, 2 * (b == 4) + (c == 4)] = 1.0
+        kinds[2 * (b == 4) + (c == 4), k] = 1.0
+        if c == 4:
+            kinds[4 + (b == 4), k] = 1.0
         for i in range(2):
             to_x[i, (4 * i + a) % 8, k] = 1.0
-    pairs = np.zeros((32, 4, 32), np.float32)
+    for x in range(NXL):
+        for z in range(16):
+            spread[16 * x + z, x, z] = 1.0
+    pairs = np.zeros((32, 2, 32), np.float32)
     for row in range(32):
         for other in range(32):
             if row // 2 == other // 2:
-                pairs[row, 0::2, other] = 1.0
+                pairs[row, 0, other] = 1.0
             if (row // 2 - 1) % 16 == other // 2:
-                pairs[row, 1::2, other] = 1.0
+                pairs[row, 1, other] = 1.0
     bf = ml_dtypes.bfloat16
     weights = planes.reshape(3, 3 * PLANE, PLANE)
     return dict(
@@ -167,70 +166,89 @@
         half=half,
         weights=weights.astype(np.float32).astype(bf),
         lines=line_rows.astype(np.float32),
-        codes=codes,
+        cell_codes=cell_codes,
+        places=places,
         mask=mask,
         kinds=kinds,
-        to_x=to_x,
-        spread=spread.astype(bf),
-        pairs=pairs.reshape(32, 128).astype(bf),
-    )
-
-
-def pack_kernel(v_ref, st_ref, pot_ref, conn_ref, codes_ref, mask_ref, kinds_ref, to_x_ref, out_ref, pot, conn):
-    out_ref[:, :V_AT] = v_ref[...]
-    out_ref[:, S_AT:] = st_ref[...]
+        to_x=to_x.astype(bf),
+        spread=spread.reshape(128, NXL * 128).astype(bf),
+        pairs=pairs.reshape(32, 64).astype(bf),
+    )
+
+
+def message_kernel(v_ref, pot_ref, conn_ref, codes_ref, out_ref, pot):
+    out_ref[:, :NODES_DEV] = v_ref[...]
     pot[...] = jnp.zeros_like(pot)
-    pot[:125, :32] = pot_ref[...]
-    conn[...] = jnp.full_like(conn, -1)
-    conn[0:1, :32] = conn_ref[0:1, :]
-    first = conn[0:1, :]
-    exact = lax.Precision.HIGHEST
+    pot[:, :125] = pot_ref[...]
+    lane = lax.broadcasted_iota(jnp.int32, (32, 128), 1)
+    here = jnp.where(conn_ref[:, 0:1] == codes_ref[...], lane.astype(jnp.float32), 0.0)
+    cell = jnp.sum(here, axis=1, keepdims=True)
+    high = pot[...].astype(jnp.bfloat16).astype(jnp.float32)
+    low = pot[...] - high
+    out_ref[:, NODES_DEV : NODES_DEV + 128] = jnp.where(lane == 127, cell, high).astype(jnp.bfloat16)
+    out_ref[:, NODES_DEV + 128 :] = low.astype(jnp.bfloat16)
+
+
+def nodal(own, left, places_ref, kinds_ref, mask_ref, to_x_ref):
+    sides = [(own, range(4))] + ([(left, range(4, 6))] if left is not None else [])
+    rows, ones = [], ([], [])
+    for message, kind_range in sides:
+        high = message[:, NODES_DEV : NODES_DEV + 128].astype(jnp.float32)
+        low = message[:, NODES_DEV + 128 :].astype(jnp.float32)
+        cell = high[:, 127:128]
+        for kind in kind_range:
+            pick = kinds_ref[kind : kind + 1, :]
+            rows += [high * pick, low * pick]
+            for i in range(2):
+                one = jnp.where(cell == places_ref[i, kind : kind + 1, :], 1.0, 0.0)
+                ones[i].extend([one, one])
+    stack = jnp.concatenate(rows, axis=0).astype(jnp.bfloat16)
     total = jnp.zeros((8, LANES_V), jnp.float32)
     for i in range(2):
-        spread = jnp.zeros((128, LANES_V), jnp.float32)
-        for kind in range(4):
-            column = 4 * i + kind
-            placed = jnp.where(codes_ref[:, column : column + 1] == first, 1.0, 0.0)
-            spread += lax.dot_general(
-                pot[...] * kinds_ref[:, kind : kind + 1],
-                placed,
-                (((1,), (1,)), ((), ())),
-                precision=exact,
-                preferred_element_type=jnp.float32,
+        placed = jnp.concatenate(ones[i], axis=0).astype(jnp.bfloat16)
+        values = lax.dot_general(
+            stack, placed, (((0,), (0,)), ((), ())), preferred_element_type=jnp.float32
+        )
+        values = values * mask_ref[...]
+        high = values.astype(jnp.bfloat16)
+        low = (values - high.astype(jnp.float32)).astype(jnp.bfloat16)
+        total += jnp.dot(to_x_ref[i], high, preferred_element_type=jnp.float32)
+        total += jnp.dot(to_x_ref[i], low, preferred_element_type=jnp.float32)
+    return total
+
+
+def pack_kernel(c_ref, l_ref, r_ref, places_ref, kinds_ref, mask_ref, to_x_ref, out_ref, ghost):
+    messages = (l_ref, c_ref, r_ref)
+    even = lax.broadcasted_iota(jnp.int32, (32, PLANE), 0) % 2 == 0
+    for s, message in enumerate(messages):
+        out_ref[:, NODES_DEV * s : NODES_DEV * (s + 1)] = message[:, :NODES_DEV]
+        left = messages[s - 1] if s else None
+        total = nodal(message, left, places_ref, kinds_ref, mask_ref, to_x_ref)
+        high = total.astype(jnp.bfloat16).astype(jnp.float32)
+        low = total - high
+        for x in range(NXL):
+            main = jnp.where(even, high[x : x + 1, :PLANE], low[x : x + 1, :PLANE])
+            at = V_AT + NODES_DEV * s + PLANE * x
+            out_ref[:, at : at + PLANE] = main.astype(jnp.bfloat16)
+            edge = jnp.where(even[:, :128], high[x : x + 1, PLANE:], low[x : x + 1, PLANE:])
+            ghost[:, 16 * x : 16 * (x + 1)] = edge[:, :16]
+        at = G_AT + 128 * s
+        out_ref[:, at : at + 128] = ghost[...].astype(jnp.bfloat16)
+
+
+def diagonal(got, pairs_ref, spread_ref, g_ref, centre):
+    for s in range(3):
+        at = G_AT + 128 * s
+        edge = jnp.dot(got[:, at : at + 128], spread_ref[...], preferred_element_type=jnp.float32)
+        edge = edge.astype(jnp.bfloat16)
+        for x in range(NXL):
+            at = V_AT + NODES_DEV * s + PLANE * x
+            stack = jnp.concatenate([got[:, at : at + 128], edge[:, 128 * x : 128 * (x + 1)]], axis=0)
+            g_ref[x, s, :, :128] = jnp.dot(pairs_ref[...], stack, preferred_element_type=jnp.float32) - centre
+            g_ref[x, s, :, 128:] = (
+                jnp.dot(pairs_ref[:, :32], got[:, at + 128 : at + PLANE], preferred_element_type=jnp.float32)
+                - centre
             )
-        total += jnp.dot(
-            to_x_ref[i], spread * mask_ref[...], precision=exact, preferred_element_type=jnp.float32
-        )
-    high = total.astype(jnp.bfloat16).astype(jnp.float32)
-    low = total - high
-    even = lax.broadcasted_iota(jnp.int32, (32, PLANE), 0) % 2 == 0
-    for x in range(NXL):
-        main = jnp.where(even, high[x : x + 1, :PLANE], low[x : x + 1, :PLANE])
-        out_ref[:, V_AT + PLANE * x : V_AT + PLANE * (x + 1)] = main.astype(jnp.bfloat16)
-        ghost = jnp.where(even[:, :GHOST], high[x : x + 1, PLANE:], low[x : x + 1, PLANE:])
-        out_ref[:, G_AT + GHOST * x : G_AT + GHOST * (x + 1)] = ghost.astype(jnp.bfloat16)
-
-
-def diagonal(slabs, pairs_ref, spread_ref, g_ref, centre):
-    for x in range(NXL):
-        ghosts = []
-        for slab in slabs:
-            raw = slab[:, G_AT + GHOST * x : G_AT + GHOST * (x + 1)]
-            ghosts.append(
-                [
-                    jnp.dot(raw, spread_ref[part], preferred_element_type=jnp.float32).astype(jnp.bfloat16)
-                    for part in range(3)
-                ]
-            )
-        for s, slab in enumerate(slabs):
-            own = slab[:, V_AT + PLANE * x : V_AT + PLANE * (x + 1)]
-            if s == 0:
-                stack = jnp.concatenate([own, ghosts[0][0]], axis=0)
-                pairs = pairs_ref[:, :64]
-            else:
-                stack = jnp.concatenate([own, ghosts[s][0], ghosts[s - 1][1], ghosts[s - 1][2]], axis=0)
-                pairs = pairs_ref[...]
-            g_ref[x, s] = jnp.dot(pairs, stack, preferred_element_type=jnp.float32) - centre
 
 
 def filter_step(slabs, w_ref, lines_ref, g_ref, out_ref, cur, prev, acc, half):
@@ -311,35 +329,62 @@
     cur[at, s, :, lanes] = pltpu.roll(value, shift, 0).astype(jnp.bfloat16)
 
 
-def first_kernel(centre, half, c_ref, l_ref, r_ref, w_ref, lines_ref, pairs_ref, spread_ref, out_ref, g_ref, cur, prev, acc):
-    slabs = (l_ref, c_ref, r_ref)
-    diagonal(slabs, pairs_ref, spread_ref, g_ref, centre)
+def first_kernel(centre, half, got, w_ref, lines_ref, pairs_ref, spread_ref, out_ref, g_ref, cur, prev, acc):
+    diagonal(got, pairs_ref, spread_ref, g_ref, centre)
+    slabs = [got.at[:, NODES_DEV * s : NODES_DEV * (s + 1)] for s in range(3)]
     filter_step(slabs, w_ref, lines_ref, g_ref, out_ref, cur, prev, acc, half)
 
 
-def later_kernel(half, c_ref, l_ref, r_ref, w_ref, lines_ref, g_ref, out_ref, cur, prev, acc):
+def later_kernel(half, c_ref, l_ref, r_ref, st_ref, w_ref, lines_ref, g_ref, out_ref, cur, prev, acc):
+    out_ref[:, NODES_DEV:] = st_ref[...]
     filter_step((l_ref, c_ref, r_ref), w_ref, lines_ref, g_ref, out_ref, cur, prev, acc, half)
 
 
-def corr_kernel(factor, st_ref, f_ref, out_ref):
-    for part in range(2):
-        out_ref[part] = factor * lax.dot_general(
-            st_ref[:, NODES_DEV * part : NODES_DEV * (part + 1)],
-            f_ref[...],
+def corr_kernel(factor, got, filtered_ref, out_ref):
+    filtered = got[:, :NODES_DEV]
+    filtered_ref[...] = filtered
+    four = jnp.concatenate([filtered] * 4, axis=0)
+    parts = [
+        lax.dot_general(
+            got[:, NODES_DEV * (1 + part) : NODES_DEV * (2 + part)],
+            four,
             (((1,), (1,)), ((), ())),
             preferred_element_type=jnp.float32,
         )
+        for part in range(2)
+    ]
+    lane = lax.broadcasted_iota(jnp.int32, (NWF, 128), 1)
+    row = lax.broadcasted_iota(jnp.int32, (NWF, 128), 0)
+    both = jnp.where(lane // 32 % 2 == 0, parts[0], parts[1])
+    out_ref[...] = jnp.where(lane // 64 == row % 2, both * factor, 0.0)
+
+
+def share_kernel(got, out_ref):
+    total = jnp.sum(got[...], axis=0, keepdims=True)
+    lane = lax.broadcasted_iota(jnp.int32, (NWF, 128), 1)
+    row = lax.broadcasted_iota(jnp.int32, (NWF, 128), 0)
+    out_ref[...] = jnp.where(lane % NWF == row, total, 0.0)
+
+
+def total_kernel(got, out_ref):
+    total = jnp.sum(got[...], axis=0, keepdims=True)
+    lane = lax.broadcasted_iota(jnp.int32, (1, 128), 1)
+    rows = jnp.zeros((1, 128), jnp.float32)
+    for row in range(4):
+        mine = lane // 32 == row // 2 + 2 * (row % 2)
+        rows = jnp.where(lane == row, jnp.sum(jnp.where(mine, total, 0.0), axis=1, keepdims=True), rows)
+    out_ref[...] = rows[:, :4]
 
 
 def full(shape):
     return pl.BlockSpec(shape, lambda *_: (0,) * len(shape))
 
 
-def call(kernel, args, specs, outs, scratch=()):
+def call(kernel, args, outs, scratch=()):
     return pl.pallas_call(
         kernel,
         grid=(1,),
-        in_specs=specs,
+        in_specs=[full(a.shape) for a in args],
         out_specs=[full(o.shape) for o in outs],
         out_shape=list(outs),
         scratch_shapes=list(scratch),
@@ -356,64 +401,55 @@
 def shards(cur_block, stored_blocks, cell_potential, connectivity):
     t = tables()
     bf, f32 = jnp.bfloat16, jnp.float32
+    shape = jax.ShapeDtypeStruct
     n_cells, n_bands = lax.axis_size("cells"), lax.axis_size("bands")
     const = {k: jnp.asarray(v) for k, v in t.items() if isinstance(v, np.ndarray)}
+    (message,) = call(
+        message_kernel,
+        (cur_block, cell_potential.T, connectivity.T, const["cell_codes"]),
+        [shape((NWF, MESSAGE), bf)],
+        [pltpu.VMEM((32, 128), f32)],
+    )
+    left = passed_along(message, "cells", 1)
+    right = passed_along(message, "cells", -1)
     stored = stored_blocks.reshape(2, 2, n_bands, NODES_DEV).transpose(2, 1, 0, 3).reshape(NWF, 2 * NODES_DEV)
-    pack_args = (cur_block, stored, cell_potential, connectivity) + tuple(
-        const[k] for k in ("codes", "mask", "kinds", "to_x")
-    )
     (payload,) = call(
         pack_kernel,
-        pack_args,
-        [full(a.shape) for a in pack_args],
-        [jax.ShapeDtypeStruct((NWF, PAYLOAD), bf)],
-        [pltpu.VMEM((128, 128), f32), pltpu.VMEM((8, 128), jnp.int32)],
+        (message, left, right) + tuple(const[k] for k in ("places", "kinds", "mask", "to_x")),
+        [shape((NWF, PAYLOAD), bf)],
+        [pltpu.VMEM((32, 128), f32)],
     )
     got = lax.all_to_all(payload, "bands", 0, 0, tiled=True)
-    near = got[:, :S_AT]
-    left = passed_along(near, "cells", 1)
-    right = passed_along(near, "cells", -1)
     scratch = [
         pltpu.VMEM((NXL, 3, NWF, 3 * PLANE), bf),
         pltpu.VMEM((NXL, 3, NWF, PLANE), bf),
         pltpu.VMEM((NXL, 3, NWF, PLANE), f32),
     ]
-    args = (near, left, right) + tuple(const[k] for k in ("weights", "lines", "pairs", "spread"))
     block, diag = call(
         functools.partial(first_kernel, t["centre"], t["half"]),
-        args,
-        [full(a.shape) for a in args],
-        [
-            jax.ShapeDtypeStruct((NWF, NODES_DEV), bf),
-            jax.ShapeDtypeStruct((NXL, 3, NWF, PLANE), f32),
-        ],
+        (got,) + tuple(const[k] for k in ("weights", "lines", "pairs", "spread")),
+        [shape((NWF, NODES_DEV), bf), shape((NXL, 3, NWF, PLANE), f32)],
         scratch,
     )
-    for step in range(1, STEPS):
-        left = passed_along(block, "cells", 1)
-        right = passed_along(block, "cells", -1)
-        args = (block, left, right, const["weights"], const["lines"], diag)
-        (block,) = call(
-            functools.partial(later_kernel, t["half"]),
-            args,
-            [full(a.shape) for a in args],
-            [jax.ShapeDtypeStruct((NWF, NODES_DEV), bf)],
-            scratch,
-        )
-    filtered = lax.all_to_all(block, "bands", 0, 0, tiled=True)
+    left = passed_along(block, "cells", 1)
+    right = passed_along(block, "cells", -1)
+    (block,) = call(
+        functools.partial(later_kernel, t["half"]),
+        (block, left, right, stored, const["weights"], const["lines"], diag),
+        [shape((NWF, 3 * NODES_DEV), bf)],
+        scratch,
+    )
+    got = lax.all_to_all(block, "bands", 0, 0, tiled=True)
     factor = 1.0 / math.sqrt(NODES_DEV * n_cells * n_bands)
-    args = (got[:, S_AT:], filtered)
-    (partial,) = call(
+    filtered, partial = call(
         functools.partial(corr_kernel, factor),
-        args,
-        [full(a.shape) for a in args],
-        [jax.ShapeDtypeStruct((2, NWF, NWF), f32)],
-    )
-    partial = partial.reshape(2, n_bands, 2, NWF).transpose(1, 3, 0, 2).reshape(n_bands, NWF, 4)
-    partial = lax.all_to_all(partial, "bands", 0, 0, tiled=True).sum(axis=0)
-    per_cell = NWF // n_cells
-    partial = partial.reshape(n_cells, per_cell, 4)
-    total = lax.all_to_all(partial, "cells", 0, 0, tiled=True).sum(axis=0)
+        (got,),
+        [shape((NWF, NODES_DEV), bf), shape((NWF, 128), f32)],
+    )
+    partial = lax.all_to_all(partial, "bands", 0, 0, tiled=True)
+    (partial,) = call(share_kernel, (partial,), [shape((NWF, 128), f32)])
+    partial = lax.all_to_all(partial, "cells", 0, 0, tiled=True)
+    (total,) = call(total_kernel, (partial,), [shape((1, 4), f32)])
     return (filtered, total.T)
 
 

time: 120 us -> 117 us (0.975)
  waiting for transfers between devices: 31.2 us -> 6 us
  blocking collectives: 44.1 us -> 64.6 us
  local copies, waits for them, and re-layouts: 5.34 us -> 8.55 us
  other arithmetic: 1.25 us -> 0 us
    all_to_all x2 -> x3, blocking collectives: 23.5 us -> 44.8 us  [the longest x1 20.7 us: shards(): partial = lax.all_to_all(partial, 'cells', 0, 0, tiled=True)]
    ppermute x4, waiting for transfers between devices: 25 us -> 6 us  [passed_along(): return lax.ppermute(block, axis, route)]
    ppermute x4, starting transfers between devices: 19 us -> 27.1 us  [passed_along(): return lax.ppermute(block, axis, route)]
    all_to_all x1 -> x0, starting transfers between devices: 7.24 us -> none  [shards(): filtered = lax.all_to_all(block, 'bands', 0, 0, tiled=True)]
    all_to_all x1 -> x0, waiting for transfers between devices: 6.21 us -> none  [shards(): filtered = lax.all_to_all(block, 'bands', 0, 0, tiled=True)]
    unnamed x26 -> x28, local copies, waits for them, and re-layouts: 3.13 us -> 7.25 us
    pallas_call x4 -> x7, Pallas kernels: 9.92 us -> 9.41 us  [call(): pl.pallas_call(kernel, grid=(1,), in_specs=[full(a.shape) for a in args],...]
  transfers between devices with their start and end apart: 5 -> 4, of which waited for: 5 -> 3; matrix products, arithmetic and copies ran while one was open for 0% -> 0% of each run, Pallas kernels for 0% -> 0%
where the time goes in v2:
time: 117 us; the launch traced here: 116 us
  blocking collectives  64.6 us (55%)
  starting transfers between devices  27.1 us (23%)
  Pallas kernels  9.41 us (8%)
  local copies, waits for them, and re-layouts  8.55 us (7%)
  waiting for transfers between devices  6 us (5%)
    ppermute x4, starting transfers between devices, passed_along(): return lax.ppermute(block, axis, route)  27.1 us
    all_to_all x1, blocking collectives, shards(): partial = lax.all_to_all(partial, 'cells', 0, 0, tiled=True)  20.7 us
    all_to_all x1, blocking collectives, shards(): got = lax.all_to_all(payload, 'bands', 0, 0, tiled=True)  19.7 us
    all_to_all x1, blocking collectives, shards(): got = lax.all_to_all(block, 'bands', 0, 0, tiled=True)  14.7 us
    pallas_call x7, Pallas kernels, call(): pl.pallas_call(kernel, grid=(1,), in_specs=[full(a.shape) for a in args],...  9.41 us
    all_to_all x1, blocking collectives, shards(): partial = lax.all_to_all(partial, 'bands', 0, 0, tiled=True)  9.39 us
    unnamed x28, local copies, waits for them, and re-layouts  7.25 us
    ppermute x4, waiting for transfers between devices, passed_along(): return lax.ppermute(block, axis, route)  6 us
  transfers between devices with their start and end apart: 4, of which 3 were waited for; matrix products, arithmetic and copies ran while one was open for 0% of the time, Pallas kernels for 0%

profile of v2, /device:TPU:1, one launch (start us, length us, event | category | flops | bytes accessed | tf_op | source)
XLA Modules:
  0.0 116.4 jit_solution(7953028510368640309)
XLA Ops:
  0.6 0.9 copy-done.3
  1.5 0.7 copy-done.6
  2.3 0.7 copy-done.7
  3.0 0.7 copy-done.11
  3.6 0.1 shard_map.140.c_ref
  3.8 6.6 %collective-permute-start = (bf16[32,2304]{1,0:T(8,128)(2,1)S(1)}, bf16[32,2304]{1,0:T(8,128)(2,1)S(1)}, u32[]{:S(2)}, u32[]{:S(2)}) collective-permute-start(bf16[32,2304]{1,0:T(8,128)(2,1)S(1)} %shard_map.140.c_ref), channel_id=1, source_target_pairs={{496,0},{0,16},{16,32},{32,48},{48,64},{64,80},{80,96},{96,112},{1... | collective-permute-start | bytes 442376 | tf_op jit(solution)/shard_map/ppermute | solution.py:398
  10.4 9.7 %collective-permute-start.1 = (bf16[32,2304]{1,0:T(8,128)(2,1)S(1)}, bf16[32,2304]{1,0:T(8,128)(2,1)S(1)}, u32[]{:S(2)}, u32[]{:S(2)}) collective-permute-start(bf16[32,2304]{1,0:T(8,128)(2,1)S(1)} %shard_map.140.c_ref), channel_id=1, source_target_pairs={{16,0},{32,16},{48,32},{64,48},{80,64},{96,80},{112,96},{128,112},... | collective-permute-start | bytes 442376 | tf_op jit(solution)/shard_map/ppermute | solution.py:398
  20.1 4.0 %collective-permute-done.l_ref = bf16[32,2304]{1,0:T(8,128)(2,1)S(1)} collective-permute-done((bf16[32,2304]{1,0:T(8,128)(2,1)S(1)}, bf16[32,2304]{1,0:T(8,128)(2,1)S(1)}, u32[]{:S(2)}, u32[]{:S(2)}) %collective-permute-start) | collective-permute-done | bytes 147488 | tf_op jit(solution)/shard_map/ppermute | solution.py:398
  24.1 0.9 copy-done.2
  25.0 0.7 copy-done.5
  25.8 0.7 copy-done.9
  26.4 0.7 copy-done.10
  27.1 1.6 %shard_map.141 = bf16[32,12672]{1,0:T(8,128)(2,1)S(1)} custom-call(bf16[32,2304]{1,0:T(8,128)(2,1)S(1)} %shard_map.140.c_ref, bf16[32,2304]{1,0:T(8,128)(2,1)S(1)} %collective-permute-done.l_ref, bf16[32,2304]{1,0:T(8,128)(2,1)S(1)} %collective-permute-done.1.r_ref, f32[2,6,384]{2,1,0:T(8,128)S(1)} %copy-done.5, f32[6,128]{1,0:T(8,128)S(1)} %copy-done.9, ...), custom_call_target="tpu_custom_call" | custom-call | tf_op jit(solution)/shard_map/pallas_call | solution.py:384
  28.7 0.3 all_to_all.28
  29.0 19.7 %all_to_all.44 = bf16[16,2,12672]{2,1,0:T(2,128)(2,1)S(1)} all-to-all(bf16[16,2,12672]{2,1,0:T(2,128)(2,1)S(1)} %all_to_all.28), channel_id=1, replica_groups=mesh['cells'=32,'bands'=16] {'bands'}, dimensions={0} | all-to-all | bytes 1622016 | tf_op jit(solution)/shard_map/all_to_all | solution.py:422
  48.8 0.3 all_to_all.30.got
  49.1 0.9 copy-done
  50.1 3.4 %shard_map.142 = (bf16[32,2048]{1,0:T(8,128)(2,1)S(1)}, f32[8,3,32,256]{3,2,1,0:T(8,128)S(1)}) custom-call(bf16[32,12672]{1,0:T(8,128)(2,1)S(1)} %all_to_all.30.got, bf16[3,768,256]{2,1,0:T(8,128)(2,1)S(1)} %copy-done, f32[6,256]{1,0:T(8,128)S(1)} %copy-done.4, bf16[32,64]{1,0:T(8,128)(2,1)S(1)} %copy-done.8, bf16[128,1024]{1,0:T(8,128)(2,1)S(1)} %copy-done.1), custom_call_target="tpu_custom_call" | custom-call | tf_op jit(solution)/shard_map/pallas_call | solution.py:384
  53.5 4.7 %collective-permute-start.2 = (bf16[32,2048]{1,0:T(8,128)(2,1)S(1)}, bf16[32,2048]{1,0:T(8,128)(2,1)S(1)}, u32[]{:S(2)}, u32[]{:S(2)}) collective-permute-start(bf16[32,2048]{1,0:T(8,128)(2,1)S(1)} %get-tuple-element.6.c_ref), channel_id=1, source_target_pairs={{496,0},{0,16},{16,32},{32,48},{48,64},{64,80},{80,96},{96,112},{1... | collective-permute-start | bytes 393224 | tf_op jit(solution)/shard_map/ppermute | solution.py:398
  58.2 6.1 %collective-permute-start.3 = (bf16[32,2048]{1,0:T(8,128)(2,1)S(1)}, bf16[32,2048]{1,0:T(8,128)(2,1)S(1)}, u32[]{:S(2)}, u32[]{:S(2)}) collective-permute-start(bf16[32,2048]{1,0:T(8,128)(2,1)S(1)} %get-tuple-element.6.c_ref), channel_id=1, source_target_pairs={{16,0},{32,16},{48,32},{64,48},{80,64},{96,80},{112,96},{128,112},... | collective-permute-start | bytes 393224 | tf_op jit(solution)/shard_map/ppermute | solution.py:398
  64.3 0.2 copy.18
  64.4 0.3 copy.16
  64.8 1.8 %collective-permute-done.2.l_ref = bf16[32,2048]{1,0:T(8,128)(2,1)S(1)} collective-permute-done((bf16[32,2048]{1,0:T(8,128)(2,1)S(1)}, bf16[32,2048]{1,0:T(8,128)(2,1)S(1)}, u32[]{:S(2)}, u32[]{:S(2)}) %collective-permute-start.2) | collective-permute-done | bytes 131104 | tf_op jit(solution)/shard_map/ppermute | solution.py:398
  66.6 0.3 collective-permute-done.3.r_ref
  66.8 2.8 %shard_map.143 = bf16[32,6144]{1,0:T(8,128)(2,1)S(1)} custom-call(bf16[32,2048]{1,0:T(8,128)(2,1)S(1)} %get-tuple-element.6.c_ref, bf16[32,2048]{1,0:T(8,128)(2,1)S(1)} %collective-permute-done.2.l_ref, bf16[32,2048]{1,0:T(8,128)(2,1)S(1)} %collective-permute-done.3.r_ref, bf16[32,4096]{1,0:T(8,128)(2,1)S(1)} %bitcast.16, bf16[3,768,256]{2,1,0:T(8,128)(2,1)S(1)} %copy-done, ...), custom_call_target="tpu_custom_call" | custom-call | tf_op jit(solution)/shard_map/pallas_call | solution.py:384
  69.7 0.3 all_to_all.31
  69.9 14.7 %all_to_all.45 = bf16[16,2,6144]{2,1,0:T(2,128)(2,1)S(1)} all-to-all(bf16[16,2,6144]{2,1,0:T(2,128)(2,1)S(1)} %all_to_all.31), channel_id=1, replica_groups=mesh['cells'=32,'bands'=16] {'bands'}, dimensions={0} | all-to-all | bytes 786432 | tf_op jit(solution)/shard_map/all_to_all | solution.py:442
  84.6 0.1 all_to_all.33.got
  84.8 0.8 shard_map.144
  85.6 9.4 %all_to_all.46 = f32[16,2,128]{2,1,0:T(2,128)S(1)} all-to-all(f32[16,2,128]{2,1,0:T(2,128)S(1)} %bitcast.22), channel_id=1, replica_groups=mesh['cells'=32,'bands'=16] {'bands'}, dimensions={0} | all-to-all | bytes 32768 | tf_op jit(solution)/shard_map/all_to_all | solution.py:449
  95.0 20.7 %all_to_all.47 = f32[32,1,128]{2,1,0:T(1,128)S(1)} all-to-all(f32[32,1,128]{2,1,0:T(1,128)S(1)} %bitcast.18), channel_id=1, replica_groups=mesh['cells'=32,'bands'=16] {'cells'}, dimensions={0} | all-to-all | bytes 32768 | tf_op jit(solution)/shard_map/all_to_all | solution.py:451
  115.8 0.6 shard_map.146
  (20 shorter events, 0.2 us)
Async XLA Ops:
  0.6 0.9 copy-start.3
  1.5 0.7 copy-start.6
  2.3 0.7 copy-start.7
  3.0 0.7 copy-start.11
  3.8 20.3 %collective-permute-start = (bf16[32,2304]{1,0:T(8,128)(2,1)S(1)}, bf16[32,2304]{1,0:T(8,128)(2,1)S(1)}, u32[]{:S(2)}, u32[]{:S(2)}) collective-permute-start(bf16[32,2304]{1,0:T(8,128)(2,1)S(1)} %shard_map.140.c_ref), channel_id=1, source_target_pairs={{496,0},{0,16},{16,32},{32,48},{48,64},{64,80},{80,96},{96,112},{1... | collective-permute-start | bytes 442376 | tf_op jit(solution)/shard_map/ppermute | solution.py:398
  10.4 13.7 %collective-permute-start.1 = (bf16[32,2304]{1,0:T(8,128)(2,1)S(1)}, bf16[32,2304]{1,0:T(8,128)(2,1)S(1)}, u32[]{:S(2)}, u32[]{:S(2)}) collective-permute-start(bf16[32,2304]{1,0:T(8,128)(2,1)S(1)} %shard_map.140.c_ref), channel_id=1, source_target_pairs={{16,0},{32,16},{48,32},{64,48},{80,64},{96,80},{112,96},{128,112},... | collective-permute-start | bytes 442376 | tf_op jit(solution)/shard_map/ppermute | solution.py:398
  24.1 0.9 copy-start.2
  25.0 0.7 copy-start.5
  25.7 0.7 copy-start.9
  26.4 0.7 copy-start.10
  48.7 1.3 %copy-start = (bf16[3,768,256]{2,1,0:T(8,128)(2,1)S(1)}, bf16[3,768,256]{2,1,0:T(8,128)(2,1)}, u32[]{:S(2)}) copy-start(bf16[3,768,256]{2,1,0:T(8,128)(2,1)} %constant.18.clone.w_ref) | copy-start | bytes 3538948
  48.7 1.3 %copy-start.1 = (bf16[128,1024]{1,0:T(8,128)(2,1)S(1)}, bf16[128,1024]{1,0:T(8,128)(2,1)}, u32[]{:S(2)}) copy-start(bf16[128,1024]{1,0:T(8,128)(2,1)} %constant.25.clone.spread_ref) | copy-start | bytes 786436
  48.8 1.3 %copy-start.4 = (f32[6,256]{1,0:T(8,128)S(1)}, f32[6,256]{1,0:T(8,128)}, u32[]{:S(2)}) copy-start(f32[6,256]{1,0:T(8,128)} %constant.19.clone.lines_ref) | copy-start | bytes 18436
  48.8 1.3 %copy-start.8 = (bf16[32,64]{1,0:T(8,128)(2,1)S(1)}, bf16[32,64]{1,0:T(8,128)(2,1)}, u32[]{:S(2)}) copy-start(bf16[32,64]{1,0:T(8,128)(2,1)} %constant.26.clone.pairs_ref) | copy-start | bytes 12292
  50.1 14.2 %copy-start.12 = (bf16[4,32768]{1,0:T(4,128)(2,1)S(1)}, bf16[4,32768]{1,0:T(4,128)(2,1)}, u32[]{:S(2)}) copy-start(bf16[4,32768]{1,0:T(4,128)(2,1)} %param.14) | copy-start | bytes 786436
  53.5 13.1 %collective-permute-start.2 = (bf16[32,2048]{1,0:T(8,128)(2,1)S(1)}, bf16[32,2048]{1,0:T(8,128)(2,1)S(1)}, u32[]{:S(2)}, u32[]{:S(2)}) collective-permute-start(bf16[32,2048]{1,0:T(8,128)(2,1)S(1)} %get-tuple-element.6.c_ref), channel_id=1, source_target_pairs={{496,0},{0,16},{16,32},{32,48},{48,64},{64,80},{80,96},{96,112},{1... | collective-permute-start | bytes 393224 | tf_op jit(solution)/shard_map/ppermute | solution.py:398
  58.2 8.6 %collective-permute-start.3 = (bf16[32,2048]{1,0:T(8,128)(2,1)S(1)}, bf16[32,2048]{1,0:T(8,128)(2,1)S(1)}, u32[]{:S(2)}, u32[]{:S(2)}) collective-permute-start(bf16[32,2048]{1,0:T(8,128)(2,1)S(1)} %get-tuple-element.6.c_ref), channel_id=1, source_target_pairs={{16,0},{32,16},{48,32},{64,48},{80,64},{96,80},{112,96},{128,112},... | collective-permute-start | bytes 393224 | tf_op jit(solution)/shard_map/ppermute | solution.py:398

commit v3 on v2

v3 whole, which is shorter than its diff:
```python
import functools
import math

import jax
import jax.numpy as jnp
import ml_dtypes
import numpy as np
from jax import lax
from jax.experimental import pallas as pl
from jax.experimental.pallas import tpu as pltpu
from jax.sharding import PartitionSpec as P

NWF = 32
DEGREE = 4
STEPS = 2
NXL = 8
NODES_DEV = 2048
PLANE = 256
LANES_V = 384
MESSAGE = NODES_DEV + 256
V_AT = 3 * NODES_DEV
G_AT = 5 * NODES_DEV
PAYLOAD = G_AT + 2 * 128
X_ORDER = (0, 4, 1, 3, 5, 7, 2, 6)
CLASS_ROWS = ((0, 2), (2, 6), (6, 8))
VMEM = 48 * 1024 * 1024


def kinetic_table():
    points = [-1.0, -math.sqrt(3.0 / 7.0), 0.0, math.sqrt(3.0 / 7.0), 1.0]
    weights = [0.1, 49.0 / 90.0, 32.0 / 45.0, 49.0 / 90.0, 0.1]
    scales = []
    for row in range(5):
        prod_val = 1.0
        for other in range(5):
            if other != row:
                prod_val = prod_val * (points[row] - points[other])
        scales.append(prod_val)
    deriv = [[0.0] * 5 for row in range(5)]
    for row in range(5):
        for col in range(5):
            if row != col:
                deriv[row][col] = scales[row] / scales[col] / (points[row] - points[col])
            else:
                total = 0.0
                for other in range(5):
                    if other != row:
                        total = total + 1.0 / (points[row] - points[other])
                deriv[row][col] = total
    stiff_one = [
        [sum((deriv[i][a] * weights[i] * deriv[i][b] for i in range(5))) for b in range(5)]
        for a in range(5)
    ]
    mass_one = [[weights[a] if a == b else 0.0 for b in range(5)] for a in range(5)]
    table = [[0.0] * 125 for row in range(125)]
    for k in range(125):
        ka, kb, kc = (k // 25, k // 5 % 5, k % 5)
        for j in range(125):
            ja, jb, jc = (j // 25, j // 5 % 5, j % 5)
            table[k][j] = 0.5 * (
                stiff_one[ka][ja] * mass_one[kb][jb] * mass_one[kc][jc]
                + mass_one[ka][ja] * stiff_one[kb][jb] * mass_one[kc][jc]
                + mass_one[ka][ja] * mass_one[kb][jb] * stiff_one[kc][jc]
            )
    assembled = [dict() for row in range(512)]
    for cell_x in range(2):
        for cell_y in range(2):
            for cell_z in range(2):
                global_ids = []
                for k in range(125):
                    node_x = (4 * cell_x + k // 25) % 8
                    node_y = (4 * cell_y + k // 5 % 5) % 8
                    node_z = (4 * cell_z + k % 5) % 8
                    global_ids.append((node_x * 8 + node_y) * 8 + node_z)
                for k in range(125):
                    row_map = assembled[global_ids[k]]
                    for j in range(125):
                        target = global_ids[j]
                        row_map[target] = row_map.get(target, 0.0) + table[k][j]
    largest = 0.0
    for row_map in assembled:
        total = sum((abs(value) for value in row_map.values()))
        largest = max(largest, total)
    bound = largest + 8.0 * 2.0
    return (np.array(table), float(0.55 * bound), float(0.45 * bound))


@functools.lru_cache(maxsize=None)
def tables():
    table, centre, half = kinetic_table()
    kin = table.astype(np.float32).astype(ml_dtypes.bfloat16).astype(np.float64)
    kin = kin.reshape(5, 5, 5, 5, 5, 5)
    planes = np.zeros((3, 3, PLANE, PLANE))
    lines = np.zeros((5, 5, PLANE))
    for j in range(-1, 5):
        for l in range(-1, 5):
            for b in range(5):
                for c in range(5):
                    y, z = 4 * j + b, 4 * l + c
                    if not (0 <= y < 16 and 0 <= z < 16):
                        continue
                    at = 16 * y + z
                    for a in range(5):
                        for other in range(5):
                            if other != a:
                                lines[a, other, at] += kin[a, b, c, other, b, c]
                    for b2 in range(5):
                        for c2 in range(5):
                            y2, z2 = 4 * j + b2, 4 * l + c2
                            far_y, far_z = y2 // 16, z2 // 16
                            source = 16 * (y2 % 16) + z2 % 16
                            for kind, locals_a in enumerate(((0, 4), (1,), (2,))):
                                value = sum(kin[a, b, c, a, b2, c2] for a in locals_a)
                                if value == 0.0:
                                    continue
                                assert far_y == 0 or far_z == 0
                                part = 1 if far_y else 2 if far_z else 0
                                planes[kind, part, source, at] += value
    line_rows = np.stack(
        [lines[0, 1], lines[0, 2], lines[0, 3], 2.0 * lines[0, 4], lines[1, 2], lines[1, 3]]
    )
    bf = ml_dtypes.bfloat16
    weights = np.zeros((3 * 3 * PLANE + 16, PLANE))
    weights[: 9 * PLANE] = planes.reshape(9 * PLANE, PLANE)
    weights[9 * PLANE : 9 * PLANE + 6] = line_rows
    return weights.astype(np.float32).astype(bf), centre, half


def iota(shape, dim):
    return lax.broadcasted_iota(jnp.int32, shape, dim)


def local_node(k):
    a = (k * 41) >> 10
    rest = k - 25 * a
    b = (rest * 205) >> 10
    return a, b, rest - 5 * b


def message_kernel(v_hbm, pot_hbm, conn_hbm, out_ref, raw, conn, pot, sems):
    copies = [
        pltpu.make_async_copy(pot_hbm, raw, sems.at[0]),
        pltpu.make_async_copy(conn_hbm, conn, sems.at[1]),
        pltpu.make_async_copy(v_hbm, out_ref.at[:, :NODES_DEV], sems.at[2]),
    ]
    for copy in copies:
        copy.start()
    lane = iota((32, 128), 1)
    code = (4 * (lane >> 4) * 17 + 4 * ((lane >> 2) & 3)) * 17 + 4 * (lane & 3)
    pot[...] = jnp.zeros_like(pot)
    copies[0].wait()
    copies[1].wait()
    pot[:, :125] = raw[...]
    here = jnp.where((conn[:, 0:1] == code) & (lane < 32), lane.astype(jnp.float32), 0.0)
    cell = jnp.sum(here, axis=1, keepdims=True)
    high = pot[...].astype(jnp.bfloat16).astype(jnp.float32)
    low = pot[...] - high
    out_ref[:, NODES_DEV : NODES_DEV + 128] = jnp.where(lane == 127, cell, high).astype(jnp.bfloat16)
    out_ref[:, NODES_DEV + 128 :] = low.astype(jnp.bfloat16)
    copies[2].wait()


def pick_kind(kind):
    a, b, c = local_node(iota((1, 128), 1))
    if kind < 4:
        hit = (b == 4) == (kind >= 2), (c == 4) == (kind % 2 == 1)
    else:
        hit = (b == 4) == (kind == 5), c == 4
    return jnp.where(hit[0] & hit[1] & (iota((1, 128), 1) < 125), 1.0, 0.0)


def place_of(i, kind):
    lane = iota((1, LANES_V), 1)
    y, z = lane >> 4, lane & 15
    j = (y >> 2) - (kind // 2 if kind < 4 else kind - 4)
    l = (z >> 2) - kind % 2 if kind < 4 else jnp.where(z == 0, 3, -1)
    good = (lane < PLANE + 16) & (j >= 0) & (j < 4) & (l >= 0)
    return jnp.where(good, 16 * i + 4 * j + l, -1).astype(jnp.float32)


def nodal(own, left, mask):
    sides = [(own, range(4))] + ([(left, range(4, 6))] if left is not None else [])
    rows, ones = [], ([], [])
    for message, kind_range in sides:
        high = message[:, NODES_DEV : NODES_DEV + 128].astype(jnp.float32)
        low = message[:, NODES_DEV + 128 :].astype(jnp.float32)
        cell = high[:, 127:128]
        for kind in kind_range:
            pick = pick_kind(kind)
            rows += [high * pick, low * pick]
            for i in range(2):
                one = jnp.where(cell == place_of(i, kind), 1.0, 0.0)
                ones[i].extend([one, one])
    stack = jnp.concatenate(rows, axis=0).astype(jnp.bfloat16)
    total = jnp.zeros((8, LANES_V), jnp.float32)
    k = iota((8, 128), 1)
    along = local_node(k)[0]
    for i in range(2):
        placed = jnp.concatenate(ones[i], axis=0).astype(jnp.bfloat16)
        values = lax.dot_general(
            stack, placed, (((0,), (0,)), ((), ())), preferred_element_type=jnp.float32
        )
        values = values * mask
        high = values.astype(jnp.bfloat16)
        low = (values - high.astype(jnp.float32)).astype(jnp.bfloat16)
        to_x = jnp.where((((4 * i + along) & 7) == iota((8, 128), 0)) & (k < 125), 1.0, 0.0)
        to_x = to_x.astype(jnp.bfloat16)
        total += jnp.dot(to_x, high, preferred_element_type=jnp.float32)
        total += jnp.dot(to_x, low, preferred_element_type=jnp.float32)
    return total


def pack_kernel(c_ref, l_ref, r_ref, out_ref, ghost):
    messages = (l_ref, c_ref, r_ref)
    even = iota((32, PLANE), 0) % 2 == 0
    a, b, c = local_node(iota((128, LANES_V), 0))
    lane = iota((128, LANES_V), 1)
    fits = ((b & 3) == ((lane >> 4) & 3)) & ((c & 3) == (lane & 3)) & (lane < PLANE + 16)
    mask = jnp.where(fits, 1.0, 0.0)
    totals = []
    for s, message in enumerate(messages):
        out_ref[:, NODES_DEV * s : NODES_DEV * (s + 1)] = message[:, :NODES_DEV]
        totals.append(nodal(message, messages[s - 1] if s else None, mask))
    high = totals[1].astype(jnp.bfloat16).astype(jnp.float32)
    for part, (first, second) in enumerate(((high, totals[1] - high), (totals[0], totals[2]))):
        for x in range(NXL):
            main = jnp.where(even, first[x : x + 1, :PLANE], second[x : x + 1, :PLANE])
            at = V_AT + NODES_DEV * part + PLANE * x
            out_ref[:, at : at + PLANE] = main.astype(jnp.bfloat16)
            edge = jnp.where(even[:, :128], first[x : x + 1, PLANE:], second[x : x + 1, PLANE:])
            ghost[:, 16 * x : 16 * (x + 1)] = edge[:, :16]
        at = G_AT + 128 * part
        out_ref[:, at : at + 128] = ghost[...].astype(jnp.bfloat16)


def diagonal(got, g_ref, centre):
    lane, row = iota((128, NXL * 128), 1), iota((128, NXL * 128), 0)
    spread = jnp.where(((row >> 4) == (lane >> 7)) & ((row & 15) == (lane & 127)), 1.0, 0.0)
    spread = spread.astype(jnp.bfloat16)
    lane, row = iota((32, 64), 1), iota((32, 64), 0)
    source = jnp.where(lane < 32, row >> 1, ((row >> 1) + 15) & 15)
    same = source == ((lane & 31) >> 1)
    pairs = [
        jnp.where(same & good, 1.0, 0.0).astype(jnp.bfloat16)
        for good in ((lane & 1) == 0, lane >= 0, (lane & 1) == 1)
    ]
    edges = []
    for part in range(2):
        at = G_AT + 128 * part
        edge = jnp.dot(got[:, at : at + 128], spread, preferred_element_type=jnp.float32)
        edges.append(edge.astype(jnp.bfloat16))
    for s in range(3):
        part = 0 if s == 1 else 1
        for x in range(NXL):
            at = V_AT + NODES_DEV * part + PLANE * x
            stack = jnp.concatenate([got[:, at : at + 128], edges[part][:, 128 * x : 128 * (x + 1)]], axis=0)
            g_ref[x, s, :, :128] = jnp.dot(pairs[s], stack, preferred_element_type=jnp.float32) - centre
            g_ref[x, s, :, 128:] = (
                jnp.dot(pairs[s][:, :32], got[:, at + 128 : at + PLANE], preferred_element_type=jnp.float32)
                - centre
            )


def filter_step(slabs, w_ref, g_ref, out_ref, cur, prev, acc, half, ready):
    place = {x: at for at, x in enumerate(X_ORDER)}
    right_lanes = lax.broadcasted_iota(jnp.int32, (32, PLANE), 1) % 16 < 8
    for s, slab in enumerate(slabs):
        for x in range(NXL):
            block = slab[:, PLANE * x : PLANE * (x + 1)]
            cur[place[x], s, :, :PLANE] = block
            turn(cur, place[x], s, 0, block[:, :128].astype(jnp.float32))
            turn(cur, place[x], s, 1, block[:, 128:].astype(jnp.float32))
    prev[...] = jnp.zeros_like(prev)
    ready()
    lines = w_ref[9 * PLANE :, :].astype(jnp.float32)

    def weight(kind):
        return w_ref[3 * PLANE * kind : 3 * PLANE * (kind + 1), :]

    def sides():
        for at in range(NXL):
            left, middle, right = (cur[at, s, :, :PLANE].astype(jnp.float32) for s in range(3))
            zero = jnp.zeros_like(left)
            cur[at, 0, :, 2 * PLANE :] = jnp.where(right_lanes, middle, zero).astype(jnp.bfloat16)
            cur[at, 1, :, 2 * PLANE :] = jnp.where(right_lanes, right, left).astype(jnp.bfloat16)
            cur[at, 2, :, 2 * PLANE :] = jnp.where(right_lanes, zero, middle).astype(jnp.bfloat16)

    def apply(which, alpha, beta, store):
        first, last = which[0], which[-1] + 1
        for kind, (low, high) in enumerate(CLASS_ROWS):
            rows = cur[low:high, first:last]
            count = (high - low) * (last - first) * 32
            result = jnp.dot(
                rows.reshape(count, 3 * PLANE), weight(kind), preferred_element_type=jnp.float32
            )
            acc[low:high, first:last] = result.reshape(high - low, last - first, 32, PLANE)
        for s in which:
            for part in range(2):
                lanes = slice(128 * part, 128 * (part + 1))
                v = [cur[place[x], s, :, lanes].astype(jnp.float32) for x in range(NXL)]
                c01, c02, c03, c04, c12, c13 = (lines[row : row + 1, lanes] for row in range(6))
                s17, s26, s35 = v[1] + v[7], v[2] + v[6], v[3] + v[5]
                s04 = c02 * (v[0] + v[4])
                extra = {
                    0: c01 * s17 + c02 * s26 + c03 * s35 + c04 * v[4],
                    4: c01 * s35 + c02 * s26 + c03 * s17 + c04 * v[0],
                    1: c01 * v[0] + c12 * v[2] + c13 * v[3] + c03 * v[4],
                    3: c01 * v[4] + c12 * v[2] + c13 * v[1] + c03 * v[0],
                    5: c01 * v[4] + c12 * v[6] + c13 * v[7] + c03 * v[0],
                    7: c01 * v[0] + c12 * v[6] + c13 * v[5] + c03 * v[4],
                    2: s04 + c12 * (v[1] + v[3]),
                    6: s04 + c12 * (v[5] + v[7]),
                }
                for x in range(NXL):
                    at = place[x]
                    applied = acc[at, s, :, lanes] + extra[x] + g_ref[x, s, :, lanes] * v[x]
                    store(x, at, s, part, alpha * applied - beta * prev[at, s, :, lanes].astype(jnp.float32))

    def keep(x, at, s, part, new):
        lanes = slice(128 * part, 128 * (part + 1))
        prev[at, s, :, lanes] = cur[at, s, :, lanes]
        new = new.astype(jnp.bfloat16)
        cur[at, s, :, lanes] = new
        turn(cur, at, s, part, new.astype(jnp.float32))

    def emit(x, at, s, part, new):
        out_ref[:, PLANE * x + 128 * part : PLANE * x + 128 * (part + 1)] = new.astype(jnp.bfloat16)

    def order(k, carry):
        sides()
        alpha = jnp.where(k == 0, jnp.float32(1.0 / half), jnp.float32(2.0 / half))
        beta = jnp.where(k == 0, jnp.float32(0.0), jnp.float32(1.0))
        apply((0, 1, 2), alpha, beta, keep)
        return carry

    lax.fori_loop(0, DEGREE - 1, order, 0)
    sides()
    apply((1,), jnp.float32(2.0 / half), jnp.float32(1.0), emit)


def turn(cur, at, s, part, value):
    shift = 30 if part == 0 else 2
    lanes = slice(PLANE + 128 * part, PLANE + 128 * (part + 1))
    cur[at, s, :, lanes] = pltpu.roll(value, shift, 0).astype(jnp.bfloat16)


def first_kernel(centre, half, got, w_hbm, out_ref, g_ref, cur, prev, acc, w_ref, sem):
    copy = pltpu.make_async_copy(w_hbm, w_ref, sem)
    copy.start()
    diagonal(got, g_ref, centre)
    slabs = [got.at[:, NODES_DEV * s : NODES_DEV * (s + 1)] for s in range(3)]
    filter_step(slabs, w_ref, g_ref, out_ref, cur, prev, acc, half, copy.wait)


def later_kernel(
    half, factor, c_ref, l_ref, r_ref, g_ref, w_hbm, st_hbm, out_ref, cur, prev, acc, w_ref, st_ref, sem, st_sem
):
    copy = pltpu.make_async_copy(w_hbm, w_ref, sem)
    copy.start()
    st_copy = pltpu.make_async_copy(st_hbm, st_ref, st_sem)
    st_copy.start()
    filter_step((l_ref, c_ref, r_ref), w_ref, g_ref, out_ref, cur, prev, acc, half, copy.wait)
    st_copy.wait()
    filtered = out_ref[:, :NODES_DEV]
    shape = (NWF, 256)
    lane, row = iota(shape, 1), iota(shape, 0)
    own = ((lane >> 2) & 15) == (row >> 1)
    even = (iota((NWF, 128), 0) & 1) == 0
    lane, row = iota((NWF, 128), 1), iota((NWF, 128), 0)
    result = jnp.zeros((NWF, 128), jnp.float32)
    for block in range(4):
        product = lax.dot_general(
            filtered,
            st_ref[256 * block : 256 * (block + 1), :],
            (((1,), (1,)), ((), ())),
            preferred_element_type=jnp.float32,
        )
        product = jnp.where(own, product * factor, 0.0)
        for side in range(2):
            values = product[:, 128 * side : 128 * (side + 1)]
            first = jnp.sum(jnp.where(even, values, 0.0), axis=0, keepdims=True)
            second = jnp.sum(jnp.where(even, 0.0, values), axis=0, keepdims=True)
            values = jnp.where(even, first, second)
            for shift in (4, 8, 16, 32):
                values = values + pltpu.roll(values, shift, 1)
            here = (row >> 2) == 2 * block + side
            here = here & ((lane >> 2) == 15 + 16 * ((row >> 1) & 1))
            result = jnp.where(here, values, result)
    for part in range(3):
        rounded = result.astype(jnp.bfloat16)
        out_ref[:, NODES_DEV + 128 * part : NODES_DEV + 128 * (part + 1)] = rounded
        result = result - rounded.astype(jnp.float32)


def share_kernel(got, out_ref):
    parts = [
        got[:, NODES_DEV + 128 * part : NODES_DEV + 128 * (part + 1)].astype(jnp.float32) for part in range(3)
    ]
    out_ref[...] = parts[0] + (parts[1] + parts[2])


def total_kernel(got, out_ref):
    total = jnp.sum(got[...], axis=0, keepdims=True)
    lane = iota((1, 128), 1)
    rows = jnp.zeros((1, 128), jnp.float32)
    for row in range(4):
        mine = jnp.where((lane & 3) == row, total, 0.0)
        rows = jnp.where(lane == row, jnp.sum(mine, axis=1, keepdims=True), rows)
    out_ref[...] = rows[:, :4]


def full(shape):
    return pl.BlockSpec(shape, lambda *_: (0,) * len(shape))


def call(kernel, args, outs, scratch=(), far=(), limit=VMEM):
    hbm = pl.BlockSpec(memory_space=pltpu.HBM)
    return pl.pallas_call(
        kernel,
        grid=(1,),
        in_specs=[full(a.shape) for a in args] + [hbm] * len(far),
        out_specs=[full(o.shape) for o in outs],
        out_shape=list(outs),
        scratch_shapes=list(scratch),
        compiler_params=pltpu.CompilerParams(vmem_limit_bytes=limit),
    )(*args, *far)


def passed_along(block, axis, distance):
    devices = range(lax.axis_size(axis))
    route = [((i - distance) % len(devices), i) for i in devices]
    return lax.ppermute(block, axis, route)


def shards(cur_block, stored_blocks, cell_potential, connectivity):
    weights, centre, half = tables()
    weights = jnp.asarray(weights)
    bf, f32 = jnp.bfloat16, jnp.float32
    shape = jax.ShapeDtypeStruct
    n_cells, n_bands = lax.axis_size("cells"), lax.axis_size("bands")
    stored = stored_blocks.reshape(4, n_bands, NODES_DEV).transpose(1, 0, 2).reshape(4 * n_bands, NODES_DEV)
    stored = lax.all_gather(stored, "bands", axis=0, tiled=True)
    dma = pltpu.SemaphoreType.DMA
    (message,) = call(
        message_kernel,
        (),
        [shape((NWF, MESSAGE), bf)],
        [
            pltpu.VMEM((32, 125), f32),
            pltpu.VMEM((32, 125), jnp.int32),
            pltpu.VMEM((32, 128), f32),
            dma((3,)),
        ],
        (cur_block, cell_potential.T, connectivity.T),
        62 * 1024 * 1024,
    )
    left = passed_along(message, "cells", 1)
    right = passed_along(message, "cells", -1)
    (payload,) = call(
        pack_kernel,
        (message, left, right),
        [shape((NWF, PAYLOAD), bf)],
        [pltpu.VMEM((32, 128), f32)],
    )
    got = lax.all_to_all(payload, "bands", 0, 0, tiled=True)
    scratch = [
        pltpu.VMEM((NXL, 3, NWF, 3 * PLANE), bf),
        pltpu.VMEM((NXL, 3, NWF, PLANE), bf),
        pltpu.VMEM((NXL, 3, NWF, PLANE), f32),
        pltpu.VMEM(weights.shape, bf),
    ]
    block, diag = call(
        functools.partial(first_kernel, centre, half),
        (got,),
        [shape((NWF, NODES_DEV), bf), shape((NXL, 3, NWF, PLANE), f32)],
        scratch + [dma],
        (weights,),
    )
    left = passed_along(block, "cells", 1)
    right = passed_along(block, "cells", -1)
    factor = 1.0 / math.sqrt(NODES_DEV * n_cells * n_bands)
    (block,) = call(
        functools.partial(later_kernel, half, factor),
        (block, left, right, diag),
        [shape((NWF, NODES_DEV + 3 * 128), bf)],
        scratch + [pltpu.VMEM(stored.shape, bf), dma, dma],
        (weights, stored),
    )
    got = lax.all_to_all(block, "bands", 0, 0, tiled=True)
    filtered = got[:, :NODES_DEV]
    (partial,) = call(share_kernel, (got,), [shape((NWF, 128), f32)])
    partial = lax.all_to_all(partial, "cells", 0, 0, tiled=True)
    (total,) = call(total_kernel, (partial,), [shape((1, 4), f32)])
    return (filtered, total.T)


def solution(mesh):
    in_specs = (
        P(None, ("cells", "bands")),
        P("bands", "cells"),
        P(None, ("cells", "bands")),
        P(None, ("cells", "bands")),
    )
    out_specs = (P(None, ("cells", "bands")), P("bands", "cells"))
    return jax.shard_map(shards, mesh=mesh, in_specs=in_specs, out_specs=out_specs, check_vma=False)
```

time: 117 us -> 123 us (1.051)
  blocking collectives: 64.6 us -> 36.3 us
  waiting for transfers between devices: 6 us -> 28.3 us
  between operations: 0.76 us -> 14.1 us
  local copies, waits for them, and re-layouts: 8.55 us -> 4.04 us
  Pallas kernels: 9.41 us -> 12.8 us
    all_to_all x2 -> x0, blocking collectives: 30.1 us -> none  [the longest x1 20.7 us: shards(): partial = lax.all_to_all(partial, 'cells', 0, 0, tiled=True)]
    ppermute x4, waiting for transfers between devices: 6 us -> 18 us  [passed_along(): return lax.ppermute(block, axis, route)]
    all_to_all x0 -> x1, waiting for transfers between devices: none -> 10.3 us  [shards(): partial = lax.all_to_all(partial, 'cells', 0, 0, tiled=True)]
    unnamed x28 -> x4, local copies, waits for them, and re-layouts: 7.25 us -> 0.94 us
    all_to_all x1, blocking collectives: 19.7 us -> 24.8 us  [shards(): got = lax.all_to_all(payload, 'bands', 0, 0, tiled=True)]
    ppermute x4, starting transfers between devices: 27.1 us -> 22.5 us  [passed_along(): return lax.ppermute(block, axis, route)]
    all_to_all x0 -> x1, starting transfers between devices: none -> 4.53 us  [shards(): partial = lax.all_to_all(partial, 'cells', 0, 0, tiled=True)]
    pallas_call x7 -> x6, Pallas kernels: 9.41 us -> 12.8 us  [call(): pl.pallas_call(kernel, grid=(1,), in_specs=[full(a.shape) for a in args]...]
  transfers between devices with their start and end apart: 4 -> 6, of which waited for: 3 -> 5; matrix products, arithmetic and copies ran while one was open for 0% -> 1% of each run, Pallas kernels for 0% -> 6%
where the time goes in v3:
time: 123 us
  blocking collectives  36.3 us (30%)
  waiting for transfers between devices  28.3 us (23%)
  starting transfers between devices  27.1 us (22%)
  between operations  14.1 us (11%)
  Pallas kernels  12.8 us (10%)
  local copies, waits for them, and re-layouts  4.04 us (3%)
    all_to_all x1, blocking collectives, shards(): got = lax.all_to_all(payload, 'bands', 0, 0, tiled=True)  24.8 us
    ppermute x4, starting transfers between devices, passed_along(): return lax.ppermute(block, axis, route)  22.5 us
    ppermute x4, waiting for transfers between devices, passed_along(): return lax.ppermute(block, axis, route)  18 us
    pallas_call x6, Pallas kernels, call(): pl.pallas_call(kernel, grid=(1,), in_specs=[full(a.shape) for a in args]...  12.8 us
    all_to_all x1, blocking collectives, shards(): got = lax.all_to_all(block, 'bands', 0, 0, tiled=True)  11.5 us
    all_to_all x1, waiting for transfers between devices, shards(): partial = lax.all_to_all(partial, 'cells', 0, 0, tiled=True)  10.3 us
    all_to_all x1, starting transfers between devices, shards(): partial = lax.all_to_all(partial, 'cells', 0, 0, tiled=True)  4.53 us
  transfers between devices with their start and end apart: 6, of which 5 were waited for; matrix products, arithmetic and copies ran while one was open for 1% of the time, Pallas kernels for 6%

profile of v3, /device:TPU:1, one launch (start us, length us, event | category | flops | bytes accessed | tf_op | source)
XLA Modules:
  0.0 122.6 jit_solution(4794166149355322771)
XLA Ops:
  7.2 0.0 copy-start
  7.2 0.0 all-gather.2.cloned.1.call-start
  7.2 1.8 %reshape.17 = bf16[64,2048]{1,0:T(8,128)(2,1)} reshape(bf16[16,4,2048]{2,1,0:T(4,128)(2,1)} %bitcast.11) | data formatting | bytes 524288 | tf_op jit(solution)/shard_map/reshape | solution.py:441
  9.0 0.0 all-gather.2.cloned.1.call-update
  9.1 1.6 %shard_map.68.c_ref = bf16[32,2304]{1,0:T(8,128)(2,1)} custom-call(bf16[32,2048]{1,0:T(8,128)(2,1)} %v_hbm.1, f32[32,125]{1,0:T(8,128)} %bitcast.12, s32[32,125]{1,0:T(8,128)} %bitcast.13), custom_call_target="tpu_custom_call" | custom-call | tf_op jit(solution)/shard_map/pallas_call | solution.py:418
  10.7 14.4 %collective-permute-start.1 = (bf16[32,2304]{1,0:T(8,128)(2,1)}, bf16[32,2304]{1,0:T(8,128)(2,1)S(1)}, u32[]{:S(2)}, u32[]{:S(2)}) collective-permute-start(bf16[32,2304]{1,0:T(8,128)(2,1)} %shard_map.68.c_ref), channel_id=1, source_target_pairs={{16,0},{32,16},{48,32},{64,48},{80,64},{96,80},{112,96},{128,112},... | collective-permute-start | bytes 442376 | tf_op jit(solution)/shard_map/ppermute | solution.py:432
  25.1 1.9 %collective-permute-start = (bf16[32,2304]{1,0:T(8,128)(2,1)}, bf16[32,2304]{1,0:T(8,128)(2,1)S(1)}, u32[]{:S(2)}, u32[]{:S(2)}) collective-permute-start(bf16[32,2304]{1,0:T(8,128)(2,1)} %shard_map.68.c_ref), channel_id=1, source_target_pairs={{496,0},{0,16},{16,32},{32,48},{48,64},{64,80},{80,96},{96,112},{1... | collective-permute-start | bytes 442376 | tf_op jit(solution)/shard_map/ppermute | solution.py:432
  27.0 0.9 collective-permute-done.1.r_ref
  27.9 9.7 %collective-permute-done.l_ref = bf16[32,2304]{1,0:T(8,128)(2,1)S(1)} collective-permute-done((bf16[32,2304]{1,0:T(8,128)(2,1)}, bf16[32,2304]{1,0:T(8,128)(2,1)S(1)}, u32[]{:S(2)}, u32[]{:S(2)}) %collective-permute-start) | collective-permute-done | bytes 147488 | tf_op jit(solution)/shard_map/ppermute | solution.py:432
  37.6 0.0 copy-start.1
  37.6 0.9 copy-done.1
  38.5 1.6 %shard_map.69 = bf16[32,10496]{1,0:T(8,128)(2,1)S(1)} custom-call(bf16[32,2304]{1,0:T(8,128)(2,1)S(1)} %copy-done.1, bf16[32,2304]{1,0:T(8,128)(2,1)S(1)} %collective-permute-done.l_ref, bf16[32,2304]{1,0:T(8,128)(2,1)S(1)} %collective-permute-done.1.r_ref), custom_call_target="tpu_custom_call" | custom-call | tf_op jit(solution)/shard_map/pallas_call | solution.py:418
  40.0 0.3 all_to_all.21
  40.3 24.8 %all_to_all.33 = bf16[16,2,10496]{2,1,0:T(2,128)(2,1)S(1)} all-to-all(bf16[16,2,10496]{2,1,0:T(2,128)(2,1)S(1)} %all_to_all.21), channel_id=1, replica_groups=mesh['cells'=32,'bands'=16] {'bands'}, dimensions={0} | all-to-all | bytes 1343488 | tf_op jit(solution)/shard_map/all_to_all | solution.py:465
  65.1 0.3 all_to_all.23.got
  65.3 0.0 copy-done
  65.3 3.6 %shard_map.70 = (bf16[32,2048]{1,0:T(8,128)(2,1)S(1)}, f32[8,3,32,256]{3,2,1,0:T(8,128)S(1)}) custom-call(bf16[32,10496]{1,0:T(8,128)(2,1)S(1)} %all_to_all.23.got, bf16[2320,256]{1,0:T(8,128)(2,1)S(1)} %copy-done), custom_call_target="tpu_custom_call" | custom-call | tf_op jit(solution)/shard_map/pallas_call | solution.py:418
  68.9 2.3 %collective-permute-start.3 = (bf16[32,2048]{1,0:T(8,128)(2,1)S(1)}, bf16[32,2048]{1,0:T(8,128)(2,1)S(1)}, u32[]{:S(2)}, u32[]{:S(2)}) collective-permute-start(bf16[32,2048]{1,0:T(8,128)(2,1)S(1)} %get-tuple-element.4.c_ref), channel_id=1, source_target_pairs={{16,0},{32,16},{48,32},{64,48},{80,64},{96,80},{112,96},{128,112},... | collective-permute-start | bytes 393224 | tf_op jit(solution)/shard_map/ppermute | solution.py:432
  71.2 3.9 %collective-permute-start.2 = (bf16[32,2048]{1,0:T(8,128)(2,1)S(1)}, bf16[32,2048]{1,0:T(8,128)(2,1)S(1)}, u32[]{:S(2)}, u32[]{:S(2)}) collective-permute-start(bf16[32,2048]{1,0:T(8,128)(2,1)S(1)} %get-tuple-element.4.c_ref), channel_id=1, source_target_pairs={{496,0},{0,16},{16,32},{32,48},{48,64},{64,80},{80,96},{96,112},{1... | collective-permute-start | bytes 393224 | tf_op jit(solution)/shard_map/ppermute | solution.py:432
  75.1 4.1 %collective-permute-done.3.r_ref = bf16[32,2048]{1,0:T(8,128)(2,1)S(1)} collective-permute-done((bf16[32,2048]{1,0:T(8,128)(2,1)S(1)}, bf16[32,2048]{1,0:T(8,128)(2,1)S(1)}, u32[]{:S(2)}, u32[]{:S(2)}) %collective-permute-start.3) | collective-permute-done | bytes 131104 | tf_op jit(solution)/shard_map/ppermute | solution.py:432
  79.2 3.3 %collective-permute-done.2.l_ref = bf16[32,2048]{1,0:T(8,128)(2,1)S(1)} collective-permute-done((bf16[32,2048]{1,0:T(8,128)(2,1)S(1)}, bf16[32,2048]{1,0:T(8,128)(2,1)S(1)}, u32[]{:S(2)}, u32[]{:S(2)}) %collective-permute-start.2) | collective-permute-done | bytes 131104 | tf_op jit(solution)/shard_map/ppermute | solution.py:432
  82.6 0.0 all-gather.2.cloned.1.call-done.st_hbm
  82.6 4.8 %shard_map.71 = bf16[32,2432]{1,0:T(8,128)(2,1)S(1)} custom-call(bf16[32,2048]{1,0:T(8,128)(2,1)S(1)} %get-tuple-element.4.c_ref, bf16[32,2048]{1,0:T(8,128)(2,1)S(1)} %collective-permute-done.2.l_ref, bf16[32,2048]{1,0:T(8,128)(2,1)S(1)} %collective-permute-done.3.r_ref, f32[8,3,32,256]{3,2,1,0:T(8,128)S(1)} %get-tuple-element.5.g_ref, ...), custom_call_target="tpu_custom_call" | custom-call | tf_op jit(solution)/shard_map/pallas_call | solution.py:418
  87.4 0.1 all_to_all.24
  87.4 11.5 %all_to_all.34 = bf16[16,2,2432]{2,1,0:T(2,128)(2,1)S(1)} all-to-all(bf16[16,2,2432]{2,1,0:T(2,128)(2,1)S(1)} %all_to_all.24), channel_id=1, replica_groups=mesh['cells'=32,'bands'=16] {'bands'}, dimensions={0} | all-to-all | bytes 311296 | tf_op jit(solution)/shard_map/all_to_all | solution.py:489
  98.9 0.1 all_to_all.26.got
  99.0 0.6 shard_map.72
  99.6 4.5 %all-to-all-start.2 = ((f32[32,1,128]{2,1,0:T(1,128)}), f32[32,1,128]{2,1,0:T(1,128)S(1)}, u32[]{:S(2)}, u32[]{:S(2)}) async-start(f32[32,1,128]{2,1,0:T(1,128)} %bitcast.5), calls=%async_computation.2 | async-start | bytes 32768 | tf_op jit(solution)/shard_map/all_to_all | solution.py:492
  104.1 0.7 slice.4
  104.8 10.3 %all-to-all-done.2 = f32[32,1,128]{2,1,0:T(1,128)S(1)} async-done(((f32[32,1,128]{2,1,0:T(1,128)}), f32[32,1,128]{2,1,0:T(1,128)S(1)}, u32[]{:S(2)}, u32[]{:S(2)}) %all-to-all-start.2) | async-done | bytes 16416 | tf_op jit(solution)/shard_map/all_to_all | solution.py:492
  115.1 0.6 shard_map.73
Async XLA Ops:
  7.2 58.2 %copy-start = (bf16[2320,256]{1,0:T(8,128)(2,1)S(1)}, bf16[2320,256]{1,0:T(8,128)(2,1)}, u32[]{:S(2)}) copy-start(bf16[2320,256]{1,0:T(8,128)(2,1)} %constant.2.clone.w_hbm) | copy-start | bytes 3563524
  7.2 75.4 %all-gather.2.cloned.1.call-start = ((), (), s32[]{:S(2)}) async-start(), calls=%async_computation.3 | async-start | bytes 4456448 | tf_op jit(solution)/shard_map/all_gather | solution.py:442
  10.7 17.2 %collective-permute-start.1 = (bf16[32,2304]{1,0:T(8,128)(2,1)}, bf16[32,2304]{1,0:T(8,128)(2,1)S(1)}, u32[]{:S(2)}, u32[]{:S(2)}) collective-permute-start(bf16[32,2304]{1,0:T(8,128)(2,1)} %shard_map.68.c_ref), channel_id=1, source_target_pairs={{16,0},{32,16},{48,32},{64,48},{80,64},{96,80},{112,96},{128,112},... | collective-permute-start | bytes 442376 | tf_op jit(solution)/shard_map/ppermute | solution.py:432
  25.1 12.5 %collective-permute-start = (bf16[32,2304]{1,0:T(8,128)(2,1)}, bf16[32,2304]{1,0:T(8,128)(2,1)S(1)}, u32[]{:S(2)}, u32[]{:S(2)}) collective-permute-start(bf16[32,2304]{1,0:T(8,128)(2,1)} %shard_map.68.c_ref), channel_id=1, source_target_pairs={{496,0},{0,16},{16,32},{32,48},{48,64},{64,80},{80,96},{96,112},{1... | collective-permute-start | bytes 442376 | tf_op jit(solution)/shard_map/ppermute | solution.py:432
  37.6 0.9 copy-start.1
  68.9 10.3 %collective-permute-start.3 = (bf16[32,2048]{1,0:T(8,128)(2,1)S(1)}, bf16[32,2048]{1,0:T(8,128)(2,1)S(1)}, u32[]{:S(2)}, u32[]{:S(2)}) collective-permute-start(bf16[32,2048]{1,0:T(8,128)(2,1)S(1)} %get-tuple-element.4.c_ref), channel_id=1, source_target_pairs={{16,0},{32,16},{48,32},{64,48},{80,64},{96,80},{112,96},{128,112},... | collective-permute-start | bytes 393224 | tf_op jit(solution)/shard_map/ppermute | solution.py:432
  71.2 11.3 %collective-permute-start.2 = (bf16[32,2048]{1,0:T(8,128)(2,1)S(1)}, bf16[32,2048]{1,0:T(8,128)(2,1)S(1)}, u32[]{:S(2)}, u32[]{:S(2)}) collective-permute-start(bf16[32,2048]{1,0:T(8,128)(2,1)S(1)} %get-tuple-element.4.c_ref), channel_id=1, source_target_pairs={{496,0},{0,16},{16,32},{32,48},{48,64},{64,80},{80,96},{96,112},{1... | collective-permute-start | bytes 393224 | tf_op jit(solution)/shard_map/ppermute | solution.py:432
  99.6 15.5 %all-to-all-start.2 = ((f32[32,1,128]{2,1,0:T(1,128)}), f32[32,1,128]{2,1,0:T(1,128)S(1)}, u32[]{:S(2)}, u32[]{:S(2)}) async-start(f32[32,1,128]{2,1,0:T(1,128)} %bitcast.5), calls=%async_computation.2 | async-start | bytes 32768 | tf_op jit(solution)/shard_map/all_to_all | solution.py:492
Sparse Core Ops, SparseCore 0:
  10.2 57.1 all-gather.1

commit v4 on v3

--- a/solution.py
+++ b/solution.py
@@ -352,51 +352,32 @@
     filter_step(slabs, w_ref, g_ref, out_ref, cur, prev, acc, half, copy.wait)
 
 
-def later_kernel(
-    half, factor, c_ref, l_ref, r_ref, g_ref, w_hbm, st_hbm, out_ref, cur, prev, acc, w_ref, st_ref, sem, st_sem
-):
+def later_kernel(half, c_ref, l_ref, r_ref, g_ref, st_ref, w_hbm, out_ref, cur, prev, acc, w_ref, sem):
     copy = pltpu.make_async_copy(w_hbm, w_ref, sem)
     copy.start()
-    st_copy = pltpu.make_async_copy(st_hbm, st_ref, st_sem)
-    st_copy.start()
+    out_ref[:, NODES_DEV:] = st_ref[...]
     filter_step((l_ref, c_ref, r_ref), w_ref, g_ref, out_ref, cur, prev, acc, half, copy.wait)
-    st_copy.wait()
-    filtered = out_ref[:, :NODES_DEV]
-    shape = (NWF, 256)
-    lane, row = iota(shape, 1), iota(shape, 0)
-    own = ((lane >> 2) & 15) == (row >> 1)
-    even = (iota((NWF, 128), 0) & 1) == 0
-    lane, row = iota((NWF, 128), 1), iota((NWF, 128), 0)
-    result = jnp.zeros((NWF, 128), jnp.float32)
-    for block in range(4):
-        product = lax.dot_general(
-            filtered,
-            st_ref[256 * block : 256 * (block + 1), :],
+
+
+def corr_kernel(factor, got, out_ref):
+    four = jnp.concatenate([got[:, :NODES_DEV]] * 4, axis=0)
+    parts = [
+        lax.dot_general(
+            got[:, NODES_DEV * (1 + part) : NODES_DEV * (2 + part)],
+            four,
             (((1,), (1,)), ((), ())),
             preferred_element_type=jnp.float32,
         )
-        product = jnp.where(own, product * factor, 0.0)
-        for side in range(2):
-            values = product[:, 128 * side : 128 * (side + 1)]
-            first = jnp.sum(jnp.where(even, values, 0.0), axis=0, keepdims=True)
-            second = jnp.sum(jnp.where(even, 0.0, values), axis=0, keepdims=True)
-            values = jnp.where(even, first, second)
-            for shift in (4, 8, 16, 32):
-                values = values + pltpu.roll(values, shift, 1)
-            here = (row >> 2) == 2 * block + side
-            here = here & ((lane >> 2) == 15 + 16 * ((row >> 1) & 1))
-            result = jnp.where(here, values, result)
-    for part in range(3):
-        rounded = result.astype(jnp.bfloat16)
-        out_ref[:, NODES_DEV + 128 * part : NODES_DEV + 128 * (part + 1)] = rounded
-        result = result - rounded.astype(jnp.float32)
+        for part in range(2)
+    ]
+    lane, row = iota((NWF, 128), 1), iota((NWF, 128), 0)
+    both = jnp.where(((lane >> 5) & 1) == 0, parts[0], parts[1])
+    out_ref[...] = jnp.where((lane >> 6) == (row & 1), both * factor, 0.0)
 
 
 def share_kernel(got, out_ref):
-    parts = [
-        got[:, NODES_DEV + 128 * part : NODES_DEV + 128 * (part + 1)].astype(jnp.float32) for part in range(3)
-    ]
-    out_ref[...] = parts[0] + (parts[1] + parts[2])
+    total = jnp.sum(got[...], axis=0, keepdims=True)
+    out_ref[...] = jnp.where((iota((NWF, 128), 1) & 31) == iota((NWF, 128), 0), total, 0.0)
 
 
 def total_kernel(got, out_ref):
@@ -404,7 +385,7 @@
     lane = iota((1, 128), 1)
     rows = jnp.zeros((1, 128), jnp.float32)
     for row in range(4):
-        mine = jnp.where((lane & 3) == row, total, 0.0)
+        mine = jnp.where((lane >> 5) == row // 2 + 2 * (row % 2), total, 0.0)
         rows = jnp.where(lane == row, jnp.sum(mine, axis=1, keepdims=True), rows)
     out_ref[...] = rows[:, :4]
 
@@ -438,8 +419,7 @@
     bf, f32 = jnp.bfloat16, jnp.float32
     shape = jax.ShapeDtypeStruct
     n_cells, n_bands = lax.axis_size("cells"), lax.axis_size("bands")
-    stored = stored_blocks.reshape(4, n_bands, NODES_DEV).transpose(1, 0, 2).reshape(4 * n_bands, NODES_DEV)
-    stored = lax.all_gather(stored, "bands", axis=0, tiled=True)
+    stored = stored_blocks.reshape(2, 2, n_bands, NODES_DEV).transpose(2, 1, 0, 3).reshape(NWF, 2 * NODES_DEV)
     dma = pltpu.SemaphoreType.DMA
     (message,) = call(
         message_kernel,
@@ -480,15 +460,17 @@
     right = passed_along(block, "cells", -1)
     factor = 1.0 / math.sqrt(NODES_DEV * n_cells * n_bands)
     (block,) = call(
-        functools.partial(later_kernel, half, factor),
-        (block, left, right, diag),
-        [shape((NWF, NODES_DEV + 3 * 128), bf)],
-        scratch + [pltpu.VMEM(stored.shape, bf), dma, dma],
-        (weights, stored),
+        functools.partial(later_kernel, half),
+        (block, left, right, diag, stored),
+        [shape((NWF, 3 * NODES_DEV), bf)],
+        scratch + [dma],
+        (weights,),
     )
     got = lax.all_to_all(block, "bands", 0, 0, tiled=True)
     filtered = got[:, :NODES_DEV]
-    (partial,) = call(share_kernel, (got,), [shape((NWF, 128), f32)])
+    (partial,) = call(functools.partial(corr_kernel, factor), (got,), [shape((NWF, 128), f32)])
+    partial = lax.all_to_all(partial, "bands", 0, 0, tiled=True)
+    (partial,) = call(share_kernel, (partial,), [shape((NWF, 128), f32)])
     partial = lax.all_to_all(partial, "cells", 0, 0, tiled=True)
     (total,) = call(total_kernel, (partial,), [shape((1, 4), f32)])
     return (filtered, total.T)

time: 123 us -> 113 us (0.919)
  between operations: 14.1 us -> 0.78 us
  blocking collectives: 36.3 us -> 43.3 us
  Pallas kernels: 12.8 us -> 11.3 us
    all_to_all x0 -> x1, blocking collectives: none -> 9.42 us  [shards(): partial = lax.all_to_all(partial, 'bands', 0, 0, tiled=True)]
    all_to_all x1, blocking collectives: 24.8 us -> 20.1 us  [shards(): got = lax.all_to_all(payload, 'bands', 0, 0, tiled=True)]
    all_to_all x1, blocking collectives: 11.5 us -> 13.8 us  [shards(): got = lax.all_to_all(block, 'bands', 0, 0, tiled=True)]
    reshape x1, local copies, waits for them, and re-layouts: 1.8 us -> 0.27 us  [shards(): stored_blocks.reshape(2, 2, n_bands, NODES_DEV).transpose(2, 1, 0, 3)]
    pallas_call x6 -> x7, Pallas kernels: 12.8 us -> 11.3 us  [call(): pl.pallas_call(kernel, grid=(1,), in_specs=[full(a.shape) for a in args]...]
  transfers between devices with their start and end apart: 6 -> 5, of which waited for: 5 -> 5; matrix products, arithmetic and copies ran while one was open for 1% -> 1% of each run, Pallas kernels for 6% -> 0%
where the time goes in v4:
time: 113 us; the launch traced here: 112 us
  blocking collectives  43.3 us (38%)
  waiting for transfers between devices  27.6 us (24%)
  starting transfers between devices  26.4 us (23%)
  Pallas kernels  11.3 us (10%)
  local copies, waits for them, and re-layouts  3.02 us (3%)
    ppermute x4, starting transfers between devices, passed_along(): return lax.ppermute(block, axis, route)  22.5 us
    all_to_all x1, blocking collectives, shards(): got = lax.all_to_all(payload, 'bands', 0, 0, tiled=True)  20.1 us
    ppermute x4, waiting for transfers between devices, passed_along(): return lax.ppermute(block, axis, route)  17.3 us
    all_to_all x1, blocking collectives, shards(): got = lax.all_to_all(block, 'bands', 0, 0, tiled=True)  13.8 us
    pallas_call x7, Pallas kernels, call(): pl.pallas_call(kernel, grid=(1,), in_specs=[full(a.shape) for a in args]...  11.3 us
    all_to_all x1, waiting for transfers between devices, shards(): partial = lax.all_to_all(partial, 'cells', 0, 0, tiled=True)  10.3 us
    all_to_all x1, blocking collectives, shards(): partial = lax.all_to_all(partial, 'bands', 0, 0, tiled=True)  9.42 us
    all_to_all x1, starting transfers between devices, shards(): partial = lax.all_to_all(partial, 'cells', 0, 0, tiled=True)  3.92 us
  transfers between devices with their start and end apart: 5, of which 5 were waited for; matrix products, arithmetic and copies ran while one was open for 1% of the time, Pallas kernels for 0%

profile of v4, /device:TPU:1, one launch (start us, length us, event | category | flops | bytes accessed | tf_op | source)
XLA Modules:
  0.0 112.4 jit_solution(1262380476818141049)
XLA Ops:
  0.6 1.6 %shard_map.68.c_ref = bf16[32,2304]{1,0:T(8,128)(2,1)} custom-call(bf16[32,2048]{1,0:T(8,128)(2,1)} %v_hbm.1, f32[32,125]{1,0:T(8,128)} %bitcast.23, s32[32,125]{1,0:T(8,128)} %bitcast.24), custom_call_target="tpu_custom_call" | custom-call | tf_op jit(solution)/shard_map/pallas_call | solution.py:399
  2.2 14.4 %collective-permute-start.1 = (bf16[32,2304]{1,0:T(8,128)(2,1)}, bf16[32,2304]{1,0:T(8,128)(2,1)S(1)}, u32[]{:S(2)}, u32[]{:S(2)}) collective-permute-start(bf16[32,2304]{1,0:T(8,128)(2,1)} %shard_map.68.c_ref), channel_id=1, source_target_pairs={{16,0},{32,16},{48,32},{64,48},{80,64},{96,80},{112,96},{128,112},... | collective-permute-start | bytes 442376 | tf_op jit(solution)/shard_map/ppermute | solution.py:413
  16.6 1.9 %collective-permute-start = (bf16[32,2304]{1,0:T(8,128)(2,1)}, bf16[32,2304]{1,0:T(8,128)(2,1)S(1)}, u32[]{:S(2)}, u32[]{:S(2)}) collective-permute-start(bf16[32,2304]{1,0:T(8,128)(2,1)} %shard_map.68.c_ref), channel_id=1, source_target_pairs={{496,0},{0,16},{16,32},{32,48},{48,64},{64,80},{80,96},{96,112},{1... | collective-permute-start | bytes 442376 | tf_op jit(solution)/shard_map/ppermute | solution.py:413
  18.6 0.9 collective-permute-done.1.r_ref
  19.5 9.7 %collective-permute-done.l_ref = bf16[32,2304]{1,0:T(8,128)(2,1)S(1)} collective-permute-done((bf16[32,2304]{1,0:T(8,128)(2,1)}, bf16[32,2304]{1,0:T(8,128)(2,1)S(1)}, u32[]{:S(2)}, u32[]{:S(2)}) %collective-permute-start) | collective-permute-done | bytes 147488 | tf_op jit(solution)/shard_map/ppermute | solution.py:413
  29.1 0.9 copy-done.1
  30.0 1.5 %shard_map.69 = bf16[32,10496]{1,0:T(8,128)(2,1)S(1)} custom-call(bf16[32,2304]{1,0:T(8,128)(2,1)S(1)} %copy-done.1, bf16[32,2304]{1,0:T(8,128)(2,1)S(1)} %collective-permute-done.l_ref, bf16[32,2304]{1,0:T(8,128)(2,1)S(1)} %collective-permute-done.1.r_ref), custom_call_target="tpu_custom_call" | custom-call | tf_op jit(solution)/shard_map/pallas_call | solution.py:399
  31.6 0.3 all_to_all.28
  31.8 0.0 copy-start
  31.8 20.1 %all_to_all.44 = bf16[16,2,10496]{2,1,0:T(2,128)(2,1)S(1)} all-to-all(bf16[16,2,10496]{2,1,0:T(2,128)(2,1)S(1)} %all_to_all.28), channel_id=1, replica_groups=mesh['cells'=32,'bands'=16] {'bands'}, dimensions={0} | all-to-all | bytes 1343488 | tf_op jit(solution)/shard_map/all_to_all | solution.py:445
  52.0 0.3 all_to_all.30.got
  52.2 0.0 copy-start.2
  52.2 3.5 %shard_map.70 = (bf16[32,2048]{1,0:T(8,128)(2,1)S(1)}, f32[8,3,32,256]{3,2,1,0:T(8,128)S(1)}) custom-call(bf16[32,10496]{1,0:T(8,128)(2,1)S(1)} %all_to_all.30.got, bf16[2320,256]{1,0:T(8,128)(2,1)S(1)} %copy-done), custom_call_target="tpu_custom_call" | custom-call | tf_op jit(solution)/shard_map/pallas_call | solution.py:399
  55.7 1.9 %collective-permute-start.3 = (bf16[32,2048]{1,0:T(8,128)(2,1)S(1)}, bf16[32,2048]{1,0:T(8,128)(2,1)S(1)}, u32[]{:S(2)}, u32[]{:S(2)}) collective-permute-start(bf16[32,2048]{1,0:T(8,128)(2,1)S(1)} %get-tuple-element.4.c_ref), channel_id=1, source_target_pairs={{16,0},{32,16},{48,32},{64,48},{80,64},{96,80},{112,96},{128,112},... | collective-permute-start | bytes 393224 | tf_op jit(solution)/shard_map/ppermute | solution.py:413
  57.7 4.3 %collective-permute-start.2 = (bf16[32,2048]{1,0:T(8,128)(2,1)S(1)}, bf16[32,2048]{1,0:T(8,128)(2,1)S(1)}, u32[]{:S(2)}, u32[]{:S(2)}) collective-permute-start(bf16[32,2048]{1,0:T(8,128)(2,1)S(1)} %get-tuple-element.4.c_ref), channel_id=1, source_target_pairs={{496,0},{0,16},{16,32},{32,48},{48,64},{64,80},{80,96},{96,112},{1... | collective-permute-start | bytes 393224 | tf_op jit(solution)/shard_map/ppermute | solution.py:413
  61.9 0.0 copy-done.2
  61.9 0.2 copy.10
  62.1 0.3 copy.8
  62.4 0.1 copy.11
  62.5 3.5 %collective-permute-done.3.r_ref = bf16[32,2048]{1,0:T(8,128)(2,1)S(1)} collective-permute-done((bf16[32,2048]{1,0:T(8,128)(2,1)S(1)}, bf16[32,2048]{1,0:T(8,128)(2,1)S(1)}, u32[]{:S(2)}, u32[]{:S(2)}) %collective-permute-start.3) | collective-permute-done | bytes 131104 | tf_op jit(solution)/shard_map/ppermute | solution.py:413
  66.0 3.2 %collective-permute-done.2.l_ref = bf16[32,2048]{1,0:T(8,128)(2,1)S(1)} collective-permute-done((bf16[32,2048]{1,0:T(8,128)(2,1)S(1)}, bf16[32,2048]{1,0:T(8,128)(2,1)S(1)}, u32[]{:S(2)}, u32[]{:S(2)}) %collective-permute-start.2) | collective-permute-done | bytes 131104 | tf_op jit(solution)/shard_map/ppermute | solution.py:413
  69.2 3.1 %shard_map.71 = bf16[32,6144]{1,0:T(8,128)(2,1)S(1)} custom-call(bf16[32,2048]{1,0:T(8,128)(2,1)S(1)} %get-tuple-element.4.c_ref, bf16[32,2048]{1,0:T(8,128)(2,1)S(1)} %collective-permute-done.2.l_ref, bf16[32,2048]{1,0:T(8,128)(2,1)S(1)} %collective-permute-done.3.r_ref, f32[8,3,32,256]{3,2,1,0:T(8,128)S(1)} %get-tuple-element.5.g_ref, ...), custom_call_target="tpu_custom_call" | custom-call | tf_op jit(solution)/shard_map/pallas_call | solution.py:399
  72.3 0.3 all_to_all.31
  72.5 13.8 %all_to_all.45 = bf16[16,2,6144]{2,1,0:T(2,128)(2,1)S(1)} all-to-all(bf16[16,2,6144]{2,1,0:T(2,128)(2,1)S(1)} %all_to_all.31), channel_id=1, replica_groups=mesh['cells'=32,'bands'=16] {'bands'}, dimensions={0} | all-to-all | bytes 786432 | tf_op jit(solution)/shard_map/all_to_all | solution.py:469
  86.3 0.1 all_to_all.33.got
  86.4 0.4 shard_map.72
  86.8 9.4 %all_to_all.46 = f32[16,2,128]{2,1,0:T(2,128)S(1)} all-to-all(f32[16,2,128]{2,1,0:T(2,128)S(1)} %bitcast.17), channel_id=1, replica_groups=mesh['cells'=32,'bands'=16] {'bands'}, dimensions={0} | all-to-all | bytes 32768 | tf_op jit(solution)/shard_map/all_to_all | solution.py:472
  96.3 0.6 shard_map.73
  96.9 3.9 %all-to-all-start.3 = ((f32[32,1,128]{2,1,0:T(1,128)}), f32[32,1,128]{2,1,0:T(1,128)S(1)}, u32[]{:S(2)}, u32[]{:S(2)}) async-start(f32[32,1,128]{2,1,0:T(1,128)} %bitcast.6), calls=%async_computation.3 | async-start | bytes 32768 | tf_op jit(solution)/shard_map/all_to_all | solution.py:474
  100.8 0.7 slice.4
  101.5 10.3 %all-to-all-done.3 = f32[32,1,128]{2,1,0:T(1,128)S(1)} async-done(((f32[32,1,128]{2,1,0:T(1,128)}), f32[32,1,128]{2,1,0:T(1,128)S(1)}, u32[]{:S(2)}, u32[]{:S(2)}) %all-to-all-start.3) | async-done | bytes 16416 | tf_op jit(solution)/shard_map/all_to_all | solution.py:474
  111.8 0.6 shard_map.74
  (2 shorter events, 0.0 us)
Async XLA Ops:
  2.2 17.2 %collective-permute-start.1 = (bf16[32,2304]{1,0:T(8,128)(2,1)}, bf16[32,2304]{1,0:T(8,128)(2,1)S(1)}, u32[]{:S(2)}, u32[]{:S(2)}) collective-permute-start(bf16[32,2304]{1,0:T(8,128)(2,1)} %shard_map.68.c_ref), channel_id=1, source_target_pairs={{16,0},{32,16},{48,32},{64,48},{80,64},{96,80},{112,96},{128,112},... | collective-permute-start | bytes 442376 | tf_op jit(solution)/shard_map/ppermute | solution.py:413
  16.6 12.5 %collective-permute-start = (bf16[32,2304]{1,0:T(8,128)(2,1)}, bf16[32,2304]{1,0:T(8,128)(2,1)S(1)}, u32[]{:S(2)}, u32[]{:S(2)}) collective-permute-start(bf16[32,2304]{1,0:T(8,128)(2,1)} %shard_map.68.c_ref), channel_id=1, source_target_pairs={{496,0},{0,16},{16,32},{32,48},{48,64},{64,80},{80,96},{96,112},{1... | collective-permute-start | bytes 442376 | tf_op jit(solution)/shard_map/ppermute | solution.py:413
  29.1 0.9 copy-start.1
  31.8 20.4 %copy-start = (bf16[2320,256]{1,0:T(8,128)(2,1)S(1)}, bf16[2320,256]{1,0:T(8,128)(2,1)}, u32[]{:S(2)}) copy-start(bf16[2320,256]{1,0:T(8,128)(2,1)} %constant.2.clone.w_hbm) | copy-start | bytes 3563524
  52.2 9.7 %copy-start.2 = (bf16[4,32768]{1,0:T(4,128)(2,1)S(1)}, bf16[4,32768]{1,0:T(4,128)(2,1)}, u32[]{:S(2)}) copy-start(bf16[4,32768]{1,0:T(4,128)(2,1)} %param.6) | copy-start | bytes 786436
  55.7 10.2 %collective-permute-start.3 = (bf16[32,2048]{1,0:T(8,128)(2,1)S(1)}, bf16[32,2048]{1,0:T(8,128)(2,1)S(1)}, u32[]{:S(2)}, u32[]{:S(2)}) collective-permute-start(bf16[32,2048]{1,0:T(8,128)(2,1)S(1)} %get-tuple-element.4.c_ref), channel_id=1, source_target_pairs={{16,0},{32,16},{48,32},{64,48},{80,64},{96,80},{112,96},{128,112},... | collective-permute-start | bytes 393224 | tf_op jit(solution)/shard_map/ppermute | solution.py:413
  57.7 11.5 %collective-permute-start.2 = (bf16[32,2048]{1,0:T(8,128)(2,1)S(1)}, bf16[32,2048]{1,0:T(8,128)(2,1)S(1)}, u32[]{:S(2)}, u32[]{:S(2)}) collective-permute-start(bf16[32,2048]{1,0:T(8,128)(2,1)S(1)} %get-tuple-element.4.c_ref), channel_id=1, source_target_pairs={{496,0},{0,16},{16,32},{32,48},{48,64},{64,80},{80,96},{96,112},{1... | collective-permute-start | bytes 393224 | tf_op jit(solution)/shard_map/ppermute | solution.py:413
  96.9 14.9 %all-to-all-start.3 = ((f32[32,1,128]{2,1,0:T(1,128)}), f32[32,1,128]{2,1,0:T(1,128)S(1)}, u32[]{:S(2)}, u32[]{:S(2)}) async-start(f32[32,1,128]{2,1,0:T(1,128)} %bitcast.6), calls=%async_computation.3 | async-start | bytes 32768 | tf_op jit(solution)/shard_map/all_to_all | solution.py:474

commit v5 on v4

--- a/solution.py
+++ b/solution.py
@@ -178,19 +178,24 @@
     return jnp.where(good, 16 * i + 4 * j + l, -1).astype(jnp.float32)
 
 
-def nodal(own, left, mask):
-    sides = [(own, range(4))] + ([(left, range(4, 6))] if left is not None else [])
+def fitting():
+    a, b, c = local_node(iota((128, LANES_V), 0))
+    lane = iota((128, LANES_V), 1)
+    fits = ((b & 3) == ((lane >> 4) & 3)) & ((c & 3) == (lane & 3)) & (lane < PLANE + 16)
+    return jnp.where(fits, 1.0, 0.0)
+
+
+def nodal(message, kind_range, mask):
     rows, ones = [], ([], [])
-    for message, kind_range in sides:
-        high = message[:, NODES_DEV : NODES_DEV + 128].astype(jnp.float32)
-        low = message[:, NODES_DEV + 128 :].astype(jnp.float32)
-        cell = high[:, 127:128]
-        for kind in kind_range:
-            pick = pick_kind(kind)
-            rows += [high * pick, low * pick]
-            for i in range(2):
-                one = jnp.where(cell == place_of(i, kind), 1.0, 0.0)
-                ones[i].extend([one, one])
+    high = message[:, NODES_DEV : NODES_DEV + 128].astype(jnp.float32)
+    low = message[:, NODES_DEV + 128 :].astype(jnp.float32)
+    cell = high[:, 127:128]
+    for kind in kind_range:
+        pick = pick_kind(kind)
+        rows += [high * pick, low * pick]
+        for i in range(2):
+            one = jnp.where(cell == place_of(i, kind), 1.0, 0.0)
+            ones[i].extend([one, one])
     stack = jnp.concatenate(rows, axis=0).astype(jnp.bfloat16)
     total = jnp.zeros((8, LANES_V), jnp.float32)
     k = iota((8, 128), 1)
@@ -210,19 +215,24 @@
     return total
 
 
-def pack_kernel(c_ref, l_ref, r_ref, out_ref, ghost):
-    messages = (l_ref, c_ref, r_ref)
+def own_kernel(c_ref, v_ref, own_ref, edge_ref, mask_ref):
+    v_ref[...] = c_ref[:, :NODES_DEV]
+    mask = fitting()
+    mask_ref[...] = mask
+    own_ref[...] = nodal(c_ref, range(4), mask)
+    edge_ref[...] = nodal(c_ref, range(4, 6), mask)
+
+
+def pack_kernel(l_ref, r_ref, c_ref, own_ref, edge_ref, mask_ref, out_ref, ghost):
     even = iota((32, PLANE), 0) % 2 == 0
-    a, b, c = local_node(iota((128, LANES_V), 0))
-    lane = iota((128, LANES_V), 1)
-    fits = ((b & 3) == ((lane >> 4) & 3)) & ((c & 3) == (lane & 3)) & (lane < PLANE + 16)
-    mask = jnp.where(fits, 1.0, 0.0)
-    totals = []
-    for s, message in enumerate(messages):
+    mask = mask_ref[...]
+    for s, message in enumerate((l_ref, c_ref, r_ref)):
         out_ref[:, NODES_DEV * s : NODES_DEV * (s + 1)] = message[:, :NODES_DEV]
-        totals.append(nodal(message, messages[s - 1] if s else None, mask))
-    high = totals[1].astype(jnp.bfloat16).astype(jnp.float32)
-    for part, (first, second) in enumerate(((high, totals[1] - high), (totals[0], totals[2]))):
+    own = own_ref[...] + nodal(l_ref, range(4, 6), mask)
+    left = nodal(l_ref, range(4), mask)
+    right = nodal(r_ref, range(4), mask) + edge_ref[...]
+    high = own.astype(jnp.bfloat16).astype(jnp.float32)
+    for part, (first, second) in enumerate(((high, own - high), (left, right))):
         for x in range(NXL):
             main = jnp.where(even, first[x : x + 1, :PLANE], second[x : x + 1, :PLANE])
             at = V_AT + NODES_DEV * part + PLANE * x
@@ -436,9 +446,11 @@
     )
     left = passed_along(message, "cells", 1)
     right = passed_along(message, "cells", -1)
+    shapes = [shape((8, LANES_V), f32), shape((8, LANES_V), f32), shape((128, LANES_V), f32)]
+    own = call(own_kernel, (message,), [shape((NWF, NODES_DEV), bf)] + shapes)
     (payload,) = call(
         pack_kernel,
-        (message, left, right),
+        (left, right, *own),
         [shape((NWF, PAYLOAD), bf)],
         [pltpu.VMEM((32, 128), f32)],
     )

time: 113 us -> 111 us (0.982)
  waiting for transfers between devices: 27.6 us -> 16.8 us
  starting transfers between devices: 26.4 us -> 36.9 us
  blocking collectives: 43.3 us -> 40.5 us
    ppermute x4, waiting for transfers between devices: 17.3 us -> 6.62 us  [passed_along(): return lax.ppermute(block, axis, route)]
    all_to_all x1, starting transfers between devices: 3.92 us -> 9.84 us  [shards(): partial = lax.all_to_all(partial, 'cells', 0, 0, tiled=True)]
    ppermute x4, starting transfers between devices: 22.5 us -> 27.1 us  [passed_along(): return lax.ppermute(block, axis, route)]
    all_to_all x1, blocking collectives: 13.8 us -> 12.2 us  [shards(): got = lax.all_to_all(block, 'bands', 0, 0, tiled=True)]
    all_to_all x1, blocking collectives: 20.1 us -> 18.9 us  [shards(): got = lax.all_to_all(payload, 'bands', 0, 0, tiled=True)]
    pallas_call x7 -> x8, Pallas kernels: 11.3 us -> 12.4 us  [call(): pl.pallas_call(kernel, grid=(1,), in_specs=[full(a.shape) for a in args]...]
  transfers between devices with their start and end apart: 5 -> 5, of which waited for: 5 -> 4; matrix products, arithmetic and copies ran while one was open for 1% -> 1% of each run, Pallas kernels for 0% -> 1%
where the time goes in v5:
time: 111 us; the launch traced here: 110 us
  blocking collectives  40.5 us (36%)
  starting transfers between devices  36.9 us (33%)
  waiting for transfers between devices  16.8 us (15%)
  Pallas kernels  12.4 us (11%)
  local copies, waits for them, and re-layouts  3.01 us (3%)
    ppermute x4, starting transfers between devices, passed_along(): return lax.ppermute(block, axis, route)  27.1 us
    all_to_all x1, blocking collectives, shards(): got = lax.all_to_all(payload, 'bands', 0, 0, tiled=True)  18.9 us
    pallas_call x8, Pallas kernels, call(): pl.pallas_call(kernel, grid=(1,), in_specs=[full(a.shape) for a in args]...  12.4 us
    all_to_all x1, blocking collectives, shards(): got = lax.all_to_all(block, 'bands', 0, 0, tiled=True)  12.2 us
    all_to_all x1, waiting for transfers between devices, shards(): partial = lax.all_to_all(partial, 'cells', 0, 0, tiled=True)  10.2 us
    all_to_all x1, starting transfers between devices, shards(): partial = lax.all_to_all(partial, 'cells', 0, 0, tiled=True)  9.84 us
    all_to_all x1, blocking collectives, shards(): partial = lax.all_to_all(partial, 'bands', 0, 0, tiled=True)  9.42 us
    ppermute x4, waiting for transfers between devices, passed_along(): return lax.ppermute(block, axis, route)  6.62 us
  transfers between devices with their start and end apart: 5, of which 4 were waited for; matrix products, arithmetic and copies ran while one was open for 1% of the time, Pallas kernels for 1%

profile of v5, /device:TPU:1, one launch (start us, length us, event | category | flops | bytes accessed | tf_op | source)
XLA Modules:
  0.0 110.4 jit_solution(5061740027266375260)
XLA Ops:
  0.6 1.6 %shard_map.68.c_ref = bf16[32,2304]{1,0:T(8,128)(2,1)} custom-call(bf16[32,2048]{1,0:T(8,128)(2,1)} %v_hbm.1, f32[32,125]{1,0:T(8,128)} %bitcast.23, s32[32,125]{1,0:T(8,128)} %bitcast.24), custom_call_target="tpu_custom_call" | custom-call | tf_op jit(solution)/shard_map/pallas_call | solution.py:409
  2.3 6.6 %collective-permute-start = (bf16[32,2304]{1,0:T(8,128)(2,1)}, bf16[32,2304]{1,0:T(8,128)(2,1)S(1)}, u32[]{:S(2)}, u32[]{:S(2)}) collective-permute-start(bf16[32,2304]{1,0:T(8,128)(2,1)} %shard_map.68.c_ref), channel_id=1, source_target_pairs={{496,0},{0,16},{16,32},{32,48},{48,64},{64,80},{80,96},{96,112},{1... | collective-permute-start | bytes 442376 | tf_op jit(solution)/shard_map/ppermute | solution.py:423
  8.9 9.7 %collective-permute-start.1 = (bf16[32,2304]{1,0:T(8,128)(2,1)}, bf16[32,2304]{1,0:T(8,128)(2,1)S(1)}, u32[]{:S(2)}, u32[]{:S(2)}) collective-permute-start(bf16[32,2304]{1,0:T(8,128)(2,1)} %shard_map.68.c_ref), channel_id=1, source_target_pairs={{16,0},{32,16},{48,32},{64,48},{80,64},{96,80},{112,96},{128,112},... | collective-permute-start | bytes 442376 | tf_op jit(solution)/shard_map/ppermute | solution.py:423
  18.6 0.9 copy-done.1
  19.5 0.9 shard_map.69
  20.4 2.3 %collective-permute-done.l_ref = bf16[32,2304]{1,0:T(8,128)(2,1)S(1)} collective-permute-done((bf16[32,2304]{1,0:T(8,128)(2,1)}, bf16[32,2304]{1,0:T(8,128)(2,1)S(1)}, u32[]{:S(2)}, u32[]{:S(2)}) %collective-permute-start) | collective-permute-done | bytes 147488 | tf_op jit(solution)/shard_map/ppermute | solution.py:423
  22.8 0.0 collective-permute-done.1.r_ref
  22.8 1.5 %shard_map.70 = bf16[32,10496]{1,0:T(8,128)(2,1)S(1)} custom-call(bf16[32,2304]{1,0:T(8,128)(2,1)S(1)} %collective-permute-done.l_ref, bf16[32,2304]{1,0:T(8,128)(2,1)S(1)} %collective-permute-done.1.r_ref, bf16[32,2048]{1,0:T(8,128)(2,1)S(1)} %get-tuple-element.8.c_ref, f32[8,384]{1,0:T(8,128)S(1)} %get-tuple-element.9.own_ref, ...), custom_call_target="tpu_custom_call" | custom-call | tf_op jit(solution)/shard_map/pallas_call | solution.py:409
  24.2 0.3 all_to_all.28
  24.5 0.0 copy-start
  24.5 18.9 %all_to_all.44 = bf16[16,2,10496]{2,1,0:T(2,128)(2,1)S(1)} all-to-all(bf16[16,2,10496]{2,1,0:T(2,128)(2,1)S(1)} %all_to_all.28), channel_id=1, replica_groups=mesh['cells'=32,'bands'=16] {'bands'}, dimensions={0} | all-to-all | bytes 1343488 | tf_op jit(solution)/shard_map/all_to_all | solution.py:457
  43.4 0.3 all_to_all.30.got
  43.6 0.0 copy-start.2
  43.7 3.6 %shard_map.71 = (bf16[32,2048]{1,0:T(8,128)(2,1)S(1)}, f32[8,3,32,256]{3,2,1,0:T(8,128)S(1)}) custom-call(bf16[32,10496]{1,0:T(8,128)(2,1)S(1)} %all_to_all.30.got, bf16[2320,256]{1,0:T(8,128)(2,1)S(1)} %copy-done), custom_call_target="tpu_custom_call" | custom-call | tf_op jit(solution)/shard_map/pallas_call | solution.py:409
  47.3 4.7 %collective-permute-start.2 = (bf16[32,2048]{1,0:T(8,128)(2,1)S(1)}, bf16[32,2048]{1,0:T(8,128)(2,1)S(1)}, u32[]{:S(2)}, u32[]{:S(2)}) collective-permute-start(bf16[32,2048]{1,0:T(8,128)(2,1)S(1)} %get-tuple-element.12.c_ref), channel_id=1, source_target_pairs={{496,0},{0,16},{16,32},{32,48},{48,64},{64,80},{80,96},{96,112},{1... | collective-permute-start | bytes 393224 | tf_op jit(solution)/shard_map/ppermute | solution.py:423
  52.0 6.1 %collective-permute-start.3 = (bf16[32,2048]{1,0:T(8,128)(2,1)S(1)}, bf16[32,2048]{1,0:T(8,128)(2,1)S(1)}, u32[]{:S(2)}, u32[]{:S(2)}) collective-permute-start(bf16[32,2048]{1,0:T(8,128)(2,1)S(1)} %get-tuple-element.12.c_ref), channel_id=1, source_target_pairs={{16,0},{32,16},{48,32},{64,48},{80,64},{96,80},{112,96},{128,112},... | collective-permute-start | bytes 393224 | tf_op jit(solution)/shard_map/ppermute | solution.py:423
  58.1 0.2 copy.10
  58.2 0.3 copy.8
  58.5 0.1 copy.11
  58.6 2.8 %collective-permute-done.2.l_ref = bf16[32,2048]{1,0:T(8,128)(2,1)S(1)} collective-permute-done((bf16[32,2048]{1,0:T(8,128)(2,1)S(1)}, bf16[32,2048]{1,0:T(8,128)(2,1)S(1)}, u32[]{:S(2)}, u32[]{:S(2)}) %collective-permute-start.2) | collective-permute-done | bytes 131104 | tf_op jit(solution)/shard_map/ppermute | solution.py:423
  61.3 1.5 %collective-permute-done.3.r_ref = bf16[32,2048]{1,0:T(8,128)(2,1)S(1)} collective-permute-done((bf16[32,2048]{1,0:T(8,128)(2,1)S(1)}, bf16[32,2048]{1,0:T(8,128)(2,1)S(1)}, u32[]{:S(2)}, u32[]{:S(2)}) %collective-permute-start.3) | collective-permute-done | bytes 131104 | tf_op jit(solution)/shard_map/ppermute | solution.py:423
  62.9 3.2 %shard_map.72 = bf16[32,6144]{1,0:T(8,128)(2,1)S(1)} custom-call(bf16[32,2048]{1,0:T(8,128)(2,1)S(1)} %get-tuple-element.12.c_ref, bf16[32,2048]{1,0:T(8,128)(2,1)S(1)} %collective-permute-done.2.l_ref, bf16[32,2048]{1,0:T(8,128)(2,1)S(1)} %collective-permute-done.3.r_ref, f32[8,3,32,256]{3,2,1,0:T(8,128)S(1)} %get-tuple-element.13.g_ref, ...), custom_call_target="tpu_custom_call" | custom-call | tf_op jit(solution)/shard_map/pallas_call | solution.py:409
  66.0 0.3 all_to_all.31
  66.3 12.2 %all_to_all.45 = bf16[16,2,6144]{2,1,0:T(2,128)(2,1)S(1)} all-to-all(bf16[16,2,6144]{2,1,0:T(2,128)(2,1)S(1)} %all_to_all.31), channel_id=1, replica_groups=mesh['cells'=32,'bands'=16] {'bands'}, dimensions={0} | all-to-all | bytes 786432 | tf_op jit(solution)/shard_map/all_to_all | solution.py:481
  78.5 0.1 all_to_all.33.got
  78.6 0.4 shard_map.73
  79.0 9.4 %all_to_all.46 = f32[16,2,128]{2,1,0:T(2,128)S(1)} all-to-all(f32[16,2,128]{2,1,0:T(2,128)S(1)} %bitcast.17), channel_id=1, replica_groups=mesh['cells'=32,'bands'=16] {'bands'}, dimensions={0} | all-to-all | bytes 32768 | tf_op jit(solution)/shard_map/all_to_all | solution.py:484
  88.5 0.6 shard_map.74
  89.1 9.8 %all-to-all-start.3 = ((f32[32,1,128]{2,1,0:T(1,128)}), f32[32,1,128]{2,1,0:T(1,128)S(1)}, u32[]{:S(2)}, u32[]{:S(2)}) async-start(f32[32,1,128]{2,1,0:T(1,128)} %bitcast.6), calls=%async_computation.3 | async-start | bytes 32768 | tf_op jit(solution)/shard_map/all_to_all | solution.py:486
  98.9 0.7 slice.4
  99.6 10.2 %all-to-all-done.3 = f32[32,1,128]{2,1,0:T(1,128)S(1)} async-done(((f32[32,1,128]{2,1,0:T(1,128)}), f32[32,1,128]{2,1,0:T(1,128)S(1)}, u32[]{:S(2)}, u32[]{:S(2)}) %all-to-all-start.3) | async-done | bytes 16416 | tf_op jit(solution)/shard_map/all_to_all | solution.py:486
  109.8 0.6 shard_map.75
  (3 shorter events, 0.0 us)
Async XLA Ops:
  2.3 20.5 %collective-permute-start = (bf16[32,2304]{1,0:T(8,128)(2,1)}, bf16[32,2304]{1,0:T(8,128)(2,1)S(1)}, u32[]{:S(2)}, u32[]{:S(2)}) collective-permute-start(bf16[32,2304]{1,0:T(8,128)(2,1)} %shard_map.68.c_ref), channel_id=1, source_target_pairs={{496,0},{0,16},{16,32},{32,48},{48,64},{64,80},{80,96},{96,112},{1... | collective-permute-start | bytes 442376 | tf_op jit(solution)/shard_map/ppermute | solution.py:423
  8.9 13.9 %collective-permute-start.1 = (bf16[32,2304]{1,0:T(8,128)(2,1)}, bf16[32,2304]{1,0:T(8,128)(2,1)S(1)}, u32[]{:S(2)}, u32[]{:S(2)}) collective-permute-start(bf16[32,2304]{1,0:T(8,128)(2,1)} %shard_map.68.c_ref), channel_id=1, source_target_pairs={{16,0},{32,16},{48,32},{64,48},{80,64},{96,80},{112,96},{128,112},... | collective-permute-start | bytes 442376 | tf_op jit(solution)/shard_map/ppermute | solution.py:423
  18.6 0.9 copy-start.1
  24.5 19.1 %copy-start = (bf16[2320,256]{1,0:T(8,128)(2,1)S(1)}, bf16[2320,256]{1,0:T(8,128)(2,1)}, u32[]{:S(2)}) copy-start(bf16[2320,256]{1,0:T(8,128)(2,1)} %constant.2.clone.w_hbm) | copy-start | bytes 3563524
  43.6 14.4 %copy-start.2 = (bf16[4,32768]{1,0:T(4,128)(2,1)S(1)}, bf16[4,32768]{1,0:T(4,128)(2,1)}, u32[]{:S(2)}) copy-start(bf16[4,32768]{1,0:T(4,128)(2,1)} %param.6) | copy-start | bytes 786436
  47.3 14.1 %collective-permute-start.2 = (bf16[32,2048]{1,0:T(8,128)(2,1)S(1)}, bf16[32,2048]{1,0:T(8,128)(2,1)S(1)}, u32[]{:S(2)}, u32[]{:S(2)}) collective-permute-start(bf16[32,2048]{1,0:T(8,128)(2,1)S(1)} %get-tuple-element.12.c_ref), channel_id=1, source_target_pairs={{496,0},{0,16},{16,32},{32,48},{48,64},{64,80},{80,96},{96,112},{1... | collective-permute-start | bytes 393224 | tf_op jit(solution)/shard_map/ppermute | solution.py:423
  52.0 10.9 %collective-permute-start.3 = (bf16[32,2048]{1,0:T(8,128)(2,1)S(1)}, bf16[32,2048]{1,0:T(8,128)(2,1)S(1)}, u32[]{:S(2)}, u32[]{:S(2)}) collective-permute-start(bf16[32,2048]{1,0:T(8,128)(2,1)S(1)} %get-tuple-element.12.c_ref), channel_id=1, source_target_pairs={{16,0},{32,16},{48,32},{64,48},{80,64},{96,80},{112,96},{128,112},... | collective-permute-start | bytes 393224 | tf_op jit(solution)/shard_map/ppermute | solution.py:423
  89.1 20.7 %all-to-all-start.3 = ((f32[32,1,128]{2,1,0:T(1,128)}), f32[32,1,128]{2,1,0:T(1,128)S(1)}, u32[]{:S(2)}, u32[]{:S(2)}) async-start(f32[32,1,128]{2,1,0:T(1,128)} %bitcast.6), calls=%async_computation.3 | async-start | bytes 32768 | tf_op jit(solution)/shard_map/all_to_all | solution.py:486

commit v6 on v5

--- a/solution.py
+++ b/solution.py
@@ -185,33 +185,35 @@
     return jnp.where(fits, 1.0, 0.0)
 
 
-def nodal(message, kind_range, mask):
+def nodal(message, kind_range, mask, exact):
     rows, ones = [], ([], [])
-    high = message[:, NODES_DEV : NODES_DEV + 128].astype(jnp.float32)
-    low = message[:, NODES_DEV + 128 :].astype(jnp.float32)
-    cell = high[:, 127:128]
+    parts = [message[:, NODES_DEV : NODES_DEV + 128].astype(jnp.float32)]
+    cell = parts[0][:, 127:128]
+    if exact:
+        parts.append(message[:, NODES_DEV + 128 :].astype(jnp.float32))
     for kind in kind_range:
         pick = pick_kind(kind)
-        rows += [high * pick, low * pick]
+        rows += [part * pick for part in parts]
         for i in range(2):
             one = jnp.where(cell == place_of(i, kind), 1.0, 0.0)
-            ones[i].extend([one, one])
+            ones[i].extend([one] * len(parts))
     stack = jnp.concatenate(rows, axis=0).astype(jnp.bfloat16)
+    placed = jnp.concatenate([jnp.concatenate(one, axis=0) for one in ones], axis=1)
+    both = lax.dot_general(
+        stack, placed.astype(jnp.bfloat16), (((0,), (0,)), ((), ())), preferred_element_type=jnp.float32
+    )
     total = jnp.zeros((8, LANES_V), jnp.float32)
     k = iota((8, 128), 1)
     along = local_node(k)[0]
     for i in range(2):
-        placed = jnp.concatenate(ones[i], axis=0).astype(jnp.bfloat16)
-        values = lax.dot_general(
-            stack, placed, (((0,), (0,)), ((), ())), preferred_element_type=jnp.float32
-        )
-        values = values * mask
+        values = both[:, LANES_V * i : LANES_V * (i + 1)] * mask
         high = values.astype(jnp.bfloat16)
-        low = (values - high.astype(jnp.float32)).astype(jnp.bfloat16)
         to_x = jnp.where((((4 * i + along) & 7) == iota((8, 128), 0)) & (k < 125), 1.0, 0.0)
         to_x = to_x.astype(jnp.bfloat16)
         total += jnp.dot(to_x, high, preferred_element_type=jnp.float32)
-        total += jnp.dot(to_x, low, preferred_element_type=jnp.float32)
+        if exact:
+            low = (values - high.astype(jnp.float32)).astype(jnp.bfloat16)
+            total += jnp.dot(to_x, low, preferred_element_type=jnp.float32)
     return total
 
 
@@ -219,8 +221,8 @@
     v_ref[...] = c_ref[:, :NODES_DEV]
     mask = fitting()
     mask_ref[...] = mask
-    own_ref[...] = nodal(c_ref, range(4), mask)
-    edge_ref[...] = nodal(c_ref, range(4, 6), mask)
+    own_ref[...] = nodal(c_ref, range(4), mask, True)
+    edge_ref[...] = nodal(c_ref, range(4, 6), mask, True)
 
 
 def pack_kernel(l_ref, r_ref, c_ref, own_ref, edge_ref, mask_ref, out_ref, ghost):
@@ -228,9 +230,9 @@
     mask = mask_ref[...]
     for s, message in enumerate((l_ref, c_ref, r_ref)):
         out_ref[:, NODES_DEV * s : NODES_DEV * (s + 1)] = message[:, :NODES_DEV]
-    own = own_ref[...] + nodal(l_ref, range(4, 6), mask)
-    left = nodal(l_ref, range(4), mask)
-    right = nodal(r_ref, range(4), mask) + edge_ref[...]
+    own = own_ref[...] + nodal(l_ref, range(4, 6), mask, True)
+    left = nodal(l_ref, range(4), mask, False)
+    right = nodal(r_ref, range(4), mask, False) + edge_ref[...]
     high = own.astype(jnp.bfloat16).astype(jnp.float32)
     for part, (first, second) in enumerate(((high, own - high), (left, right))):
         for x in range(NXL):
@@ -271,7 +273,7 @@
             )
 
 
-def filter_step(slabs, w_ref, g_ref, out_ref, cur, prev, acc, half, ready):
+def filter_step(slabs, w_ref, g_ref, out_ref, cur, prev, acc, half):
     place = {x: at for at, x in enumerate(X_ORDER)}
     right_lanes = lax.broadcasted_iota(jnp.int32, (32, PLANE), 1) % 16 < 8
     for s, slab in enumerate(slabs):
@@ -281,7 +283,6 @@
             turn(cur, place[x], s, 0, block[:, :128].astype(jnp.float32))
             turn(cur, place[x], s, 1, block[:, 128:].astype(jnp.float32))
     prev[...] = jnp.zeros_like(prev)
-    ready()
     lines = w_ref[9 * PLANE :, :].astype(jnp.float32)
 
     def weight(kind):
@@ -294,6 +295,18 @@
             cur[at, 0, :, 2 * PLANE :] = jnp.where(right_lanes, middle, zero).astype(jnp.bfloat16)
             cur[at, 1, :, 2 * PLANE :] = jnp.where(right_lanes, right, left).astype(jnp.bfloat16)
             cur[at, 2, :, 2 * PLANE :] = jnp.where(right_lanes, zero, middle).astype(jnp.bfloat16)
+
+    def merge():
+        def pick(ref, at, lanes):
+            left, right = (ref[at, s, :, lanes].astype(jnp.float32) for s in (0, 2))
+            ref[at, 2, :, lanes] = jnp.where(right_lanes, right, left).astype(jnp.bfloat16)
+
+        for at in range(NXL):
+            pick(cur, at, slice(0, PLANE))
+            pick(cur, at, slice(PLANE, 2 * PLANE))
+            pick(prev, at, slice(0, PLANE))
+            cur[at, 2, :, 2 * PLANE :] = cur[at, 1, :, :PLANE]
+            cur[at, 1, :, 2 * PLANE :] = cur[at, 2, :, :PLANE]
 
     def apply(which, alpha, beta, store):
         first, last = which[0], which[-1] + 1
@@ -323,7 +336,10 @@
                 }
                 for x in range(NXL):
                     at = place[x]
-                    applied = acc[at, s, :, lanes] + extra[x] + g_ref[x, s, :, lanes] * v[x]
+                    diag = g_ref[x, s, :, lanes]
+                    if which == (1, 2) and s == 2:
+                        diag = jnp.where(right_lanes[:, :128], diag, g_ref[x, 0, :, lanes])
+                    applied = acc[at, s, :, lanes] + extra[x] + diag * v[x]
                     store(x, at, s, part, alpha * applied - beta * prev[at, s, :, lanes].astype(jnp.float32))
 
     def keep(x, at, s, part, new):
@@ -343,9 +359,13 @@
         apply((0, 1, 2), alpha, beta, keep)
         return carry
 
-    lax.fori_loop(0, DEGREE - 1, order, 0)
-    sides()
-    apply((1,), jnp.float32(2.0 / half), jnp.float32(1.0), emit)
+    lax.fori_loop(0, DEGREE - 2, order, 0)
+    merge()
+    two = jnp.float32(2.0 / half), jnp.float32(1.0)
+    apply((1, 2), *two, keep)
+    for at in range(NXL):
+        cur[at, 1, :, 2 * PLANE :] = cur[at, 2, :, :PLANE]
+    apply((1,), *two, emit)
 
 
 def turn(cur, at, s, part, value):
@@ -354,19 +374,15 @@
     cur[at, s, :, lanes] = pltpu.roll(value, shift, 0).astype(jnp.bfloat16)
 
 
-def first_kernel(centre, half, got, w_hbm, out_ref, g_ref, cur, prev, acc, w_ref, sem):
-    copy = pltpu.make_async_copy(w_hbm, w_ref, sem)
-    copy.start()
+def first_kernel(centre, half, got, w_ref, out_ref, g_ref, cur, prev, acc):
     diagonal(got, g_ref, centre)
     slabs = [got.at[:, NODES_DEV * s : NODES_DEV * (s + 1)] for s in range(3)]
-    filter_step(slabs, w_ref, g_ref, out_ref, cur, prev, acc, half, copy.wait)
-
-
-def later_kernel(half, c_ref, l_ref, r_ref, g_ref, st_ref, w_hbm, out_ref, cur, prev, acc, w_ref, sem):
-    copy = pltpu.make_async_copy(w_hbm, w_ref, sem)
-    copy.start()
+    filter_step(slabs, w_ref, g_ref, out_ref, cur, prev, acc, half)
+
+
+def later_kernel(half, c_ref, l_ref, r_ref, g_ref, st_ref, w_ref, out_ref, cur, prev, acc):
     out_ref[:, NODES_DEV:] = st_ref[...]
-    filter_step((l_ref, c_ref, r_ref), w_ref, g_ref, out_ref, cur, prev, acc, half, copy.wait)
+    filter_step((l_ref, c_ref, r_ref), w_ref, g_ref, out_ref, cur, prev, acc, half)
 
 
 def corr_kernel(factor, got, out_ref):
@@ -459,24 +475,21 @@
         pltpu.VMEM((NXL, 3, NWF, 3 * PLANE), bf),
         pltpu.VMEM((NXL, 3, NWF, PLANE), bf),
         pltpu.VMEM((NXL, 3, NWF, PLANE), f32),
-        pltpu.VMEM(weights.shape, bf),
     ]
     block, diag = call(
         functools.partial(first_kernel, centre, half),
-        (got,),
+        (got, weights),
         [shape((NWF, NODES_DEV), bf), shape((NXL, 3, NWF, PLANE), f32)],
-        scratch + [dma],
-        (weights,),
+        scratch,
     )
     left = passed_along(block, "cells", 1)
     right = passed_along(block, "cells", -1)
     factor = 1.0 / math.sqrt(NODES_DEV * n_cells * n_bands)
     (block,) = call(
         functools.partial(later_kernel, half),
-        (block, left, right, diag, stored),
+        (block, left, right, diag, stored, weights),
         [shape((NWF, 3 * NODES_DEV), bf)],
-        scratch + [dma],
-        (weights,),
+        scratch,
     )
     got = lax.all_to_all(block, "bands", 0, 0, tiled=True)
     filtered = got[:, :NODES_DEV]

time: 111 us -> 109 us (0.982)
  Pallas kernels: 12.4 us -> 10.6 us
    pallas_call x8, Pallas kernels: 12.4 us -> 10.6 us  [call(): pl.pallas_call(kernel, grid=(1,), in_specs=[full(a.shape) for a in args]...]
where the time goes in v6:
time: 109 us
  blocking collectives  40.5 us (37%)
  starting transfers between devices  36.9 us (34%)
  waiting for transfers between devices  17.1 us (16%)
  Pallas kernels  10.6 us (10%)
  local copies, waits for them, and re-layouts  3.01 us (3%)
    ppermute x4, starting transfers between devices, passed_along(): return lax.ppermute(block, axis, route)  27.1 us
    all_to_all x1, blocking collectives, shards(): got = lax.all_to_all(payload, 'bands', 0, 0, tiled=True)  18.9 us
    all_to_all x1, blocking collectives, shards(): got = lax.all_to_all(block, 'bands', 0, 0, tiled=True)  12.2 us
    pallas_call x8, Pallas kernels, call(): pl.pallas_call(kernel, grid=(1,), in_specs=[full(a.shape) for a in args]...  10.6 us
    all_to_all x1, waiting for transfers between devices, shards(): partial = lax.all_to_all(partial, 'cells', 0, 0, tiled=True)  10.2 us
    all_to_all x1, starting transfers between devices, shards(): partial = lax.all_to_all(partial, 'cells', 0, 0, tiled=True)  9.83 us
    all_to_all x1, blocking collectives, shards(): partial = lax.all_to_all(partial, 'bands', 0, 0, tiled=True)  9.42 us
    ppermute x4, waiting for transfers between devices, passed_along(): return lax.ppermute(block, axis, route)  6.98 us
  transfers between devices with their start and end apart: 5, of which 4 were waited for; matrix products, arithmetic and copies ran while one was open for 1% of the time, Pallas kernels for 1%

profile of v6, /device:TPU:1, one launch (start us, length us, event | category | flops | bytes accessed | tf_op | source)
XLA Modules:
  0.0 108.9 jit_solution(15742875536639910497)
XLA Ops:
  0.6 1.6 %shard_map.68.c_ref = bf16[32,2304]{1,0:T(8,128)(2,1)} custom-call(bf16[32,2048]{1,0:T(8,128)(2,1)} %v_hbm.1, f32[32,125]{1,0:T(8,128)} %bitcast.23, s32[32,125]{1,0:T(8,128)} %bitcast.24), custom_call_target="tpu_custom_call" | custom-call | tf_op jit(solution)/shard_map/pallas_call | solution.py:425
  2.3 6.6 %collective-permute-start = (bf16[32,2304]{1,0:T(8,128)(2,1)}, bf16[32,2304]{1,0:T(8,128)(2,1)S(1)}, u32[]{:S(2)}, u32[]{:S(2)}) collective-permute-start(bf16[32,2304]{1,0:T(8,128)(2,1)} %shard_map.68.c_ref), channel_id=1, source_target_pairs={{496,0},{0,16},{16,32},{32,48},{48,64},{64,80},{80,96},{96,112},{1... | collective-permute-start | bytes 442376 | tf_op jit(solution)/shard_map/ppermute | solution.py:439
  8.9 9.7 %collective-permute-start.1 = (bf16[32,2304]{1,0:T(8,128)(2,1)}, bf16[32,2304]{1,0:T(8,128)(2,1)S(1)}, u32[]{:S(2)}, u32[]{:S(2)}) collective-permute-start(bf16[32,2304]{1,0:T(8,128)(2,1)} %shard_map.68.c_ref), channel_id=1, source_target_pairs={{16,0},{32,16},{48,32},{64,48},{80,64},{96,80},{112,96},{128,112},... | collective-permute-start | bytes 442376 | tf_op jit(solution)/shard_map/ppermute | solution.py:439
  18.6 0.9 copy-done.1
  19.5 0.6 shard_map.69
  20.1 2.7 %collective-permute-done.l_ref = bf16[32,2304]{1,0:T(8,128)(2,1)S(1)} collective-permute-done((bf16[32,2304]{1,0:T(8,128)(2,1)}, bf16[32,2304]{1,0:T(8,128)(2,1)S(1)}, u32[]{:S(2)}, u32[]{:S(2)}) %collective-permute-start) | collective-permute-done | bytes 147488 | tf_op jit(solution)/shard_map/ppermute | solution.py:439
  22.8 0.0 collective-permute-done.1.r_ref
  22.8 1.0 shard_map.70
  23.8 0.3 all_to_all.28
  24.0 0.0 copy-start
  24.0 18.9 %all_to_all.44 = bf16[16,2,10496]{2,1,0:T(2,128)(2,1)S(1)} all-to-all(bf16[16,2,10496]{2,1,0:T(2,128)(2,1)S(1)} %all_to_all.28), channel_id=1, replica_groups=mesh['cells'=32,'bands'=16] {'bands'}, dimensions={0} | all-to-all | bytes 1343488 | tf_op jit(solution)/shard_map/all_to_all | solution.py:473
  42.9 0.3 all_to_all.30.got
  43.2 0.0 copy-start.2
  43.2 3.1 %shard_map.71 = (bf16[32,2048]{1,0:T(8,128)(2,1)S(1)}, f32[8,3,32,256]{3,2,1,0:T(8,128)S(1)}) custom-call(bf16[32,10496]{1,0:T(8,128)(2,1)S(1)} %all_to_all.30.got, bf16[2320,256]{1,0:T(8,128)(2,1)S(1)} %copy-done), custom_call_target="tpu_custom_call" | custom-call | tf_op jit(solution)/shard_map/pallas_call | solution.py:425
  46.3 4.7 %collective-permute-start.2 = (bf16[32,2048]{1,0:T(8,128)(2,1)S(1)}, bf16[32,2048]{1,0:T(8,128)(2,1)S(1)}, u32[]{:S(2)}, u32[]{:S(2)}) collective-permute-start(bf16[32,2048]{1,0:T(8,128)(2,1)S(1)} %get-tuple-element.12.c_ref), channel_id=1, source_target_pairs={{496,0},{0,16},{16,32},{32,48},{48,64},{64,80},{80,96},{96,112},{1... | collective-permute-start | bytes 393224 | tf_op jit(solution)/shard_map/ppermute | solution.py:439
  51.0 6.1 %collective-permute-start.3 = (bf16[32,2048]{1,0:T(8,128)(2,1)S(1)}, bf16[32,2048]{1,0:T(8,128)(2,1)S(1)}, u32[]{:S(2)}, u32[]{:S(2)}) collective-permute-start(bf16[32,2048]{1,0:T(8,128)(2,1)S(1)} %get-tuple-element.12.c_ref), channel_id=1, source_target_pairs={{16,0},{32,16},{48,32},{64,48},{80,64},{96,80},{112,96},{128,112},... | collective-permute-start | bytes 393224 | tf_op jit(solution)/shard_map/ppermute | solution.py:439
  57.1 0.2 copy.10
  57.2 0.3 copy.8
  57.5 0.1 copy.11
  57.6 2.8 %collective-permute-done.2.l_ref = bf16[32,2048]{1,0:T(8,128)(2,1)S(1)} collective-permute-done((bf16[32,2048]{1,0:T(8,128)(2,1)S(1)}, bf16[32,2048]{1,0:T(8,128)(2,1)S(1)}, u32[]{:S(2)}, u32[]{:S(2)}) %collective-permute-start.2) | collective-permute-done | bytes 131104 | tf_op jit(solution)/shard_map/ppermute | solution.py:439
  60.4 1.5 %collective-permute-done.3.r_ref = bf16[32,2048]{1,0:T(8,128)(2,1)S(1)} collective-permute-done((bf16[32,2048]{1,0:T(8,128)(2,1)S(1)}, bf16[32,2048]{1,0:T(8,128)(2,1)S(1)}, u32[]{:S(2)}, u32[]{:S(2)}) %collective-permute-start.3) | collective-permute-done | bytes 131104 | tf_op jit(solution)/shard_map/ppermute | solution.py:439
  61.9 2.7 %shard_map.72 = bf16[32,6144]{1,0:T(8,128)(2,1)S(1)} custom-call(bf16[32,2048]{1,0:T(8,128)(2,1)S(1)} %get-tuple-element.12.c_ref, bf16[32,2048]{1,0:T(8,128)(2,1)S(1)} %collective-permute-done.2.l_ref, bf16[32,2048]{1,0:T(8,128)(2,1)S(1)} %collective-permute-done.3.r_ref, f32[8,3,32,256]{3,2,1,0:T(8,128)S(1)} %get-tuple-element.13.g_ref, ...), custom_call_target="tpu_custom_call" | custom-call | tf_op jit(solution)/shard_map/pallas_call | solution.py:425
  64.6 0.3 all_to_all.31
  64.8 12.2 %all_to_all.45 = bf16[16,2,6144]{2,1,0:T(2,128)(2,1)S(1)} all-to-all(bf16[16,2,6144]{2,1,0:T(2,128)(2,1)S(1)} %all_to_all.31), channel_id=1, replica_groups=mesh['cells'=32,'bands'=16] {'bands'}, dimensions={0} | all-to-all | bytes 786432 | tf_op jit(solution)/shard_map/all_to_all | solution.py:494
  77.1 0.1 all_to_all.33.got
  77.2 0.4 shard_map.73
  77.6 9.4 %all_to_all.46 = f32[16,2,128]{2,1,0:T(2,128)S(1)} all-to-all(f32[16,2,128]{2,1,0:T(2,128)S(1)} %bitcast.17), channel_id=1, replica_groups=mesh['cells'=32,'bands'=16] {'bands'}, dimensions={0} | all-to-all | bytes 32768 | tf_op jit(solution)/shard_map/all_to_all | solution.py:497
  87.0 0.6 shard_map.74
  87.7 9.8 %all-to-all-start.3 = ((f32[32,1,128]{2,1,0:T(1,128)}), f32[32,1,128]{2,1,0:T(1,128)S(1)}, u32[]{:S(2)}, u32[]{:S(2)}) async-start(f32[32,1,128]{2,1,0:T(1,128)} %bitcast.6), calls=%async_computation.3 | async-start | bytes 32768 | tf_op jit(solution)/shard_map/all_to_all | solution.py:499
  97.5 0.7 slice.4
  98.2 10.2 %all-to-all-done.3 = f32[32,1,128]{2,1,0:T(1,128)S(1)} async-done(((f32[32,1,128]{2,1,0:T(1,128)}), f32[32,1,128]{2,1,0:T(1,128)S(1)}, u32[]{:S(2)}, u32[]{:S(2)}) %all-to-all-start.3) | async-done | bytes 16416 | tf_op jit(solution)/shard_map/all_to_all | solution.py:499
  108.3 0.6 shard_map.75
  (3 shorter events, 0.0 us)
Async XLA Ops:
  2.3 20.5 %collective-permute-start = (bf16[32,2304]{1,0:T(8,128)(2,1)}, bf16[32,2304]{1,0:T(8,128)(2,1)S(1)}, u32[]{:S(2)}, u32[]{:S(2)}) collective-permute-start(bf16[32,2304]{1,0:T(8,128)(2,1)} %shard_map.68.c_ref), channel_id=1, source_target_pairs={{496,0},{0,16},{16,32},{32,48},{48,64},{64,80},{80,96},{96,112},{1... | collective-permute-start | bytes 442376 | tf_op jit(solution)/shard_map/ppermute | solution.py:439
  8.9 13.9 %collective-permute-start.1 = (bf16[32,2304]{1,0:T(8,128)(2,1)}, bf16[32,2304]{1,0:T(8,128)(2,1)S(1)}, u32[]{:S(2)}, u32[]{:S(2)}) collective-permute-start(bf16[32,2304]{1,0:T(8,128)(2,1)} %shard_map.68.c_ref), channel_id=1, source_target_pairs={{16,0},{32,16},{48,32},{64,48},{80,64},{96,80},{112,96},{128,112},... | collective-permute-start | bytes 442376 | tf_op jit(solution)/shard_map/ppermute | solution.py:439
  18.6 0.9 copy-start.1
  24.0 19.1 %copy-start = (bf16[2320,256]{1,0:T(8,128)(2,1)S(1)}, bf16[2320,256]{1,0:T(8,128)(2,1)}, u32[]{:S(2)}) copy-start(bf16[2320,256]{1,0:T(8,128)(2,1)} %constant.2.clone.w_ref) | copy-start | bytes 3563524
  43.2 13.9 %copy-start.2 = (bf16[4,32768]{1,0:T(4,128)(2,1)S(1)}, bf16[4,32768]{1,0:T(4,128)(2,1)}, u32[]{:S(2)}) copy-start(bf16[4,32768]{1,0:T(4,128)(2,1)} %param.6) | copy-start | bytes 786436
  46.3 14.1 %collective-permute-start.2 = (bf16[32,2048]{1,0:T(8,128)(2,1)S(1)}, bf16[32,2048]{1,0:T(8,128)(2,1)S(1)}, u32[]{:S(2)}, u32[]{:S(2)}) collective-permute-start(bf16[32,2048]{1,0:T(8,128)(2,1)S(1)} %get-tuple-element.12.c_ref), channel_id=1, source_target_pairs={{496,0},{0,16},{16,32},{32,48},{48,64},{64,80},{80,96},{96,112},{1... | collective-permute-start | bytes 393224 | tf_op jit(solution)/shard_map/ppermute | solution.py:439
  51.0 10.9 %collective-permute-start.3 = (bf16[32,2048]{1,0:T(8,128)(2,1)S(1)}, bf16[32,2048]{1,0:T(8,128)(2,1)S(1)}, u32[]{:S(2)}, u32[]{:S(2)}) collective-permute-start(bf16[32,2048]{1,0:T(8,128)(2,1)S(1)} %get-tuple-element.12.c_ref), channel_id=1, source_target_pairs={{16,0},{32,16},{48,32},{64,48},{80,64},{96,80},{112,96},{128,112},... | collective-permute-start | bytes 393224 | tf_op jit(solution)/shard_map/ppermute | solution.py:439
  87.7 20.7 %all-to-all-start.3 = ((f32[32,1,128]{2,1,0:T(1,128)}), f32[32,1,128]{2,1,0:T(1,128)S(1)}, u32[]{:S(2)}, u32[]{:S(2)}) async-start(f32[32,1,128]{2,1,0:T(1,128)} %bitcast.6), calls=%async_computation.3 | async-start | bytes 32768 | tf_op jit(solution)/shard_map/all_to_all | solution.py:499

commit v7 on v6

--- a/solution.py
+++ b/solution.py
@@ -137,11 +137,11 @@
     return a, b, rest - 5 * b
 
 
-def message_kernel(v_hbm, pot_hbm, conn_hbm, out_ref, raw, conn, pot, sems):
+def message_kernel(v_hbm, pot_hbm, conn_hbm, out_hbm, raw, conn, pot, packed, sems):
     copies = [
         pltpu.make_async_copy(pot_hbm, raw, sems.at[0]),
         pltpu.make_async_copy(conn_hbm, conn, sems.at[1]),
-        pltpu.make_async_copy(v_hbm, out_ref.at[:, :NODES_DEV], sems.at[2]),
+        pltpu.make_async_copy(v_hbm, out_hbm.at[:, :NODES_DEV], sems.at[2]),
     ]
     for copy in copies:
         copy.start()
@@ -155,9 +155,12 @@
     cell = jnp.sum(here, axis=1, keepdims=True)
     high = pot[...].astype(jnp.bfloat16).astype(jnp.float32)
     low = pot[...] - high
-    out_ref[:, NODES_DEV : NODES_DEV + 128] = jnp.where(lane == 127, cell, high).astype(jnp.bfloat16)
-    out_ref[:, NODES_DEV + 128 :] = low.astype(jnp.bfloat16)
+    packed[:, :128] = jnp.where(lane == 127, cell, high).astype(jnp.bfloat16)
+    packed[:, 128:] = low.astype(jnp.bfloat16)
+    last = pltpu.make_async_copy(packed, out_hbm.at[:, NODES_DEV:], sems.at[3])
+    last.start()
     copies[2].wait()
+    last.wait()
 
 
 def pick_kind(kind):
@@ -263,126 +266,123 @@
         edges.append(edge.astype(jnp.bfloat16))
     for s in range(3):
         part = 0 if s == 1 else 1
+        at = V_AT + NODES_DEV * part
+        base = jnp.dot(pairs[s][:, :32], got[:, at : at + NODES_DEV], preferred_element_type=jnp.float32)
+        edge = jnp.dot(pairs[s][:, 32:], edges[part], preferred_element_type=jnp.float32)
         for x in range(NXL):
-            at = V_AT + NODES_DEV * part + PLANE * x
-            stack = jnp.concatenate([got[:, at : at + 128], edges[part][:, 128 * x : 128 * (x + 1)]], axis=0)
-            g_ref[x, s, :, :128] = jnp.dot(pairs[s], stack, preferred_element_type=jnp.float32) - centre
-            g_ref[x, s, :, 128:] = (
-                jnp.dot(pairs[s][:, :32], got[:, at + 128 : at + PLANE], preferred_element_type=jnp.float32)
-                - centre
-            )
-
-
-def filter_step(slabs, w_ref, g_ref, out_ref, cur, prev, acc, half):
+            at = PLANE * x
+            first = base[:, at : at + 128] + edge[:, 128 * x : 128 * (x + 1)]
+            g_ref[x, s, :, :128] = first - centre
+            g_ref[x, s, :, 128:] = base[:, at + 128 : at + PLANE] - centre
+
+
+def filter_step(slabs, w_ref, g_ref, out_ref, here, there, half):
     place = {x: at for at, x in enumerate(X_ORDER)}
-    right_lanes = lax.broadcasted_iota(jnp.int32, (32, PLANE), 1) % 16 < 8
-    for s, slab in enumerate(slabs):
-        for x in range(NXL):
-            block = slab[:, PLANE * x : PLANE * (x + 1)]
-            cur[place[x], s, :, :PLANE] = block
-            turn(cur, place[x], s, 0, block[:, :128].astype(jnp.float32))
-            turn(cur, place[x], s, 1, block[:, 128:].astype(jnp.float32))
-    prev[...] = jnp.zeros_like(prev)
+    right_lanes = (iota((32, 128), 1) & 15) < 8
     lines = w_ref[9 * PLANE :, :].astype(jnp.float32)
-
-    def weight(kind):
-        return w_ref[3 * PLANE * kind : 3 * PLANE * (kind + 1), :]
-
-    def sides():
-        for at in range(NXL):
-            left, middle, right = (cur[at, s, :, :PLANE].astype(jnp.float32) for s in range(3))
-            zero = jnp.zeros_like(left)
-            cur[at, 0, :, 2 * PLANE :] = jnp.where(right_lanes, middle, zero).astype(jnp.bfloat16)
-            cur[at, 1, :, 2 * PLANE :] = jnp.where(right_lanes, right, left).astype(jnp.bfloat16)
-            cur[at, 2, :, 2 * PLANE :] = jnp.where(right_lanes, zero, middle).astype(jnp.bfloat16)
-
-    def merge():
-        def pick(ref, at, lanes):
-            left, right = (ref[at, s, :, lanes].astype(jnp.float32) for s in (0, 2))
-            ref[at, 2, :, lanes] = jnp.where(right_lanes, right, left).astype(jnp.bfloat16)
-
-        for at in range(NXL):
-            pick(cur, at, slice(0, PLANE))
-            pick(cur, at, slice(PLANE, 2 * PLANE))
-            pick(prev, at, slice(0, PLANE))
-            cur[at, 2, :, 2 * PLANE :] = cur[at, 1, :, :PLANE]
-            cur[at, 1, :, 2 * PLANE :] = cur[at, 2, :, :PLANE]
-
-    def apply(which, alpha, beta, store):
+    halves = [slice(128 * part, 128 * (part + 1)) for part in range(2)]
+
+    def turned(part, value):
+        return pltpu.roll(value, 30 if part == 0 else 2, 0)
+
+    def put(ref, at, s, section, part, value):
+        ref[at, s, :, PLANE * section + 128 * part : PLANE * section + 128 * (part + 1)] = value.astype(
+            jnp.bfloat16
+        )
+
+    def put_sides(ref, at, part, left, middle, right):
+        zero = jnp.zeros_like(left)
+        put(ref, at, 0, 2, part, jnp.where(right_lanes, middle, zero))
+        put(ref, at, 1, 2, part, jnp.where(right_lanes, right, left))
+        put(ref, at, 2, 2, part, jnp.where(right_lanes, zero, middle))
+
+    for x in range(NXL):
+        for part in range(2):
+            values = []
+            for s, slab in enumerate(slabs):
+                value = slab[:, PLANE * x + 128 * part : PLANE * x + 128 * (part + 1)].astype(jnp.float32)
+                values.append(value)
+                put(here, place[x], s, 0, part, value)
+                put(here, place[x], s, 1, part, turned(part, value))
+            put_sides(here, place[x], part, *values)
+
+    def apply(src, dst, which, order):
+        alpha = (1.0 if order == 0 else 2.0) / half
         first, last = which[0], which[-1] + 1
-        for kind, (low, high) in enumerate(CLASS_ROWS):
-            rows = cur[low:high, first:last]
+        for kind in (1, 0, 2):
+            low, high = CLASS_ROWS[kind]
             count = (high - low) * (last - first) * 32
             result = jnp.dot(
-                rows.reshape(count, 3 * PLANE), weight(kind), preferred_element_type=jnp.float32
-            )
-            acc[low:high, first:last] = result.reshape(high - low, last - first, 32, PLANE)
-        for s in which:
-            for part in range(2):
-                lanes = slice(128 * part, 128 * (part + 1))
-                v = [cur[place[x], s, :, lanes].astype(jnp.float32) for x in range(NXL)]
-                c01, c02, c03, c04, c12, c13 = (lines[row : row + 1, lanes] for row in range(6))
-                s17, s26, s35 = v[1] + v[7], v[2] + v[6], v[3] + v[5]
-                s04 = c02 * (v[0] + v[4])
-                extra = {
-                    0: c01 * s17 + c02 * s26 + c03 * s35 + c04 * v[4],
-                    4: c01 * s35 + c02 * s26 + c03 * s17 + c04 * v[0],
-                    1: c01 * v[0] + c12 * v[2] + c13 * v[3] + c03 * v[4],
-                    3: c01 * v[4] + c12 * v[2] + c13 * v[1] + c03 * v[0],
-                    5: c01 * v[4] + c12 * v[6] + c13 * v[7] + c03 * v[0],
-                    7: c01 * v[0] + c12 * v[6] + c13 * v[5] + c03 * v[4],
-                    2: s04 + c12 * (v[1] + v[3]),
-                    6: s04 + c12 * (v[5] + v[7]),
-                }
-                for x in range(NXL):
-                    at = place[x]
-                    diag = g_ref[x, s, :, lanes]
-                    if which == (1, 2) and s == 2:
-                        diag = jnp.where(right_lanes[:, :128], diag, g_ref[x, 0, :, lanes])
-                    applied = acc[at, s, :, lanes] + extra[x] + diag * v[x]
-                    store(x, at, s, part, alpha * applied - beta * prev[at, s, :, lanes].astype(jnp.float32))
-
-    def keep(x, at, s, part, new):
-        lanes = slice(128 * part, 128 * (part + 1))
-        prev[at, s, :, lanes] = cur[at, s, :, lanes]
-        new = new.astype(jnp.bfloat16)
-        cur[at, s, :, lanes] = new
-        turn(cur, at, s, part, new.astype(jnp.float32))
-
-    def emit(x, at, s, part, new):
-        out_ref[:, PLANE * x + 128 * part : PLANE * x + 128 * (part + 1)] = new.astype(jnp.bfloat16)
-
-    def order(k, carry):
-        sides()
-        alpha = jnp.where(k == 0, jnp.float32(1.0 / half), jnp.float32(2.0 / half))
-        beta = jnp.where(k == 0, jnp.float32(0.0), jnp.float32(1.0))
-        apply((0, 1, 2), alpha, beta, keep)
-        return carry
-
-    lax.fori_loop(0, DEGREE - 2, order, 0)
-    merge()
-    two = jnp.float32(2.0 / half), jnp.float32(1.0)
-    apply((1, 2), *two, keep)
-    for at in range(NXL):
-        cur[at, 1, :, 2 * PLANE :] = cur[at, 2, :, :PLANE]
-    apply((1,), *two, emit)
-
-
-def turn(cur, at, s, part, value):
-    shift = 30 if part == 0 else 2
-    lanes = slice(PLANE + 128 * part, PLANE + 128 * (part + 1))
-    cur[at, s, :, lanes] = pltpu.roll(value, shift, 0).astype(jnp.bfloat16)
-
-
-def first_kernel(centre, half, got, w_ref, out_ref, g_ref, cur, prev, acc):
+                src[low:high, first:last].reshape(count, 3 * PLANE),
+                w_ref[3 * PLANE * kind : 3 * PLANE * (kind + 1), :],
+                preferred_element_type=jnp.float32,
+            ).reshape(high - low, last - first, 32, PLANE)
+            for at in range(low, high):
+                x = X_ORDER[at]
+                for part in range(2):
+                    lanes = halves[part]
+                    c01, c02, c03, c04, c12, c13 = (lines[row : row + 1, lanes] for row in range(6))
+                    values = {}
+                    for s in which:
+                        v = lambda other: src[place[other % 8], s, :, lanes].astype(jnp.float32)
+                        if x in (0, 4):
+                            extra = c01 * (v(x + 1) + v(x + 7)) + c02 * (v(x + 2) + v(x + 6))
+                            extra = extra + c03 * (v(x + 3) + v(x + 5)) + c04 * v(x + 4)
+                        elif x in (2, 6):
+                            extra = c02 * (v(x - 2) + v(x + 2)) + c12 * (v(x - 1) + v(x + 1))
+                        else:
+                            step = 1 if x in (1, 5) else -1
+                            extra = c01 * v(x - step) + c12 * v(x + step)
+                            extra = extra + c13 * v(x + 2 * step) + c03 * v(x + 3 * step)
+                        diag = g_ref[x, s, :, lanes]
+                        if which == (1, 2) and s == 2:
+                            diag = jnp.where(right_lanes, diag, g_ref[x, 0, :, lanes])
+                        new = alpha * (result[at - low, s - first, :, lanes] + extra + diag * v(x))
+                        if order:
+                            new = new - dst[at, s, :, lanes].astype(jnp.float32)
+                        if order < DEGREE - 1:
+                            new = new.astype(jnp.bfloat16).astype(jnp.float32)
+                            put(dst, at, s, 0, part, new)
+                            values[s] = new
+                        else:
+                            out_ref[:, PLANE * x + 128 * part : PLANE * x + 128 * (part + 1)] = new.astype(
+                                jnp.bfloat16
+                            )
+                    if order == 0:
+                        for s in which:
+                            put(dst, at, s, 1, part, turned(part, values[s]))
+                        put_sides(dst, at, part, values[0], values[1], values[2])
+                    elif order == 1:
+                        edge = jnp.where(right_lanes, values[2], values[0])
+                        old = [src[at, s, :, lanes].astype(jnp.float32) for s in (0, 2)]
+                        put(dst, at, 1, 1, part, turned(part, values[1]))
+                        put(dst, at, 1, 2, part, edge)
+                        put(dst, at, 2, 0, part, edge)
+                        put(dst, at, 2, 1, part, turned(part, edge))
+                        put(dst, at, 2, 2, part, values[1])
+                        edges.append((at, part, jnp.where(right_lanes, old[1], old[0])))
+                    elif order == 2:
+                        put(dst, at, 1, 1, part, turned(part, values[1]))
+                        put(dst, at, 1, 2, part, values[2])
+
+    edges = []
+    apply(here, there, (0, 1, 2), 0)
+    apply(there, here, (0, 1, 2), 1)
+    for at, part, edge in edges:
+        put(there, at, 2, 0, part, edge)
+    apply(here, there, (1, 2), 2)
+    apply(there, here, (1,), 3)
+
+
+def first_kernel(centre, half, got, w_ref, out_ref, g_ref, here, there):
     diagonal(got, g_ref, centre)
     slabs = [got.at[:, NODES_DEV * s : NODES_DEV * (s + 1)] for s in range(3)]
-    filter_step(slabs, w_ref, g_ref, out_ref, cur, prev, acc, half)
-
-
-def later_kernel(half, c_ref, l_ref, r_ref, g_ref, st_ref, w_ref, out_ref, cur, prev, acc):
+    filter_step(slabs, w_ref, g_ref, out_ref, here, there, half)
+
+
+def later_kernel(half, c_ref, l_ref, r_ref, g_ref, st_ref, w_ref, out_ref, here, there):
     out_ref[:, NODES_DEV:] = st_ref[...]
-    filter_step((l_ref, c_ref, r_ref), w_ref, g_ref, out_ref, cur, prev, acc, half)
+    filter_step((l_ref, c_ref, r_ref), w_ref, g_ref, out_ref, here, there, half)
 
 
 def corr_kernel(factor, got, out_ref):
@@ -420,17 +420,16 @@
     return pl.BlockSpec(shape, lambda *_: (0,) * len(shape))
 
 
-def call(kernel, args, outs, scratch=(), far=(), limit=VMEM):
-    hbm = pl.BlockSpec(memory_space=pltpu.HBM)
+def call(kernel, args, outs, scratch=()):
     return pl.pallas_call(
         kernel,
         grid=(1,),
-        in_specs=[full(a.shape) for a in args] + [hbm] * len(far),
+        in_specs=[full(a.shape) for a in args],
         out_specs=[full(o.shape) for o in outs],
         out_shape=list(outs),
         scratch_shapes=list(scratch),
-        compiler_params=pltpu.CompilerParams(vmem_limit_bytes=limit),
-    )(*args, *far)
+        compiler_params=pltpu.CompilerParams(vmem_limit_bytes=VMEM),
+    )(*args)
 
 
 def passed_along(block, axis, distance):
@@ -446,20 +445,21 @@
     shape = jax.ShapeDtypeStruct
     n_cells, n_bands = lax.axis_size("cells"), lax.axis_size("bands")
     stored = stored_blocks.reshape(2, 2, n_bands, NODES_DEV).transpose(2, 1, 0, 3).reshape(NWF, 2 * NODES_DEV)
-    dma = pltpu.SemaphoreType.DMA
-    (message,) = call(
+    hbm = pl.BlockSpec(memory_space=pltpu.HBM)
+    message = pl.pallas_call(
         message_kernel,
-        (),
-        [shape((NWF, MESSAGE), bf)],
-        [
+        in_specs=[hbm] * 3,
+        out_specs=hbm,
+        out_shape=shape((NWF, MESSAGE), bf),
+        scratch_shapes=[
             pltpu.VMEM((32, 125), f32),
             pltpu.VMEM((32, 125), jnp.int32),
             pltpu.VMEM((32, 128), f32),
-            dma((3,)),
+            pltpu.VMEM((32, 256), bf),
+            pltpu.SemaphoreType.DMA((4,)),
         ],
-        (cur_block, cell_potential.T, connectivity.T),
-        62 * 1024 * 1024,
-    )
+        compiler_params=pltpu.CompilerParams(vmem_limit_bytes=62 * 1024 * 1024),
+    )(cur_block, cell_potential.T, connectivity.T)
     left = passed_along(message, "cells", 1)
     right = passed_along(message, "cells", -1)
     shapes = [shape((8, LANES_V), f32), shape((8, LANES_V), f32), shape((128, LANES_V), f32)]
@@ -473,8 +473,7 @@
     got = lax.all_to_all(payload, "bands", 0, 0, tiled=True)
     scratch = [
         pltpu.VMEM((NXL, 3, NWF, 3 * PLANE), bf),
-        pltpu.VMEM((NXL, 3, NWF, PLANE), bf),
-        pltpu.VMEM((NXL, 3, NWF, PLANE), f32),
+        pltpu.VMEM((NXL, 3, NWF, 3 * PLANE), bf),
     ]
     block, diag = call(
         functools.partial(first_kernel, centre, half),

time: 109 us -> 112 us (1.028)
  Pallas kernels: 10.6 us -> 13.6 us
    pallas_call x8, Pallas kernels: 10.6 us -> 13.6 us  [the longest x7 8.46 us: call(): pl.pallas_call(kernel, grid=(1,), in_specs=[full(a.shape) for a in args],...]
where the time goes in v7:
time: 112 us
  blocking collectives  40.5 us (36%)
  starting transfers between devices  36.9 us (33%)
  waiting for transfers between devices  17.1 us (15%)
  Pallas kernels  13.6 us (12%)
  local copies, waits for them, and re-layouts  3.01 us (3%)
    ppermute x4, starting transfers between devices, passed_along(): return lax.ppermute(block, axis, route)  27.1 us
    all_to_all x1, blocking collectives, shards(): got = lax.all_to_all(payload, 'bands', 0, 0, tiled=True)  18.9 us
    all_to_all x1, blocking collectives, shards(): got = lax.all_to_all(block, 'bands', 0, 0, tiled=True)  12.2 us
    all_to_all x1, waiting for transfers between devices, shards(): partial = lax.all_to_all(partial, 'cells', 0, 0, tiled=True)  10.2 us
    all_to_all x1, starting transfers between devices, shards(): partial = lax.all_to_all(partial, 'cells', 0, 0, tiled=True)  9.83 us
    all_to_all x1, blocking collectives, shards(): partial = lax.all_to_all(partial, 'bands', 0, 0, tiled=True)  9.42 us
    pallas_call x7, Pallas kernels, call(): pl.pallas_call(kernel, grid=(1,), in_specs=[full(a.shape) for a in args],...  8.46 us
    ppermute x4, waiting for transfers between devices, passed_along(): return lax.ppermute(block, axis, route)  6.98 us
  transfers between devices with their start and end apart: 5, of which 4 were waited for; matrix products, arithmetic and copies ran while one was open for 1% of the time, Pallas kernels for 1%

profile of v7, /device:TPU:1, one launch (start us, length us, event | category | flops | bytes accessed | tf_op | source)
XLA Modules:
  0.0 111.9 jit_solution(15507838708232078725)
XLA Ops:
  0.6 5.1 %shard_map.68.c_ref = bf16[32,2304]{1,0:T(8,128)(2,1)} custom-call(bf16[32,2048]{1,0:T(8,128)(2,1)} %v_hbm.1, f32[32,125]{1,0:T(8,128)} %bitcast.23, s32[32,125]{1,0:T(8,128)} %bitcast.24), custom_call_target="tpu_custom_call" | custom-call | tf_op jit(solution)/shard_map/pallas_call | solution.py:449
  5.7 6.6 %collective-permute-start = (bf16[32,2304]{1,0:T(8,128)(2,1)}, bf16[32,2304]{1,0:T(8,128)(2,1)S(1)}, u32[]{:S(2)}, u32[]{:S(2)}) collective-permute-start(bf16[32,2304]{1,0:T(8,128)(2,1)} %shard_map.68.c_ref), channel_id=1, source_target_pairs={{496,0},{0,16},{16,32},{32,48},{48,64},{64,80},{80,96},{96,112},{1... | collective-permute-start | bytes 442376 | tf_op jit(solution)/shard_map/ppermute | solution.py:438
  12.4 9.7 %collective-permute-start.1 = (bf16[32,2304]{1,0:T(8,128)(2,1)}, bf16[32,2304]{1,0:T(8,128)(2,1)S(1)}, u32[]{:S(2)}, u32[]{:S(2)}) collective-permute-start(bf16[32,2304]{1,0:T(8,128)(2,1)} %shard_map.68.c_ref), channel_id=1, source_target_pairs={{16,0},{32,16},{48,32},{64,48},{80,64},{96,80},{112,96},{128,112},... | collective-permute-start | bytes 442376 | tf_op jit(solution)/shard_map/ppermute | solution.py:438
  22.1 0.9 copy-done.1
  23.0 0.6 shard_map.69
  23.6 2.7 %collective-permute-done.l_ref = bf16[32,2304]{1,0:T(8,128)(2,1)S(1)} collective-permute-done((bf16[32,2304]{1,0:T(8,128)(2,1)}, bf16[32,2304]{1,0:T(8,128)(2,1)S(1)}, u32[]{:S(2)}, u32[]{:S(2)}) %collective-permute-start) | collective-permute-done | bytes 147488 | tf_op jit(solution)/shard_map/ppermute | solution.py:438
  26.3 0.0 collective-permute-done.1.r_ref
  26.3 1.0 shard_map.70
  27.3 0.3 all_to_all.28
  27.5 0.0 copy-start
  27.5 18.9 %all_to_all.44 = bf16[16,2,10496]{2,1,0:T(2,128)(2,1)S(1)} all-to-all(bf16[16,2,10496]{2,1,0:T(2,128)(2,1)S(1)} %all_to_all.28), channel_id=1, replica_groups=mesh['cells'=32,'bands'=16] {'bands'}, dimensions={0} | all-to-all | bytes 1343488 | tf_op jit(solution)/shard_map/all_to_all | solution.py:473
  46.4 0.3 all_to_all.30.got
  46.7 0.0 copy-start.2
  46.7 2.8 %shard_map.71 = (bf16[32,2048]{1,0:T(8,128)(2,1)S(1)}, f32[8,3,32,256]{3,2,1,0:T(8,128)S(1)}) custom-call(bf16[32,10496]{1,0:T(8,128)(2,1)S(1)} %all_to_all.30.got, bf16[2320,256]{1,0:T(8,128)(2,1)S(1)} %copy-done), custom_call_target="tpu_custom_call" | custom-call | tf_op jit(solution)/shard_map/pallas_call | solution.py:424
  49.5 4.7 %collective-permute-start.2 = (bf16[32,2048]{1,0:T(8,128)(2,1)S(1)}, bf16[32,2048]{1,0:T(8,128)(2,1)S(1)}, u32[]{:S(2)}, u32[]{:S(2)}) collective-permute-start(bf16[32,2048]{1,0:T(8,128)(2,1)S(1)} %get-tuple-element.12.c_ref), channel_id=1, source_target_pairs={{496,0},{0,16},{16,32},{32,48},{48,64},{64,80},{80,96},{96,112},{1... | collective-permute-start | bytes 393224 | tf_op jit(solution)/shard_map/ppermute | solution.py:438
  54.2 6.1 %collective-permute-start.3 = (bf16[32,2048]{1,0:T(8,128)(2,1)S(1)}, bf16[32,2048]{1,0:T(8,128)(2,1)S(1)}, u32[]{:S(2)}, u32[]{:S(2)}) collective-permute-start(bf16[32,2048]{1,0:T(8,128)(2,1)S(1)} %get-tuple-element.12.c_ref), channel_id=1, source_target_pairs={{16,0},{32,16},{48,32},{64,48},{80,64},{96,80},{112,96},{128,112},... | collective-permute-start | bytes 393224 | tf_op jit(solution)/shard_map/ppermute | solution.py:438
  60.3 0.2 copy.10
  60.5 0.3 copy.8
  60.8 0.1 copy.11
  60.8 2.8 %collective-permute-done.2.l_ref = bf16[32,2048]{1,0:T(8,128)(2,1)S(1)} collective-permute-done((bf16[32,2048]{1,0:T(8,128)(2,1)S(1)}, bf16[32,2048]{1,0:T(8,128)(2,1)S(1)}, u32[]{:S(2)}, u32[]{:S(2)}) %collective-permute-start.2) | collective-permute-done | bytes 131104 | tf_op jit(solution)/shard_map/ppermute | solution.py:438
  63.6 1.5 %collective-permute-done.3.r_ref = bf16[32,2048]{1,0:T(8,128)(2,1)S(1)} collective-permute-done((bf16[32,2048]{1,0:T(8,128)(2,1)S(1)}, bf16[32,2048]{1,0:T(8,128)(2,1)S(1)}, u32[]{:S(2)}, u32[]{:S(2)}) %collective-permute-start.3) | collective-permute-done | bytes 131104 | tf_op jit(solution)/shard_map/ppermute | solution.py:438
  65.1 2.4 %shard_map.72 = bf16[32,6144]{1,0:T(8,128)(2,1)S(1)} custom-call(bf16[32,2048]{1,0:T(8,128)(2,1)S(1)} %get-tuple-element.12.c_ref, bf16[32,2048]{1,0:T(8,128)(2,1)S(1)} %collective-permute-done.2.l_ref, bf16[32,2048]{1,0:T(8,128)(2,1)S(1)} %collective-permute-done.3.r_ref, f32[8,3,32,256]{3,2,1,0:T(8,128)S(1)} %get-tuple-element.13.g_ref, ...), custom_call_target="tpu_custom_call" | custom-call | tf_op jit(solution)/shard_map/pallas_call | solution.py:424
  67.6 0.3 all_to_all.31
  67.8 12.2 %all_to_all.45 = bf16[16,2,6144]{2,1,0:T(2,128)(2,1)S(1)} all-to-all(bf16[16,2,6144]{2,1,0:T(2,128)(2,1)S(1)} %all_to_all.31), channel_id=1, replica_groups=mesh['cells'=32,'bands'=16] {'bands'}, dimensions={0} | all-to-all | bytes 786432 | tf_op jit(solution)/shard_map/all_to_all | solution.py:493
  80.0 0.1 all_to_all.33.got
  80.2 0.4 shard_map.73
  80.6 9.4 %all_to_all.46 = f32[16,2,128]{2,1,0:T(2,128)S(1)} all-to-all(f32[16,2,128]{2,1,0:T(2,128)S(1)} %bitcast.17), channel_id=1, replica_groups=mesh['cells'=32,'bands'=16] {'bands'}, dimensions={0} | all-to-all | bytes 32768 | tf_op jit(solution)/shard_map/all_to_all | solution.py:496
  90.0 0.6 shard_map.74
  90.6 9.8 %all-to-all-start.3 = ((f32[32,1,128]{2,1,0:T(1,128)}), f32[32,1,128]{2,1,0:T(1,128)S(1)}, u32[]{:S(2)}, u32[]{:S(2)}) async-start(f32[32,1,128]{2,1,0:T(1,128)} %bitcast.6), calls=%async_computation.3 | async-start | bytes 32768 | tf_op jit(solution)/shard_map/all_to_all | solution.py:498
  100.5 0.7 slice.4
  101.2 10.2 %all-to-all-done.3 = f32[32,1,128]{2,1,0:T(1,128)S(1)} async-done(((f32[32,1,128]{2,1,0:T(1,128)}), f32[32,1,128]{2,1,0:T(1,128)S(1)}, u32[]{:S(2)}, u32[]{:S(2)}) %all-to-all-start.3) | async-done | bytes 16416 | tf_op jit(solution)/shard_map/all_to_all | solution.py:498
  111.3 0.6 shard_map.75
  (3 shorter events, 0.0 us)
Async XLA Ops:
  5.7 20.5 %collective-permute-start = (bf16[32,2304]{1,0:T(8,128)(2,1)}, bf16[32,2304]{1,0:T(8,128)(2,1)S(1)}, u32[]{:S(2)}, u32[]{:S(2)}) collective-permute-start(bf16[32,2304]{1,0:T(8,128)(2,1)} %shard_map.68.c_ref), channel_id=1, source_target_pairs={{496,0},{0,16},{16,32},{32,48},{48,64},{64,80},{80,96},{96,112},{1... | collective-permute-start | bytes 442376 | tf_op jit(solution)/shard_map/ppermute | solution.py:438
  12.4 13.9 %collective-permute-start.1 = (bf16[32,2304]{1,0:T(8,128)(2,1)}, bf16[32,2304]{1,0:T(8,128)(2,1)S(1)}, u32[]{:S(2)}, u32[]{:S(2)}) collective-permute-start(bf16[32,2304]{1,0:T(8,128)(2,1)} %shard_map.68.c_ref), channel_id=1, source_target_pairs={{16,0},{32,16},{48,32},{64,48},{80,64},{96,80},{112,96},{128,112},... | collective-permute-start | bytes 442376 | tf_op jit(solution)/shard_map/ppermute | solution.py:438
  22.1 0.9 copy-start.1
  27.5 19.1 %copy-start = (bf16[2320,256]{1,0:T(8,128)(2,1)S(1)}, bf16[2320,256]{1,0:T(8,128)(2,1)}, u32[]{:S(2)}) copy-start(bf16[2320,256]{1,0:T(8,128)(2,1)} %constant.2.clone.w_ref) | copy-start | bytes 3563524
  46.7 13.6 %copy-start.2 = (bf16[4,32768]{1,0:T(4,128)(2,1)S(1)}, bf16[4,32768]{1,0:T(4,128)(2,1)}, u32[]{:S(2)}) copy-start(bf16[4,32768]{1,0:T(4,128)(2,1)} %param.6) | copy-start | bytes 786436
  49.5 14.1 %collective-permute-start.2 = (bf16[32,2048]{1,0:T(8,128)(2,1)S(1)}, bf16[32,2048]{1,0:T(8,128)(2,1)S(1)}, u32[]{:S(2)}, u32[]{:S(2)}) collective-permute-start(bf16[32,2048]{1,0:T(8,128)(2,1)S(1)} %get-tuple-element.12.c_ref), channel_id=1, source_target_pairs={{496,0},{0,16},{16,32},{32,48},{48,64},{64,80},{80,96},{96,112},{1... | collective-permute-start | bytes 393224 | tf_op jit(solution)/shard_map/ppermute | solution.py:438
  54.2 10.9 %collective-permute-start.3 = (bf16[32,2048]{1,0:T(8,128)(2,1)S(1)}, bf16[32,2048]{1,0:T(8,128)(2,1)S(1)}, u32[]{:S(2)}, u32[]{:S(2)}) collective-permute-start(bf16[32,2048]{1,0:T(8,128)(2,1)S(1)} %get-tuple-element.12.c_ref), channel_id=1, source_target_pairs={{16,0},{32,16},{48,32},{64,48},{80,64},{96,80},{112,96},{128,112},... | collective-permute-start | bytes 393224 | tf_op jit(solution)/shard_map/ppermute | solution.py:438
  90.6 20.7 %all-to-all-start.3 = ((f32[32,1,128]{2,1,0:T(1,128)}), f32[32,1,128]{2,1,0:T(1,128)S(1)}, u32[]{:S(2)}, u32[]{:S(2)}) async-start(f32[32,1,128]{2,1,0:T(1,128)} %bitcast.6), calls=%async_computation.3 | async-start | bytes 32768 | tf_op jit(solution)/shard_map/all_to_all | solution.py:498

commit v8 on v7

--- a/solution.py
+++ b/solution.py
@@ -137,11 +137,11 @@
     return a, b, rest - 5 * b
 
 
-def message_kernel(v_hbm, pot_hbm, conn_hbm, out_hbm, raw, conn, pot, packed, sems):
+def message_kernel(v_hbm, pot_hbm, conn_hbm, out_ref, raw, conn, pot, sems):
     copies = [
         pltpu.make_async_copy(pot_hbm, raw, sems.at[0]),
         pltpu.make_async_copy(conn_hbm, conn, sems.at[1]),
-        pltpu.make_async_copy(v_hbm, out_hbm.at[:, :NODES_DEV], sems.at[2]),
+        pltpu.make_async_copy(v_hbm, out_ref.at[:, :NODES_DEV], sems.at[2]),
     ]
     for copy in copies:
         copy.start()
@@ -155,12 +155,9 @@
     cell = jnp.sum(here, axis=1, keepdims=True)
     high = pot[...].astype(jnp.bfloat16).astype(jnp.float32)
     low = pot[...] - high
-    packed[:, :128] = jnp.where(lane == 127, cell, high).astype(jnp.bfloat16)
-    packed[:, 128:] = low.astype(jnp.bfloat16)
-    last = pltpu.make_async_copy(packed, out_hbm.at[:, NODES_DEV:], sems.at[3])
-    last.start()
+    out_ref[:, NODES_DEV : NODES_DEV + 128] = jnp.where(lane == 127, cell, high).astype(jnp.bfloat16)
+    out_ref[:, NODES_DEV + 128 :] = low.astype(jnp.bfloat16)
     copies[2].wait()
-    last.wait()
 
 
 def pick_kind(kind):
@@ -420,16 +417,17 @@
     return pl.BlockSpec(shape, lambda *_: (0,) * len(shape))
 
 
-def call(kernel, args, outs, scratch=()):
+def call(kernel, args, outs, scratch=(), far=(), limit=VMEM):
+    hbm = pl.BlockSpec(memory_space=pltpu.HBM)
     return pl.pallas_call(
         kernel,
         grid=(1,),
-        in_specs=[full(a.shape) for a in args],
+        in_specs=[full(a.shape) for a in args] + [hbm] * len(far),
         out_specs=[full(o.shape) for o in outs],
         out_shape=list(outs),
         scratch_shapes=list(scratch),
-        compiler_params=pltpu.CompilerParams(vmem_limit_bytes=VMEM),
-    )(*args)
+        compiler_params=pltpu.CompilerParams(vmem_limit_bytes=limit),
+    )(*args, *far)
 
 
 def passed_along(block, axis, distance):
@@ -445,21 +443,19 @@
     shape = jax.ShapeDtypeStruct
     n_cells, n_bands = lax.axis_size("cells"), lax.axis_size("bands")
     stored = stored_blocks.reshape(2, 2, n_bands, NODES_DEV).transpose(2, 1, 0, 3).reshape(NWF, 2 * NODES_DEV)
-    hbm = pl.BlockSpec(memory_space=pltpu.HBM)
-    message = pl.pallas_call(
+    (message,) = call(
         message_kernel,
-        in_specs=[hbm] * 3,
-        out_specs=hbm,
-        out_shape=shape((NWF, MESSAGE), bf),
-        scratch_shapes=[
+        (),
+        [shape((NWF, MESSAGE), bf)],
+        [
             pltpu.VMEM((32, 125), f32),
             pltpu.VMEM((32, 125), jnp.int32),
             pltpu.VMEM((32, 128), f32),
-            pltpu.VMEM((32, 256), bf),
-            pltpu.SemaphoreType.DMA((4,)),
+            pltpu.SemaphoreType.DMA((3,)),
         ],
-        compiler_params=pltpu.CompilerParams(vmem_limit_bytes=62 * 1024 * 1024),
-    )(cur_block, cell_potential.T, connectivity.T)
+        (cur_block, cell_potential.T, connectivity.T),
+        62 * 1024 * 1024,
+    )
     left = passed_along(message, "cells", 1)
     right = passed_along(message, "cells", -1)
     shapes = [shape((8, LANES_V), f32), shape((8, LANES_V), f32), shape((128, LANES_V), f32)]

time: 112 us -> 109 us (0.973)
  Pallas kernels: 13.6 us -> 10.1 us
    pallas_call x8, Pallas kernels: 13.6 us -> 10.1 us  [call(): pl.pallas_call(kernel, grid=(1,), in_specs=[full(a.shape) for a in args]...]
where the time goes in v8:
time: 109 us; the launch traced here: 108 us
  blocking collectives  40.5 us (37%)
  starting transfers between devices  36.9 us (34%)
  waiting for transfers between devices  17.1 us (16%)
  Pallas kernels  10.1 us (9%)
  local copies, waits for them, and re-layouts  3.01 us (3%)
    ppermute x4, starting transfers between devices, passed_along(): return lax.ppermute(block, axis, route)  27.1 us
    all_to_all x1, blocking collectives, shards(): got = lax.all_to_all(payload, 'bands', 0, 0, tiled=True)  18.9 us
    all_to_all x1, blocking collectives, shards(): got = lax.all_to_all(block, 'bands', 0, 0, tiled=True)  12.2 us
    all_to_all x1, waiting for transfers between devices, shards(): partial = lax.all_to_all(partial, 'cells', 0, 0, tiled=True)  10.2 us
    pallas_call x8, Pallas kernels, call(): pl.pallas_call(kernel, grid=(1,), in_specs=[full(a.shape) for a in args]...  10.1 us
    all_to_all x1, starting transfers between devices, shards(): partial = lax.all_to_all(partial, 'cells', 0, 0, tiled=True)  9.84 us
    all_to_all x1, blocking collectives, shards(): partial = lax.all_to_all(partial, 'bands', 0, 0, tiled=True)  9.42 us
    ppermute x4, waiting for transfers between devices, passed_along(): return lax.ppermute(block, axis, route)  6.98 us
  transfers between devices with their start and end apart: 5, of which 4 were waited for; matrix products, arithmetic and copies ran while one was open for 1% of the time, Pallas kernels for 1%

profile of v8, /device:TPU:1, one launch (start us, length us, event | category | flops | bytes accessed | tf_op | source)
XLA Modules:
  0.0 108.4 jit_solution(10203152401883157728)
XLA Ops:
  0.6 1.6 %shard_map.68.c_ref = bf16[32,2304]{1,0:T(8,128)(2,1)} custom-call(bf16[32,2048]{1,0:T(8,128)(2,1)} %v_hbm.1, f32[32,125]{1,0:T(8,128)} %bitcast.23, s32[32,125]{1,0:T(8,128)} %bitcast.24), custom_call_target="tpu_custom_call" | custom-call | tf_op jit(solution)/shard_map/pallas_call | solution.py:422
  2.3 6.6 %collective-permute-start = (bf16[32,2304]{1,0:T(8,128)(2,1)}, bf16[32,2304]{1,0:T(8,128)(2,1)S(1)}, u32[]{:S(2)}, u32[]{:S(2)}) collective-permute-start(bf16[32,2304]{1,0:T(8,128)(2,1)} %shard_map.68.c_ref), channel_id=1, source_target_pairs={{496,0},{0,16},{16,32},{32,48},{48,64},{64,80},{80,96},{96,112},{1... | collective-permute-start | bytes 442376 | tf_op jit(solution)/shard_map/ppermute | solution.py:436
  8.9 9.7 %collective-permute-start.1 = (bf16[32,2304]{1,0:T(8,128)(2,1)}, bf16[32,2304]{1,0:T(8,128)(2,1)S(1)}, u32[]{:S(2)}, u32[]{:S(2)}) collective-permute-start(bf16[32,2304]{1,0:T(8,128)(2,1)} %shard_map.68.c_ref), channel_id=1, source_target_pairs={{16,0},{32,16},{48,32},{64,48},{80,64},{96,80},{112,96},{128,112},... | collective-permute-start | bytes 442376 | tf_op jit(solution)/shard_map/ppermute | solution.py:436
  18.6 0.9 copy-done.1
  19.5 0.6 shard_map.69
  20.1 2.7 %collective-permute-done.l_ref = bf16[32,2304]{1,0:T(8,128)(2,1)S(1)} collective-permute-done((bf16[32,2304]{1,0:T(8,128)(2,1)}, bf16[32,2304]{1,0:T(8,128)(2,1)S(1)}, u32[]{:S(2)}, u32[]{:S(2)}) %collective-permute-start) | collective-permute-done | bytes 147488 | tf_op jit(solution)/shard_map/ppermute | solution.py:436
  22.8 0.0 collective-permute-done.1.r_ref
  22.8 1.0 shard_map.70
  23.8 0.3 all_to_all.28
  24.0 0.0 copy-start
  24.0 18.9 %all_to_all.44 = bf16[16,2,10496]{2,1,0:T(2,128)(2,1)S(1)} all-to-all(bf16[16,2,10496]{2,1,0:T(2,128)(2,1)S(1)} %all_to_all.28), channel_id=1, replica_groups=mesh['cells'=32,'bands'=16] {'bands'}, dimensions={0} | all-to-all | bytes 1343488 | tf_op jit(solution)/shard_map/all_to_all | solution.py:469
  42.9 0.3 all_to_all.30.got
  43.2 0.0 copy-start.2
  43.2 2.8 %shard_map.71 = (bf16[32,2048]{1,0:T(8,128)(2,1)S(1)}, f32[8,3,32,256]{3,2,1,0:T(8,128)S(1)}) custom-call(bf16[32,10496]{1,0:T(8,128)(2,1)S(1)} %all_to_all.30.got, bf16[2320,256]{1,0:T(8,128)(2,1)S(1)} %copy-done), custom_call_target="tpu_custom_call" | custom-call | tf_op jit(solution)/shard_map/pallas_call | solution.py:422
  46.0 4.7 %collective-permute-start.2 = (bf16[32,2048]{1,0:T(8,128)(2,1)S(1)}, bf16[32,2048]{1,0:T(8,128)(2,1)S(1)}, u32[]{:S(2)}, u32[]{:S(2)}) collective-permute-start(bf16[32,2048]{1,0:T(8,128)(2,1)S(1)} %get-tuple-element.12.c_ref), channel_id=1, source_target_pairs={{496,0},{0,16},{16,32},{32,48},{48,64},{64,80},{80,96},{96,112},{1... | collective-permute-start | bytes 393224 | tf_op jit(solution)/shard_map/ppermute | solution.py:436
  50.7 6.1 %collective-permute-start.3 = (bf16[32,2048]{1,0:T(8,128)(2,1)S(1)}, bf16[32,2048]{1,0:T(8,128)(2,1)S(1)}, u32[]{:S(2)}, u32[]{:S(2)}) collective-permute-start(bf16[32,2048]{1,0:T(8,128)(2,1)S(1)} %get-tuple-element.12.c_ref), channel_id=1, source_target_pairs={{16,0},{32,16},{48,32},{64,48},{80,64},{96,80},{112,96},{128,112},... | collective-permute-start | bytes 393224 | tf_op jit(solution)/shard_map/ppermute | solution.py:436
  56.8 0.2 copy.10
  57.0 0.3 copy.8
  57.3 0.1 copy.11
  57.3 2.8 %collective-permute-done.2.l_ref = bf16[32,2048]{1,0:T(8,128)(2,1)S(1)} collective-permute-done((bf16[32,2048]{1,0:T(8,128)(2,1)S(1)}, bf16[32,2048]{1,0:T(8,128)(2,1)S(1)}, u32[]{:S(2)}, u32[]{:S(2)}) %collective-permute-start.2) | collective-permute-done | bytes 131104 | tf_op jit(solution)/shard_map/ppermute | solution.py:436
  60.1 1.5 %collective-permute-done.3.r_ref = bf16[32,2048]{1,0:T(8,128)(2,1)S(1)} collective-permute-done((bf16[32,2048]{1,0:T(8,128)(2,1)S(1)}, bf16[32,2048]{1,0:T(8,128)(2,1)S(1)}, u32[]{:S(2)}, u32[]{:S(2)}) %collective-permute-start.3) | collective-permute-done | bytes 131104 | tf_op jit(solution)/shard_map/ppermute | solution.py:436
  61.6 2.4 %shard_map.72 = bf16[32,6144]{1,0:T(8,128)(2,1)S(1)} custom-call(bf16[32,2048]{1,0:T(8,128)(2,1)S(1)} %get-tuple-element.12.c_ref, bf16[32,2048]{1,0:T(8,128)(2,1)S(1)} %collective-permute-done.2.l_ref, bf16[32,2048]{1,0:T(8,128)(2,1)S(1)} %collective-permute-done.3.r_ref, f32[8,3,32,256]{3,2,1,0:T(8,128)S(1)} %get-tuple-element.13.g_ref, ...), custom_call_target="tpu_custom_call" | custom-call | tf_op jit(solution)/shard_map/pallas_call | solution.py:422
  64.1 0.3 all_to_all.31
  64.3 12.2 %all_to_all.45 = bf16[16,2,6144]{2,1,0:T(2,128)(2,1)S(1)} all-to-all(bf16[16,2,6144]{2,1,0:T(2,128)(2,1)S(1)} %all_to_all.31), channel_id=1, replica_groups=mesh['cells'=32,'bands'=16] {'bands'}, dimensions={0} | all-to-all | bytes 786432 | tf_op jit(solution)/shard_map/all_to_all | solution.py:489
  76.5 0.1 all_to_all.33.got
  76.7 0.4 shard_map.73
  77.1 9.4 %all_to_all.46 = f32[16,2,128]{2,1,0:T(2,128)S(1)} all-to-all(f32[16,2,128]{2,1,0:T(2,128)S(1)} %bitcast.17), channel_id=1, replica_groups=mesh['cells'=32,'bands'=16] {'bands'}, dimensions={0} | all-to-all | bytes 32768 | tf_op jit(solution)/shard_map/all_to_all | solution.py:492
  86.5 0.6 shard_map.74
  87.1 9.8 %all-to-all-start.3 = ((f32[32,1,128]{2,1,0:T(1,128)}), f32[32,1,128]{2,1,0:T(1,128)S(1)}, u32[]{:S(2)}, u32[]{:S(2)}) async-start(f32[32,1,128]{2,1,0:T(1,128)} %bitcast.6), calls=%async_computation.3 | async-start | bytes 32768 | tf_op jit(solution)/shard_map/all_to_all | solution.py:494
  97.0 0.7 slice.4
  97.7 10.2 %all-to-all-done.3 = f32[32,1,128]{2,1,0:T(1,128)S(1)} async-done(((f32[32,1,128]{2,1,0:T(1,128)}), f32[32,1,128]{2,1,0:T(1,128)S(1)}, u32[]{:S(2)}, u32[]{:S(2)}) %all-to-all-start.3) | async-done | bytes 16416 | tf_op jit(solution)/shard_map/all_to_all | solution.py:494
  107.8 0.6 shard_map.75
  (3 shorter events, 0.0 us)
Async XLA Ops:
  2.3 20.5 %collective-permute-start = (bf16[32,2304]{1,0:T(8,128)(2,1)}, bf16[32,2304]{1,0:T(8,128)(2,1)S(1)}, u32[]{:S(2)}, u32[]{:S(2)}) collective-permute-start(bf16[32,2304]{1,0:T(8,128)(2,1)} %shard_map.68.c_ref), channel_id=1, source_target_pairs={{496,0},{0,16},{16,32},{32,48},{48,64},{64,80},{80,96},{96,112},{1... | collective-permute-start | bytes 442376 | tf_op jit(solution)/shard_map/ppermute | solution.py:436
  8.9 13.9 %collective-permute-start.1 = (bf16[32,2304]{1,0:T(8,128)(2,1)}, bf16[32,2304]{1,0:T(8,128)(2,1)S(1)}, u32[]{:S(2)}, u32[]{:S(2)}) collective-permute-start(bf16[32,2304]{1,0:T(8,128)(2,1)} %shard_map.68.c_ref), channel_id=1, source_target_pairs={{16,0},{32,16},{48,32},{64,48},{80,64},{96,80},{112,96},{128,112},... | collective-permute-start | bytes 442376 | tf_op jit(solution)/shard_map/ppermute | solution.py:436
  18.6 0.9 copy-start.1
  24.0 19.1 %copy-start = (bf16[2320,256]{1,0:T(8,128)(2,1)S(1)}, bf16[2320,256]{1,0:T(8,128)(2,1)}, u32[]{:S(2)}) copy-start(bf16[2320,256]{1,0:T(8,128)(2,1)} %constant.2.clone.w_ref) | copy-start | bytes 3563524
  43.2 13.6 %copy-start.2 = (bf16[4,32768]{1,0:T(4,128)(2,1)S(1)}, bf16[4,32768]{1,0:T(4,128)(2,1)}, u32[]{:S(2)}) copy-start(bf16[4,32768]{1,0:T(4,128)(2,1)} %param.6) | copy-start | bytes 786436
  46.0 14.1 %collective-permute-start.2 = (bf16[32,2048]{1,0:T(8,128)(2,1)S(1)}, bf16[32,2048]{1,0:T(8,128)(2,1)S(1)}, u32[]{:S(2)}, u32[]{:S(2)}) collective-permute-start(bf16[32,2048]{1,0:T(8,128)(2,1)S(1)} %get-tuple-element.12.c_ref), channel_id=1, source_target_pairs={{496,0},{0,16},{16,32},{32,48},{48,64},{64,80},{80,96},{96,112},{1... | collective-permute-start | bytes 393224 | tf_op jit(solution)/shard_map/ppermute | solution.py:436
  50.7 10.9 %collective-permute-start.3 = (bf16[32,2048]{1,0:T(8,128)(2,1)S(1)}, bf16[32,2048]{1,0:T(8,128)(2,1)S(1)}, u32[]{:S(2)}, u32[]{:S(2)}) collective-permute-start(bf16[32,2048]{1,0:T(8,128)(2,1)S(1)} %get-tuple-element.12.c_ref), channel_id=1, source_target_pairs={{16,0},{32,16},{48,32},{64,48},{80,64},{96,80},{112,96},{128,112},... | collective-permute-start | bytes 393224 | tf_op jit(solution)/shard_map/ppermute | solution.py:436
  87.1 20.7 %all-to-all-start.3 = ((f32[32,1,128]{2,1,0:T(1,128)}), f32[32,1,128]{2,1,0:T(1,128)S(1)}, u32[]{:S(2)}, u32[]{:S(2)}) async-start(f32[32,1,128]{2,1,0:T(1,128)} %bitcast.6), calls=%async_computation.3 | async-start | bytes 32768 | tf_op jit(solution)/shard_map/all_to_all | solution.py:494

commit v9 on v8

--- a/solution.py
+++ b/solution.py
@@ -395,12 +395,17 @@
     ]
     lane, row = iota((NWF, 128), 1), iota((NWF, 128), 0)
     both = jnp.where(((lane >> 5) & 1) == 0, parts[0], parts[1])
-    out_ref[...] = jnp.where((lane >> 6) == (row & 1), both * factor, 0.0)
+    both = jnp.where((lane >> 6) == (row & 1), both * factor, 0.0)
+    lane, row = iota((64, NWF), 1), iota((64, NWF), 0)
+    owner = jnp.where((row & 15) == (lane >> 1), 1.0, 0.0)
+    both = jnp.dot(owner, both, precision=lax.Precision.HIGHEST, preferred_element_type=jnp.float32)
+    out_ref[...] = jnp.where((iota((64, 128), 1) & 3) == (iota((64, 128), 0) >> 4), both, 0.0)
 
 
 def share_kernel(got, out_ref):
     total = jnp.sum(got[...], axis=0, keepdims=True)
-    out_ref[...] = jnp.where((iota((NWF, 128), 1) & 31) == iota((NWF, 128), 0), total, 0.0)
+    lane, row = iota((8, 128), 1), iota((8, 128), 0)
+    out_ref[...] = jnp.where(((lane & 31) >> 2) == row, total, 0.0)
 
 
 def total_kernel(got, out_ref):
@@ -488,10 +493,12 @@
     )
     got = lax.all_to_all(block, "bands", 0, 0, tiled=True)
     filtered = got[:, :NODES_DEV]
-    (partial,) = call(functools.partial(corr_kernel, factor), (got,), [shape((NWF, 128), f32)])
-    partial = lax.all_to_all(partial, "bands", 0, 0, tiled=True)
-    (partial,) = call(share_kernel, (partial,), [shape((NWF, 128), f32)])
-    partial = lax.all_to_all(partial, "cells", 0, 0, tiled=True)
+    (partial,) = call(functools.partial(corr_kernel, factor), (got,), [shape((64, 128), f32)])
+    planes = [list(range(at, at + 64)) for at in range(0, n_cells * n_bands, 64)]
+    columns = [list(range(at, n_cells, 4)) for at in range(4)]
+    partial = lax.all_to_all(partial, ("cells", "bands"), 0, 0, tiled=True, axis_index_groups=planes)
+    (partial,) = call(share_kernel, (partial,), [shape((8, 128), f32)])
+    partial = lax.all_to_all(partial, "cells", 0, 0, tiled=True, axis_index_groups=columns)
     (total,) = call(total_kernel, (partial,), [shape((1, 4), f32)])
     return (filtered, total.T)
 

time: 109 us -> 108 us (level)
  blocking collectives: 40.5 us -> 46.6 us
  waiting for transfers between devices: 17.1 us -> 12.8 us
  starting transfers between devices: 36.9 us -> 34 us
    all_to_all x1, blocking collectives: 9.42 us -> 15.6 us  [shards(): lax.all_to_all(partial, ('cells', 'bands'), 0, 0, tiled=True, axis_index_...]
    all_to_all x1, waiting for transfers between devices: 10.2 us -> 5.85 us  [shards(): lax.all_to_all(partial, 'cells', 0, 0, tiled=True, axis_index_groups=colu...]
    all_to_all x1, starting transfers between devices: 9.84 us -> 6.9 us  [shards(): lax.all_to_all(partial, 'cells', 0, 0, tiled=True, axis_index_groups=colu...]
where the time goes in v9:
time: 108 us
  blocking collectives  46.6 us (43%)
  starting transfers between devices  34 us (31%)
  waiting for transfers between devices  12.8 us (12%)
  Pallas kernels  10.3 us (10%)
  local copies, waits for them, and re-layouts  3.01 us (3%)
    ppermute x4, starting transfers between devices, passed_along(): return lax.ppermute(block, axis, route)  27.1 us
    all_to_all x1, blocking collectives, shards(): got = lax.all_to_all(payload, 'bands', 0, 0, tiled=True)  18.9 us
    all_to_all x1, blocking collectives, shards(): lax.all_to_all(partial, ('cells', 'bands'), 0, 0, tiled=True, axis_index_...  15.6 us
    all_to_all x1, blocking collectives, shards(): got = lax.all_to_all(block, 'bands', 0, 0, tiled=True)  12.2 us
    pallas_call x8, Pallas kernels, call(): pl.pallas_call(kernel, grid=(1,), in_specs=[full(a.shape) for a in args]...  10.3 us
    ppermute x4, waiting for transfers between devices, passed_along(): return lax.ppermute(block, axis, route)  6.98 us
    all_to_all x1, starting transfers between devices, shards(): lax.all_to_all(partial, 'cells', 0, 0, tiled=True, axis_index_groups=colu...  6.9 us
    all_to_all x1, waiting for transfers between devices, shards(): lax.all_to_all(partial, 'cells', 0, 0, tiled=True, axis_index_groups=colu...  5.85 us
  transfers between devices with their start and end apart: 5, of which 4 were waited for; matrix products, arithmetic and copies ran while one was open for 1% of the time, Pallas kernels for 1%

profile of v9, /device:TPU:1, one launch (start us, length us, event | category | flops | bytes accessed | tf_op | source)
XLA Modules:
  0.0 107.5 jit_solution(8810328095146194110)
XLA Ops:
  0.6 1.6 %shard_map.68.c_ref = bf16[32,2304]{1,0:T(8,128)(2,1)} custom-call(bf16[32,2048]{1,0:T(8,128)(2,1)} %v_hbm.1, f32[32,125]{1,0:T(8,128)} %bitcast.25, s32[32,125]{1,0:T(8,128)} %bitcast.26), custom_call_target="tpu_custom_call" | custom-call | tf_op jit(solution)/shard_map/pallas_call | solution.py:427
  2.3 6.6 %collective-permute-start = (bf16[32,2304]{1,0:T(8,128)(2,1)}, bf16[32,2304]{1,0:T(8,128)(2,1)S(1)}, u32[]{:S(2)}, u32[]{:S(2)}) collective-permute-start(bf16[32,2304]{1,0:T(8,128)(2,1)} %shard_map.68.c_ref), channel_id=1, source_target_pairs={{496,0},{0,16},{16,32},{32,48},{48,64},{64,80},{80,96},{96,112},{1... | collective-permute-start | bytes 442376 | tf_op jit(solution)/shard_map/ppermute | solution.py:441
  8.9 9.7 %collective-permute-start.1 = (bf16[32,2304]{1,0:T(8,128)(2,1)}, bf16[32,2304]{1,0:T(8,128)(2,1)S(1)}, u32[]{:S(2)}, u32[]{:S(2)}) collective-permute-start(bf16[32,2304]{1,0:T(8,128)(2,1)} %shard_map.68.c_ref), channel_id=1, source_target_pairs={{16,0},{32,16},{48,32},{64,48},{80,64},{96,80},{112,96},{128,112},... | collective-permute-start | bytes 442376 | tf_op jit(solution)/shard_map/ppermute | solution.py:441
  18.6 0.9 copy-done.1
  19.5 0.6 shard_map.69
  20.1 2.7 %collective-permute-done.l_ref = bf16[32,2304]{1,0:T(8,128)(2,1)S(1)} collective-permute-done((bf16[32,2304]{1,0:T(8,128)(2,1)}, bf16[32,2304]{1,0:T(8,128)(2,1)S(1)}, u32[]{:S(2)}, u32[]{:S(2)}) %collective-permute-start) | collective-permute-done | bytes 147488 | tf_op jit(solution)/shard_map/ppermute | solution.py:441
  22.8 0.0 collective-permute-done.1.r_ref
  22.8 1.0 shard_map.70
  23.8 0.3 all_to_all.28
  24.0 0.0 copy-start
  24.0 18.9 %all_to_all.44 = bf16[16,2,10496]{2,1,0:T(2,128)(2,1)S(1)} all-to-all(bf16[16,2,10496]{2,1,0:T(2,128)(2,1)S(1)} %all_to_all.28), channel_id=1, replica_groups=mesh['cells'=32,'bands'=16] {'bands'}, dimensions={0} | all-to-all | bytes 1343488 | tf_op jit(solution)/shard_map/all_to_all | solution.py:474
  42.9 0.3 all_to_all.30.got
  43.2 0.0 copy-start.2
  43.2 2.8 %shard_map.71 = (bf16[32,2048]{1,0:T(8,128)(2,1)S(1)}, f32[8,3,32,256]{3,2,1,0:T(8,128)S(1)}) custom-call(bf16[32,10496]{1,0:T(8,128)(2,1)S(1)} %all_to_all.30.got, bf16[2320,256]{1,0:T(8,128)(2,1)S(1)} %copy-done), custom_call_target="tpu_custom_call" | custom-call | tf_op jit(solution)/shard_map/pallas_call | solution.py:427
  46.0 4.7 %collective-permute-start.2 = (bf16[32,2048]{1,0:T(8,128)(2,1)S(1)}, bf16[32,2048]{1,0:T(8,128)(2,1)S(1)}, u32[]{:S(2)}, u32[]{:S(2)}) collective-permute-start(bf16[32,2048]{1,0:T(8,128)(2,1)S(1)} %get-tuple-element.12.c_ref), channel_id=1, source_target_pairs={{496,0},{0,16},{16,32},{32,48},{48,64},{64,80},{80,96},{96,112},{1... | collective-permute-start | bytes 393224 | tf_op jit(solution)/shard_map/ppermute | solution.py:441
  50.7 6.1 %collective-permute-start.3 = (bf16[32,2048]{1,0:T(8,128)(2,1)S(1)}, bf16[32,2048]{1,0:T(8,128)(2,1)S(1)}, u32[]{:S(2)}, u32[]{:S(2)}) collective-permute-start(bf16[32,2048]{1,0:T(8,128)(2,1)S(1)} %get-tuple-element.12.c_ref), channel_id=1, source_target_pairs={{16,0},{32,16},{48,32},{64,48},{80,64},{96,80},{112,96},{128,112},... | collective-permute-start | bytes 393224 | tf_op jit(solution)/shard_map/ppermute | solution.py:441
  56.8 0.2 copy.11
  57.0 0.3 copy.8
  57.3 0.1 copy.12
  57.3 2.8 %collective-permute-done.2.l_ref = bf16[32,2048]{1,0:T(8,128)(2,1)S(1)} collective-permute-done((bf16[32,2048]{1,0:T(8,128)(2,1)S(1)}, bf16[32,2048]{1,0:T(8,128)(2,1)S(1)}, u32[]{:S(2)}, u32[]{:S(2)}) %collective-permute-start.2) | collective-permute-done | bytes 131104 | tf_op jit(solution)/shard_map/ppermute | solution.py:441
  60.1 1.5 %collective-permute-done.3.r_ref = bf16[32,2048]{1,0:T(8,128)(2,1)S(1)} collective-permute-done((bf16[32,2048]{1,0:T(8,128)(2,1)S(1)}, bf16[32,2048]{1,0:T(8,128)(2,1)S(1)}, u32[]{:S(2)}, u32[]{:S(2)}) %collective-permute-start.3) | collective-permute-done | bytes 131104 | tf_op jit(solution)/shard_map/ppermute | solution.py:441
  61.6 2.4 %shard_map.72 = bf16[32,6144]{1,0:T(8,128)(2,1)S(1)} custom-call(bf16[32,2048]{1,0:T(8,128)(2,1)S(1)} %get-tuple-element.12.c_ref, bf16[32,2048]{1,0:T(8,128)(2,1)S(1)} %collective-permute-done.2.l_ref, bf16[32,2048]{1,0:T(8,128)(2,1)S(1)} %collective-permute-done.3.r_ref, f32[8,3,32,256]{3,2,1,0:T(8,128)S(1)} %get-tuple-element.13.g_ref, ...), custom_call_target="tpu_custom_call" | custom-call | tf_op jit(solution)/shard_map/pallas_call | solution.py:427
  64.1 0.3 all_to_all.31
  64.3 12.2 %all_to_all.45 = bf16[16,2,6144]{2,1,0:T(2,128)(2,1)S(1)} all-to-all(bf16[16,2,6144]{2,1,0:T(2,128)(2,1)S(1)} %all_to_all.31), channel_id=1, replica_groups=mesh['cells'=32,'bands'=16] {'bands'}, dimensions={0} | all-to-all | bytes 786432 | tf_op jit(solution)/shard_map/all_to_all | solution.py:494
  76.5 0.1 all_to_all.33.got
  76.7 0.6 shard_map.73
  77.3 15.6 %all_to_all.46 = f32[64,1,128]{2,1,0:T(1,128)S(1)} all-to-all(f32[64,1,128]{2,1,0:T(1,128)S(1)} %bitcast.20), channel_id=1, replica_groups={{0,1,2,3,4,5,6,7,8,9,10,11,12,13,14,15,16,17,18,19,20,21,22,23,24,25,26..., dimensions={0} | all-to-all | bytes 65536 | tf_op jit(solution)/shard_map/all_to_all | solution.py:499
  92.9 0.6 shard_map.74
  93.5 6.9 %all-to-all-start.3 = ((f32[8,1,128]{2,1,0:T(1,128)}), f32[8,1,128]{2,1,0:T(1,128)S(1)}, u32[]{:S(2)}, u32[]{:S(2)}) async-start(f32[8,1,128]{2,1,0:T(1,128)} %bitcast.7), calls=%async_computation.3 | async-start | bytes 8192 | tf_op jit(solution)/shard_map/all_to_all | solution.py:501
  100.4 0.7 slice.4
  101.1 5.9 %all-to-all-done.3 = f32[8,1,128]{2,1,0:T(1,128)S(1)} async-done(((f32[8,1,128]{2,1,0:T(1,128)}), f32[8,1,128]{2,1,0:T(1,128)S(1)}, u32[]{:S(2)}, u32[]{:S(2)}) %all-to-all-start.3) | async-done | bytes 4128 | tf_op jit(solution)/shard_map/all_to_all | solution.py:501
  106.9 0.6 shard_map.75
  (3 shorter events, 0.0 us)
Async XLA Ops:
  2.3 20.5 %collective-permute-start = (bf16[32,2304]{1,0:T(8,128)(2,1)}, bf16[32,2304]{1,0:T(8,128)(2,1)S(1)}, u32[]{:S(2)}, u32[]{:S(2)}) collective-permute-start(bf16[32,2304]{1,0:T(8,128)(2,1)} %shard_map.68.c_ref), channel_id=1, source_target_pairs={{496,0},{0,16},{16,32},{32,48},{48,64},{64,80},{80,96},{96,112},{1... | collective-permute-start | bytes 442376 | tf_op jit(solution)/shard_map/ppermute | solution.py:441
  8.9 13.9 %collective-permute-start.1 = (bf16[32,2304]{1,0:T(8,128)(2,1)}, bf16[32,2304]{1,0:T(8,128)(2,1)S(1)}, u32[]{:S(2)}, u32[]{:S(2)}) collective-permute-start(bf16[32,2304]{1,0:T(8,128)(2,1)} %shard_map.68.c_ref), channel_id=1, source_target_pairs={{16,0},{32,16},{48,32},{64,48},{80,64},{96,80},{112,96},{128,112},... | collective-permute-start | bytes 442376 | tf_op jit(solution)/shard_map/ppermute | solution.py:441
  18.6 0.9 copy-start.1
  24.0 19.1 %copy-start = (bf16[2320,256]{1,0:T(8,128)(2,1)S(1)}, bf16[2320,256]{1,0:T(8,128)(2,1)}, u32[]{:S(2)}) copy-start(bf16[2320,256]{1,0:T(8,128)(2,1)} %constant.2.clone.w_ref) | copy-start | bytes 3563524
  43.2 13.6 %copy-start.2 = (bf16[4,32768]{1,0:T(4,128)(2,1)S(1)}, bf16[4,32768]{1,0:T(4,128)(2,1)}, u32[]{:S(2)}) copy-start(bf16[4,32768]{1,0:T(4,128)(2,1)} %param.6) | copy-start | bytes 786436
  46.0 14.1 %collective-permute-start.2 = (bf16[32,2048]{1,0:T(8,128)(2,1)S(1)}, bf16[32,2048]{1,0:T(8,128)(2,1)S(1)}, u32[]{:S(2)}, u32[]{:S(2)}) collective-permute-start(bf16[32,2048]{1,0:T(8,128)(2,1)S(1)} %get-tuple-element.12.c_ref), channel_id=1, source_target_pairs={{496,0},{0,16},{16,32},{32,48},{48,64},{64,80},{80,96},{96,112},{1... | collective-permute-start | bytes 393224 | tf_op jit(solution)/shard_map/ppermute | solution.py:441
  50.7 10.9 %collective-permute-start.3 = (bf16[32,2048]{1,0:T(8,128)(2,1)S(1)}, bf16[32,2048]{1,0:T(8,128)(2,1)S(1)}, u32[]{:S(2)}, u32[]{:S(2)}) collective-permute-start(bf16[32,2048]{1,0:T(8,128)(2,1)S(1)} %get-tuple-element.12.c_ref), channel_id=1, source_target_pairs={{16,0},{32,16},{48,32},{64,48},{80,64},{96,80},{112,96},{128,112},... | collective-permute-start | bytes 393224 | tf_op jit(solution)/shard_map/ppermute | solution.py:441
  93.5 13.4 %all-to-all-start.3 = ((f32[8,1,128]{2,1,0:T(1,128)}), f32[8,1,128]{2,1,0:T(1,128)S(1)}, u32[]{:S(2)}, u32[]{:S(2)}) async-start(f32[8,1,128]{2,1,0:T(1,128)} %bitcast.7), calls=%async_computation.3 | async-start | bytes 8192 | tf_op jit(solution)/shard_map/all_to_all | solution.py:501

commit v10 on v9

--- a/solution.py
+++ b/solution.py
@@ -382,7 +382,7 @@
     filter_step((l_ref, c_ref, r_ref), w_ref, g_ref, out_ref, here, there, half)
 
 
-def corr_kernel(factor, got, out_ref):
+def corr_kernel(factor, got, out_ref, pairs):
     four = jnp.concatenate([got[:, :NODES_DEV]] * 4, axis=0)
     parts = [
         lax.dot_general(
@@ -396,9 +396,9 @@
     lane, row = iota((NWF, 128), 1), iota((NWF, 128), 0)
     both = jnp.where(((lane >> 5) & 1) == 0, parts[0], parts[1])
     both = jnp.where((lane >> 6) == (row & 1), both * factor, 0.0)
-    lane, row = iota((64, NWF), 1), iota((64, NWF), 0)
-    owner = jnp.where((row & 15) == (lane >> 1), 1.0, 0.0)
-    both = jnp.dot(owner, both, precision=lax.Precision.HIGHEST, preferred_element_type=jnp.float32)
+    pairs[...] = both + pltpu.roll(both, NWF - 1, 0)
+    even = pairs[pl.ds(0, 16, stride=2), :]
+    both = jnp.concatenate([even] * 4, axis=0)
     out_ref[...] = jnp.where((iota((64, 128), 1) & 3) == (iota((64, 128), 0) >> 4), both, 0.0)
 
 
@@ -493,7 +493,12 @@
     )
     got = lax.all_to_all(block, "bands", 0, 0, tiled=True)
     filtered = got[:, :NODES_DEV]
-    (partial,) = call(functools.partial(corr_kernel, factor), (got,), [shape((64, 128), f32)])
+    (partial,) = call(
+        functools.partial(corr_kernel, factor),
+        (got,),
+        [shape((64, 128), f32)],
+        [pltpu.VMEM((NWF, 128), f32)],
+    )
     planes = [list(range(at, at + 64)) for at in range(0, n_cells * n_bands, 64)]
     columns = [list(range(at, n_cells, 4)) for at in range(4)]
     partial = lax.all_to_all(partial, ("cells", "bands"), 0, 0, tiled=True, axis_index_groups=planes)

time: 108 us -> 108 us (level)
  no operation moved by 1% of the time
where the time goes in v10:
time: 108 us; the launch traced here: 107 us
  blocking collectives  46.6 us (43%)
  starting transfers between devices  34 us (31%)
  waiting for transfers between devices  12.8 us (12%)
  Pallas kernels  10.1 us (9%)
  local copies, waits for them, and re-layouts  3.01 us (3%)
    ppermute x4, starting transfers between devices, passed_along(): return lax.ppermute(block, axis, route)  27.1 us
    all_to_all x1, blocking collectives, shards(): got = lax.all_to_all(payload, 'bands', 0, 0, tiled=True)  18.9 us
    all_to_all x1, blocking collectives, shards(): lax.all_to_all(partial, ('cells', 'bands'), 0, 0, tiled=True, axis_index_...  15.6 us
    all_to_all x1, blocking collectives, shards(): got = lax.all_to_all(block, 'bands', 0, 0, tiled=True)  12.2 us
    pallas_call x8, Pallas kernels, call(): pl.pallas_call(kernel, grid=(1,), in_specs=[full(a.shape) for a in args]...  10.1 us
    ppermute x4, waiting for transfers between devices, passed_along(): return lax.ppermute(block, axis, route)  6.98 us
    all_to_all x1, starting transfers between devices, shards(): lax.all_to_all(partial, 'cells', 0, 0, tiled=True, axis_index_groups=colu...  6.9 us
    all_to_all x1, waiting for transfers between devices, shards(): lax.all_to_all(partial, 'cells', 0, 0, tiled=True, axis_index_groups=colu...  5.85 us
  transfers between devices with their start and end apart: 5, of which 4 were waited for; matrix products, arithmetic and copies ran while one was open for 1% of the time, Pallas kernels for 1%

profile of v10, /device:TPU:1, one launch (start us, length us, event | category | flops | bytes accessed | tf_op | source)
XLA Modules:
  0.0 107.3 jit_solution(14230023229945150620)
XLA Ops:
  0.6 1.6 %shard_map.68.c_ref = bf16[32,2304]{1,0:T(8,128)(2,1)} custom-call(bf16[32,2048]{1,0:T(8,128)(2,1)} %v_hbm.1, f32[32,125]{1,0:T(8,128)} %bitcast.25, s32[32,125]{1,0:T(8,128)} %bitcast.26), custom_call_target="tpu_custom_call" | custom-call | tf_op jit(solution)/shard_map/pallas_call | solution.py:427
  2.3 6.6 %collective-permute-start = (bf16[32,2304]{1,0:T(8,128)(2,1)}, bf16[32,2304]{1,0:T(8,128)(2,1)S(1)}, u32[]{:S(2)}, u32[]{:S(2)}) collective-permute-start(bf16[32,2304]{1,0:T(8,128)(2,1)} %shard_map.68.c_ref), channel_id=1, source_target_pairs={{496,0},{0,16},{16,32},{32,48},{48,64},{64,80},{80,96},{96,112},{1... | collective-permute-start | bytes 442376 | tf_op jit(solution)/shard_map/ppermute | solution.py:441
  8.9 9.7 %collective-permute-start.1 = (bf16[32,2304]{1,0:T(8,128)(2,1)}, bf16[32,2304]{1,0:T(8,128)(2,1)S(1)}, u32[]{:S(2)}, u32[]{:S(2)}) collective-permute-start(bf16[32,2304]{1,0:T(8,128)(2,1)} %shard_map.68.c_ref), channel_id=1, source_target_pairs={{16,0},{32,16},{48,32},{64,48},{80,64},{96,80},{112,96},{128,112},... | collective-permute-start | bytes 442376 | tf_op jit(solution)/shard_map/ppermute | solution.py:441
  18.6 0.9 copy-done.1
  19.5 0.6 shard_map.69
  20.1 2.7 %collective-permute-done.l_ref = bf16[32,2304]{1,0:T(8,128)(2,1)S(1)} collective-permute-done((bf16[32,2304]{1,0:T(8,128)(2,1)}, bf16[32,2304]{1,0:T(8,128)(2,1)S(1)}, u32[]{:S(2)}, u32[]{:S(2)}) %collective-permute-start) | collective-permute-done | bytes 147488 | tf_op jit(solution)/shard_map/ppermute | solution.py:441
  22.8 0.0 collective-permute-done.1.r_ref
  22.8 1.0 shard_map.70
  23.8 0.3 all_to_all.28
  24.0 0.0 copy-start
  24.0 18.9 %all_to_all.44 = bf16[16,2,10496]{2,1,0:T(2,128)(2,1)S(1)} all-to-all(bf16[16,2,10496]{2,1,0:T(2,128)(2,1)S(1)} %all_to_all.28), channel_id=1, replica_groups=mesh['cells'=32,'bands'=16] {'bands'}, dimensions={0} | all-to-all | bytes 1343488 | tf_op jit(solution)/shard_map/all_to_all | solution.py:474
  42.9 0.3 all_to_all.30.got
  43.2 0.0 copy-start.2
  43.2 2.8 %shard_map.71 = (bf16[32,2048]{1,0:T(8,128)(2,1)S(1)}, f32[8,3,32,256]{3,2,1,0:T(8,128)S(1)}) custom-call(bf16[32,10496]{1,0:T(8,128)(2,1)S(1)} %all_to_all.30.got, bf16[2320,256]{1,0:T(8,128)(2,1)S(1)} %copy-done), custom_call_target="tpu_custom_call" | custom-call | tf_op jit(solution)/shard_map/pallas_call | solution.py:427
  46.0 4.7 %collective-permute-start.2 = (bf16[32,2048]{1,0:T(8,128)(2,1)S(1)}, bf16[32,2048]{1,0:T(8,128)(2,1)S(1)}, u32[]{:S(2)}, u32[]{:S(2)}) collective-permute-start(bf16[32,2048]{1,0:T(8,128)(2,1)S(1)} %get-tuple-element.12.c_ref), channel_id=1, source_target_pairs={{496,0},{0,16},{16,32},{32,48},{48,64},{64,80},{80,96},{96,112},{1... | collective-permute-start | bytes 393224 | tf_op jit(solution)/shard_map/ppermute | solution.py:441
  50.7 6.1 %collective-permute-start.3 = (bf16[32,2048]{1,0:T(8,128)(2,1)S(1)}, bf16[32,2048]{1,0:T(8,128)(2,1)S(1)}, u32[]{:S(2)}, u32[]{:S(2)}) collective-permute-start(bf16[32,2048]{1,0:T(8,128)(2,1)S(1)} %get-tuple-element.12.c_ref), channel_id=1, source_target_pairs={{16,0},{32,16},{48,32},{64,48},{80,64},{96,80},{112,96},{128,112},... | collective-permute-start | bytes 393224 | tf_op jit(solution)/shard_map/ppermute | solution.py:441
  56.8 0.2 copy.11
  57.0 0.3 copy.8
  57.3 0.1 copy.12
  57.3 2.8 %collective-permute-done.2.l_ref = bf16[32,2048]{1,0:T(8,128)(2,1)S(1)} collective-permute-done((bf16[32,2048]{1,0:T(8,128)(2,1)S(1)}, bf16[32,2048]{1,0:T(8,128)(2,1)S(1)}, u32[]{:S(2)}, u32[]{:S(2)}) %collective-permute-start.2) | collective-permute-done | bytes 131104 | tf_op jit(solution)/shard_map/ppermute | solution.py:441
  60.1 1.5 %collective-permute-done.3.r_ref = bf16[32,2048]{1,0:T(8,128)(2,1)S(1)} collective-permute-done((bf16[32,2048]{1,0:T(8,128)(2,1)S(1)}, bf16[32,2048]{1,0:T(8,128)(2,1)S(1)}, u32[]{:S(2)}, u32[]{:S(2)}) %collective-permute-start.3) | collective-permute-done | bytes 131104 | tf_op jit(solution)/shard_map/ppermute | solution.py:441
  61.6 2.4 %shard_map.72 = bf16[32,6144]{1,0:T(8,128)(2,1)S(1)} custom-call(bf16[32,2048]{1,0:T(8,128)(2,1)S(1)} %get-tuple-element.12.c_ref, bf16[32,2048]{1,0:T(8,128)(2,1)S(1)} %collective-permute-done.2.l_ref, bf16[32,2048]{1,0:T(8,128)(2,1)S(1)} %collective-permute-done.3.r_ref, f32[8,3,32,256]{3,2,1,0:T(8,128)S(1)} %get-tuple-element.13.g_ref, ...), custom_call_target="tpu_custom_call" | custom-call | tf_op jit(solution)/shard_map/pallas_call | solution.py:427
  64.1 0.3 all_to_all.31
  64.3 12.2 %all_to_all.45 = bf16[16,2,6144]{2,1,0:T(2,128)(2,1)S(1)} all-to-all(bf16[16,2,6144]{2,1,0:T(2,128)(2,1)S(1)} %all_to_all.31), channel_id=1, replica_groups=mesh['cells'=32,'bands'=16] {'bands'}, dimensions={0} | all-to-all | bytes 786432 | tf_op jit(solution)/shard_map/all_to_all | solution.py:494
  76.5 0.1 all_to_all.33.got
  76.7 0.4 shard_map.73
  77.1 15.6 %all_to_all.46 = f32[64,1,128]{2,1,0:T(1,128)S(1)} all-to-all(f32[64,1,128]{2,1,0:T(1,128)S(1)} %bitcast.20), channel_id=1, replica_groups={{0,1,2,3,4,5,6,7,8,9,10,11,12,13,14,15,16,17,18,19,20,21,22,23,24,25,26..., dimensions={0} | all-to-all | bytes 65536 | tf_op jit(solution)/shard_map/all_to_all | solution.py:504
  92.7 0.6 shard_map.74
  93.3 6.9 %all-to-all-start.3 = ((f32[8,1,128]{2,1,0:T(1,128)}), f32[8,1,128]{2,1,0:T(1,128)S(1)}, u32[]{:S(2)}, u32[]{:S(2)}) async-start(f32[8,1,128]{2,1,0:T(1,128)} %bitcast.7), calls=%async_computation.3 | async-start | bytes 8192 | tf_op jit(solution)/shard_map/all_to_all | solution.py:506
  100.2 0.7 slice.4
  100.9 5.9 %all-to-all-done.3 = f32[8,1,128]{2,1,0:T(1,128)S(1)} async-done(((f32[8,1,128]{2,1,0:T(1,128)}), f32[8,1,128]{2,1,0:T(1,128)S(1)}, u32[]{:S(2)}, u32[]{:S(2)}) %all-to-all-start.3) | async-done | bytes 4128 | tf_op jit(solution)/shard_map/all_to_all | solution.py:506
  106.7 0.6 shard_map.75
  (3 shorter events, 0.0 us)
Async XLA Ops:
  2.3 20.5 %collective-permute-start = (bf16[32,2304]{1,0:T(8,128)(2,1)}, bf16[32,2304]{1,0:T(8,128)(2,1)S(1)}, u32[]{:S(2)}, u32[]{:S(2)}) collective-permute-start(bf16[32,2304]{1,0:T(8,128)(2,1)} %shard_map.68.c_ref), channel_id=1, source_target_pairs={{496,0},{0,16},{16,32},{32,48},{48,64},{64,80},{80,96},{96,112},{1... | collective-permute-start | bytes 442376 | tf_op jit(solution)/shard_map/ppermute | solution.py:441
  8.9 13.9 %collective-permute-start.1 = (bf16[32,2304]{1,0:T(8,128)(2,1)}, bf16[32,2304]{1,0:T(8,128)(2,1)S(1)}, u32[]{:S(2)}, u32[]{:S(2)}) collective-permute-start(bf16[32,2304]{1,0:T(8,128)(2,1)} %shard_map.68.c_ref), channel_id=1, source_target_pairs={{16,0},{32,16},{48,32},{64,48},{80,64},{96,80},{112,96},{128,112},... | collective-permute-start | bytes 442376 | tf_op jit(solution)/shard_map/ppermute | solution.py:441
  18.6 0.9 copy-start.1
  24.0 19.1 %copy-start = (bf16[2320,256]{1,0:T(8,128)(2,1)S(1)}, bf16[2320,256]{1,0:T(8,128)(2,1)}, u32[]{:S(2)}) copy-start(bf16[2320,256]{1,0:T(8,128)(2,1)} %constant.2.clone.w_ref) | copy-start | bytes 3563524
  43.2 13.6 %copy-start.2 = (bf16[4,32768]{1,0:T(4,128)(2,1)S(1)}, bf16[4,32768]{1,0:T(4,128)(2,1)}, u32[]{:S(2)}) copy-start(bf16[4,32768]{1,0:T(4,128)(2,1)} %param.6) | copy-start | bytes 786436
  46.0 14.1 %collective-permute-start.2 = (bf16[32,2048]{1,0:T(8,128)(2,1)S(1)}, bf16[32,2048]{1,0:T(8,128)(2,1)S(1)}, u32[]{:S(2)}, u32[]{:S(2)}) collective-permute-start(bf16[32,2048]{1,0:T(8,128)(2,1)S(1)} %get-tuple-element.12.c_ref), channel_id=1, source_target_pairs={{496,0},{0,16},{16,32},{32,48},{48,64},{64,80},{80,96},{96,112},{1... | collective-permute-start | bytes 393224 | tf_op jit(solution)/shard_map/ppermute | solution.py:441
  50.7 10.9 %collective-permute-start.3 = (bf16[32,2048]{1,0:T(8,128)(2,1)S(1)}, bf16[32,2048]{1,0:T(8,128)(2,1)S(1)}, u32[]{:S(2)}, u32[]{:S(2)}) collective-permute-start(bf16[32,2048]{1,0:T(8,128)(2,1)S(1)} %get-tuple-element.12.c_ref), channel_id=1, source_target_pairs={{16,0},{32,16},{48,32},{64,48},{80,64},{96,80},{112,96},{128,112},... | collective-permute-start | bytes 393224 | tf_op jit(solution)/shard_map/ppermute | solution.py:441
  93.3 13.4 %all-to-all-start.3 = ((f32[8,1,128]{2,1,0:T(1,128)}), f32[8,1,128]{2,1,0:T(1,128)S(1)}, u32[]{:S(2)}, u32[]{:S(2)}) async-start(f32[8,1,128]{2,1,0:T(1,128)} %bitcast.7), calls=%async_computation.3 | async-start | bytes 8192 | tf_op jit(solution)/shard_map/all_to_all | solution.py:506

commit v11 on v10

--- a/solution.py
+++ b/solution.py
@@ -382,7 +382,7 @@
     filter_step((l_ref, c_ref, r_ref), w_ref, g_ref, out_ref, here, there, half)
 
 
-def corr_kernel(factor, got, out_ref, pairs):
+def corr_kernel(factor, got, out_ref, pairs, joined):
     four = jnp.concatenate([got[:, :NODES_DEV]] * 4, axis=0)
     parts = [
         lax.dot_general(
@@ -397,15 +397,21 @@
     both = jnp.where(((lane >> 5) & 1) == 0, parts[0], parts[1])
     both = jnp.where((lane >> 6) == (row & 1), both * factor, 0.0)
     pairs[...] = both + pltpu.roll(both, NWF - 1, 0)
-    even = pairs[pl.ds(0, 16, stride=2), :]
-    both = jnp.concatenate([even] * 4, axis=0)
+    for low in range(4):
+        joined[4 * low : 4 * (low + 1), :] = pairs[pl.ds(2 * low, 4, stride=8), :]
+    both = jnp.concatenate([joined[...]] * 4, axis=0)
     out_ref[...] = jnp.where((iota((64, 128), 1) & 3) == (iota((64, 128), 0) >> 4), both, 0.0)
 
 
 def share_kernel(got, out_ref):
-    total = jnp.sum(got[...], axis=0, keepdims=True)
+    total = got[0:8, :]
+    for tile in range(1, 8):
+        total = total + got[8 * tile : 8 * (tile + 1), :]
+    total = total + pltpu.roll(total, 4, 0)
     lane, row = iota((8, 128), 1), iota((8, 128), 0)
-    out_ref[...] = jnp.where(((lane & 31) >> 2) == row, total, 0.0)
+    mine = ((lane & 31) >> 2) == row
+    for x in range(4):
+        out_ref[8 * x : 8 * (x + 1), :] = jnp.where(mine, total[x : x + 1, :], 0.0)
 
 
 def total_kernel(got, out_ref):
@@ -497,13 +503,16 @@
         functools.partial(corr_kernel, factor),
         (got,),
         [shape((64, 128), f32)],
-        [pltpu.VMEM((NWF, 128), f32)],
-    )
-    planes = [list(range(at, at + 64)) for at in range(0, n_cells * n_bands, 64)]
-    columns = [list(range(at, n_cells, 4)) for at in range(4)]
-    partial = lax.all_to_all(partial, ("cells", "bands"), 0, 0, tiled=True, axis_index_groups=planes)
-    (partial,) = call(share_kernel, (partial,), [shape((8, 128), f32)])
-    partial = lax.all_to_all(partial, "cells", 0, 0, tiled=True, axis_index_groups=columns)
+        [pltpu.VMEM((NWF, 128), f32), pltpu.VMEM((16, 128), f32)],
+    )
+    n_y = n_cells // 4
+    device = [[[[(4 * y + z) * n_bands + 4 * x + low for low in range(4)] for z in range(4)] for x in range(4)] for y in range(n_y)]
+    lines = [[device[y][x][z][low] for z in range(4) for low in range(4)] for y in range(n_y) for x in range(4)]
+    across = [[device[y][x][z][low] for x in range(4) for y in range(n_y)] for z in range(4) for low in range(4)]
+    both = ("cells", "bands")
+    partial = lax.all_to_all(partial, both, 0, 0, tiled=True, axis_index_groups=lines)
+    (partial,) = call(share_kernel, (partial,), [shape((32, 128), f32)])
+    partial = lax.all_to_all(partial, both, 0, 0, tiled=True, axis_index_groups=across)
     (total,) = call(total_kernel, (partial,), [shape((1, 4), f32)])
     return (filtered, total.T)
 

time: 108 us -> 108 us (level)
  blocking collectives: 46.6 us -> 43.8 us
  waiting for transfers between devices: 12.8 us -> 14.9 us
    all_to_all x1, blocking collectives: 15.6 us -> 12.8 us  [shards(): lax.all_to_all(partial, both, 0, 0, tiled=True, axis_index_groups=lines)]
    all_to_all x1, waiting for transfers between devices: 5.85 us -> 7.97 us  [shards(): lax.all_to_all(partial, both, 0, 0, tiled=True, axis_index_groups=across)]
where the time goes in v11:
time: 108 us; the launch traced here: 107 us
  blocking collectives  43.8 us (41%)
  starting transfers between devices  34.6 us (32%)
  waiting for transfers between devices  14.9 us (14%)
  Pallas kernels  10.1 us (9%)
  local copies, waits for them, and re-layouts  3.01 us (3%)
    ppermute x4, starting transfers between devices, passed_along(): return lax.ppermute(block, axis, route)  27.1 us
    all_to_all x1, blocking collectives, shards(): got = lax.all_to_all(payload, 'bands', 0, 0, tiled=True)  18.9 us
    all_to_all x1, blocking collectives, shards(): lax.all_to_all(partial, both, 0, 0, tiled=True, axis_index_groups=lines)  12.8 us
    all_to_all x1, blocking collectives, shards(): got = lax.all_to_all(block, 'bands', 0, 0, tiled=True)  12.2 us
    pallas_call x8, Pallas kernels, call(): pl.pallas_call(kernel, grid=(1,), in_specs=[full(a.shape) for a in args]...  10.1 us
    all_to_all x1, waiting for transfers between devices, shards(): lax.all_to_all(partial, both, 0, 0, tiled=True, axis_index_groups=across)  7.97 us
    all_to_all x1, starting transfers between devices, shards(): lax.all_to_all(partial, both, 0, 0, tiled=True, axis_index_groups=across)  7.55 us
    ppermute x4, waiting for transfers between devices, passed_along(): return lax.ppermute(block, axis, route)  6.98 us
  transfers between devices with their start and end apart: 5, of which 4 were waited for; matrix products, arithmetic and copies ran while one was open for 1% of the time, Pallas kernels for 1%

profile of v11, /device:TPU:1, one launch (start us, length us, event | category | flops | bytes accessed | tf_op | source)
XLA Modules:
  0.0 107.3 jit_solution(10288590315753124003)
XLA Ops:
  0.6 1.6 %shard_map.68.c_ref = bf16[32,2304]{1,0:T(8,128)(2,1)} custom-call(bf16[32,2048]{1,0:T(8,128)(2,1)} %v_hbm.1, f32[32,125]{1,0:T(8,128)} %bitcast.23, s32[32,125]{1,0:T(8,128)} %bitcast.24), custom_call_target="tpu_custom_call" | custom-call | tf_op jit(solution)/shard_map/pallas_call | solution.py:433
  2.3 6.6 %collective-permute-start = (bf16[32,2304]{1,0:T(8,128)(2,1)}, bf16[32,2304]{1,0:T(8,128)(2,1)S(1)}, u32[]{:S(2)}, u32[]{:S(2)}) collective-permute-start(bf16[32,2304]{1,0:T(8,128)(2,1)} %shard_map.68.c_ref), channel_id=1, source_target_pairs={{496,0},{0,16},{16,32},{32,48},{48,64},{64,80},{80,96},{96,112},{1... | collective-permute-start | bytes 442376 | tf_op jit(solution)/shard_map/ppermute | solution.py:447
  8.9 9.7 %collective-permute-start.1 = (bf16[32,2304]{1,0:T(8,128)(2,1)}, bf16[32,2304]{1,0:T(8,128)(2,1)S(1)}, u32[]{:S(2)}, u32[]{:S(2)}) collective-permute-start(bf16[32,2304]{1,0:T(8,128)(2,1)} %shard_map.68.c_ref), channel_id=1, source_target_pairs={{16,0},{32,16},{48,32},{64,48},{80,64},{96,80},{112,96},{128,112},... | collective-permute-start | bytes 442376 | tf_op jit(solution)/shard_map/ppermute | solution.py:447
  18.6 0.9 copy-done.1
  19.5 0.6 shard_map.69
  20.1 2.7 %collective-permute-done.l_ref = bf16[32,2304]{1,0:T(8,128)(2,1)S(1)} collective-permute-done((bf16[32,2304]{1,0:T(8,128)(2,1)}, bf16[32,2304]{1,0:T(8,128)(2,1)S(1)}, u32[]{:S(2)}, u32[]{:S(2)}) %collective-permute-start) | collective-permute-done | bytes 147488 | tf_op jit(solution)/shard_map/ppermute | solution.py:447
  22.8 0.0 collective-permute-done.1.r_ref
  22.8 1.0 shard_map.70
  23.8 0.3 all_to_all.28
  24.0 0.0 copy-start
  24.0 18.9 %all_to_all.44 = bf16[16,2,10496]{2,1,0:T(2,128)(2,1)S(1)} all-to-all(bf16[16,2,10496]{2,1,0:T(2,128)(2,1)S(1)} %all_to_all.28), channel_id=1, replica_groups=mesh['cells'=32,'bands'=16] {'bands'}, dimensions={0} | all-to-all | bytes 1343488 | tf_op jit(solution)/shard_map/all_to_all | solution.py:480
  42.9 0.3 all_to_all.30.got
  43.2 0.0 copy-start.2
  43.2 2.8 %shard_map.71 = (bf16[32,2048]{1,0:T(8,128)(2,1)S(1)}, f32[8,3,32,256]{3,2,1,0:T(8,128)S(1)}) custom-call(bf16[32,10496]{1,0:T(8,128)(2,1)S(1)} %all_to_all.30.got, bf16[2320,256]{1,0:T(8,128)(2,1)S(1)} %copy-done), custom_call_target="tpu_custom_call" | custom-call | tf_op jit(solution)/shard_map/pallas_call | solution.py:433
  46.0 4.7 %collective-permute-start.2 = (bf16[32,2048]{1,0:T(8,128)(2,1)S(1)}, bf16[32,2048]{1,0:T(8,128)(2,1)S(1)}, u32[]{:S(2)}, u32[]{:S(2)}) collective-permute-start(bf16[32,2048]{1,0:T(8,128)(2,1)S(1)} %get-tuple-element.12.c_ref), channel_id=1, source_target_pairs={{496,0},{0,16},{16,32},{32,48},{48,64},{64,80},{80,96},{96,112},{1... | collective-permute-start | bytes 393224 | tf_op jit(solution)/shard_map/ppermute | solution.py:447
  50.7 6.1 %collective-permute-start.3 = (bf16[32,2048]{1,0:T(8,128)(2,1)S(1)}, bf16[32,2048]{1,0:T(8,128)(2,1)S(1)}, u32[]{:S(2)}, u32[]{:S(2)}) collective-permute-start(bf16[32,2048]{1,0:T(8,128)(2,1)S(1)} %get-tuple-element.12.c_ref), channel_id=1, source_target_pairs={{16,0},{32,16},{48,32},{64,48},{80,64},{96,80},{112,96},{128,112},... | collective-permute-start | bytes 393224 | tf_op jit(solution)/shard_map/ppermute | solution.py:447
  56.8 0.2 copy.10
  57.0 0.3 copy.8
  57.3 0.1 copy.11
  57.3 2.8 %collective-permute-done.2.l_ref = bf16[32,2048]{1,0:T(8,128)(2,1)S(1)} collective-permute-done((bf16[32,2048]{1,0:T(8,128)(2,1)S(1)}, bf16[32,2048]{1,0:T(8,128)(2,1)S(1)}, u32[]{:S(2)}, u32[]{:S(2)}) %collective-permute-start.2) | collective-permute-done | bytes 131104 | tf_op jit(solution)/shard_map/ppermute | solution.py:447
  60.1 1.5 %collective-permute-done.3.r_ref = bf16[32,2048]{1,0:T(8,128)(2,1)S(1)} collective-permute-done((bf16[32,2048]{1,0:T(8,128)(2,1)S(1)}, bf16[32,2048]{1,0:T(8,128)(2,1)S(1)}, u32[]{:S(2)}, u32[]{:S(2)}) %collective-permute-start.3) | collective-permute-done | bytes 131104 | tf_op jit(solution)/shard_map/ppermute | solution.py:447
  61.6 2.4 %shard_map.72 = bf16[32,6144]{1,0:T(8,128)(2,1)S(1)} custom-call(bf16[32,2048]{1,0:T(8,128)(2,1)S(1)} %get-tuple-element.12.c_ref, bf16[32,2048]{1,0:T(8,128)(2,1)S(1)} %collective-permute-done.2.l_ref, bf16[32,2048]{1,0:T(8,128)(2,1)S(1)} %collective-permute-done.3.r_ref, f32[8,3,32,256]{3,2,1,0:T(8,128)S(1)} %get-tuple-element.13.g_ref, ...), custom_call_target="tpu_custom_call" | custom-call | tf_op jit(solution)/shard_map/pallas_call | solution.py:433
  64.1 0.3 all_to_all.31
  64.3 12.2 %all_to_all.45 = bf16[16,2,6144]{2,1,0:T(2,128)(2,1)S(1)} all-to-all(bf16[16,2,6144]{2,1,0:T(2,128)(2,1)S(1)} %all_to_all.31), channel_id=1, replica_groups=mesh['cells'=32,'bands'=16] {'bands'}, dimensions={0} | all-to-all | bytes 786432 | tf_op jit(solution)/shard_map/all_to_all | solution.py:500
  76.5 0.1 all_to_all.33.got
  76.7 0.5 shard_map.73
  77.1 12.8 %all_to_all.46 = f32[16,4,128]{2,1,0:T(4,128)S(1)} all-to-all(f32[16,4,128]{2,1,0:T(4,128)S(1)} %bitcast.18), channel_id=1, replica_groups={{0,1,2,3,16,17,18,19,32,33,34,35,48,49,50,51},{4,5,6,7,20,21,22,23,36,3..., dimensions={0} | all-to-all | bytes 65536 | tf_op jit(solution)/shard_map/all_to_all | solution.py:513
  89.9 0.6 shard_map.74
  90.5 7.6 %all-to-all-start.3 = ((f32[32,1,128]{2,1,0:T(1,128)}), f32[32,1,128]{2,1,0:T(1,128)S(1)}, u32[]{:S(2)}, u32[]{:S(2)}) async-start(f32[32,1,128]{2,1,0:T(1,128)} %bitcast.6), calls=%async_computation.3 | async-start | bytes 32768 | tf_op jit(solution)/shard_map/all_to_all | solution.py:515
  98.1 0.7 slice.4
  98.8 8.0 %all-to-all-done.3 = f32[32,1,128]{2,1,0:T(1,128)S(1)} async-done(((f32[32,1,128]{2,1,0:T(1,128)}), f32[32,1,128]{2,1,0:T(1,128)S(1)}, u32[]{:S(2)}, u32[]{:S(2)}) %all-to-all-start.3) | async-done | bytes 16416 | tf_op jit(solution)/shard_map/all_to_all | solution.py:515
  106.7 0.6 shard_map.75
  (3 shorter events, 0.0 us)
Async XLA Ops:
  2.3 20.5 %collective-permute-start = (bf16[32,2304]{1,0:T(8,128)(2,1)}, bf16[32,2304]{1,0:T(8,128)(2,1)S(1)}, u32[]{:S(2)}, u32[]{:S(2)}) collective-permute-start(bf16[32,2304]{1,0:T(8,128)(2,1)} %shard_map.68.c_ref), channel_id=1, source_target_pairs={{496,0},{0,16},{16,32},{32,48},{48,64},{64,80},{80,96},{96,112},{1... | collective-permute-start | bytes 442376 | tf_op jit(solution)/shard_map/ppermute | solution.py:447
  8.9 13.9 %collective-permute-start.1 = (bf16[32,2304]{1,0:T(8,128)(2,1)}, bf16[32,2304]{1,0:T(8,128)(2,1)S(1)}, u32[]{:S(2)}, u32[]{:S(2)}) collective-permute-start(bf16[32,2304]{1,0:T(8,128)(2,1)} %shard_map.68.c_ref), channel_id=1, source_target_pairs={{16,0},{32,16},{48,32},{64,48},{80,64},{96,80},{112,96},{128,112},... | collective-permute-start | bytes 442376 | tf_op jit(solution)/shard_map/ppermute | solution.py:447
  18.6 0.9 copy-start.1
  24.0 19.1 %copy-start = (bf16[2320,256]{1,0:T(8,128)(2,1)S(1)}, bf16[2320,256]{1,0:T(8,128)(2,1)}, u32[]{:S(2)}) copy-start(bf16[2320,256]{1,0:T(8,128)(2,1)} %constant.2.clone.w_ref) | copy-start | bytes 3563524
  43.2 13.6 %copy-start.2 = (bf16[4,32768]{1,0:T(4,128)(2,1)S(1)}, bf16[4,32768]{1,0:T(4,128)(2,1)}, u32[]{:S(2)}) copy-start(bf16[4,32768]{1,0:T(4,128)(2,1)} %param.6) | copy-start | bytes 786436
  46.0 14.1 %collective-permute-start.2 = (bf16[32,2048]{1,0:T(8,128)(2,1)S(1)}, bf16[32,2048]{1,0:T(8,128)(2,1)S(1)}, u32[]{:S(2)}, u32[]{:S(2)}) collective-permute-start(bf16[32,2048]{1,0:T(8,128)(2,1)S(1)} %get-tuple-element.12.c_ref), channel_id=1, source_target_pairs={{496,0},{0,16},{16,32},{32,48},{48,64},{64,80},{80,96},{96,112},{1... | collective-permute-start | bytes 393224 | tf_op jit(solution)/shard_map/ppermute | solution.py:447
  50.7 10.9 %collective-permute-start.3 = (bf16[32,2048]{1,0:T(8,128)(2,1)S(1)}, bf16[32,2048]{1,0:T(8,128)(2,1)S(1)}, u32[]{:S(2)}, u32[]{:S(2)}) collective-permute-start(bf16[32,2048]{1,0:T(8,128)(2,1)S(1)} %get-tuple-element.12.c_ref), channel_id=1, source_target_pairs={{16,0},{32,16},{48,32},{64,48},{80,64},{96,80},{112,96},{128,112},... | collective-permute-start | bytes 393224 | tf_op jit(solution)/shard_map/ppermute | solution.py:447
  90.5 16.2 %all-to-all-start.3 = ((f32[32,1,128]{2,1,0:T(1,128)}), f32[32,1,128]{2,1,0:T(1,128)S(1)}, u32[]{:S(2)}, u32[]{:S(2)}) async-start(f32[32,1,128]{2,1,0:T(1,128)} %bitcast.6), calls=%async_computation.3 | async-start | bytes 32768 | tf_op jit(solution)/shard_map/all_to_all | solution.py:515

commit v12 on v10

--- a/solution.py
+++ b/solution.py
@@ -382,7 +382,8 @@
     filter_step((l_ref, c_ref, r_ref), w_ref, g_ref, out_ref, here, there, half)
 
 
-def corr_kernel(factor, got, out_ref, pairs):
+def corr_kernel(factor, got, out_ref, filtered_ref, pairs):
+    filtered_ref[...] = got[:, :NODES_DEV]
     four = jnp.concatenate([got[:, :NODES_DEV]] * 4, axis=0)
     parts = [
         lax.dot_general(
@@ -492,11 +493,10 @@
         scratch,
     )
     got = lax.all_to_all(block, "bands", 0, 0, tiled=True)
-    filtered = got[:, :NODES_DEV]
-    (partial,) = call(
+    partial, filtered = call(
         functools.partial(corr_kernel, factor),
         (got,),
-        [shape((64, 128), f32)],
+        [shape((64, 128), f32), shape((NWF, NODES_DEV), bf)],
         [pltpu.VMEM((NWF, 128), f32)],
     )
     planes = [list(range(at, at + 64)) for at in range(0, n_cells * n_bands, 64)]

time: 108 us -> 107 us (level)
  blocking collectives: 46.6 us -> 59.8 us
  starting transfers between devices: 34 us -> 27.1 us
  waiting for transfers between devices: 12.8 us -> 6.99 us
    all_to_all x0 -> x1, blocking collectives: none -> 13.2 us  [shards(): lax.all_to_all(partial, 'cells', 0, 0, tiled=True, axis_index_groups=colu...]
    all_to_all x1 -> x0, starting transfers between devices: 6.9 us -> none  [shards(): lax.all_to_all(partial, 'cells', 0, 0, tiled=True, axis_index_groups=colu...]
    all_to_all x1 -> x0, waiting for transfers between devices: 5.85 us -> none  [shards(): lax.all_to_all(partial, 'cells', 0, 0, tiled=True, axis_index_groups=colu...]
  transfers between devices with their start and end apart: 5 -> 4, of which waited for: 4 -> 3; matrix products, arithmetic and copies ran while one was open for 1% -> 0% of each run, Pallas kernels for 1% -> 1%
where the time goes in v12:
time: 107 us
  blocking collectives  59.8 us (56%)
  starting transfers between devices  27.1 us (25%)
  Pallas kernels  9.8 us (9%)
  waiting for transfers between devices  6.99 us (7%)
  local copies, waits for them, and re-layouts  2.35 us (2%)
    ppermute x4, starting transfers between devices, passed_along(): return lax.ppermute(block, axis, route)  27.1 us
    all_to_all x1, blocking collectives, shards(): got = lax.all_to_all(payload, 'bands', 0, 0, tiled=True)  18.9 us
    all_to_all x1, blocking collectives, shards(): lax.all_to_all(partial, ('cells', 'bands'), 0, 0, tiled=True, axis_index_...  15.6 us
    all_to_all x1, blocking collectives, shards(): lax.all_to_all(partial, 'cells', 0, 0, tiled=True, axis_index_groups=colu...  13.2 us
    all_to_all x1, blocking collectives, shards(): got = lax.all_to_all(block, 'bands', 0, 0, tiled=True)  12.2 us
    pallas_call x8, Pallas kernels, call(): pl.pallas_call(kernel, grid=(1,), in_specs=[full(a.shape) for a in args]...  9.8 us
    ppermute x4, waiting for transfers between devices, passed_along(): return lax.ppermute(block, axis, route)  6.99 us
  transfers between devices with their start and end apart: 4, of which 3 were waited for; matrix products, arithmetic and copies ran while one was open for 0% of the time, Pallas kernels for 1%

profile of v12, /device:TPU:1, one launch (start us, length us, event | category | flops | bytes accessed | tf_op | source)
XLA Modules:
  0.0 106.8 jit_solution(15312781608267539406)
XLA Ops:
  0.6 1.6 %shard_map.68.c_ref = bf16[32,2304]{1,0:T(8,128)(2,1)} custom-call(bf16[32,2048]{1,0:T(8,128)(2,1)} %v_hbm.1, f32[32,125]{1,0:T(8,128)} %bitcast.26, s32[32,125]{1,0:T(8,128)} %bitcast.27), custom_call_target="tpu_custom_call" | custom-call | tf_op jit(solution)/shard_map/pallas_call | solution.py:428
  2.2 6.6 %collective-permute-start = (bf16[32,2304]{1,0:T(8,128)(2,1)}, bf16[32,2304]{1,0:T(8,128)(2,1)S(1)}, u32[]{:S(2)}, u32[]{:S(2)}) collective-permute-start(bf16[32,2304]{1,0:T(8,128)(2,1)} %shard_map.68.c_ref), channel_id=1, source_target_pairs={{496,0},{0,16},{16,32},{32,48},{48,64},{64,80},{80,96},{96,112},{1... | collective-permute-start | bytes 442376 | tf_op jit(solution)/shard_map/ppermute | solution.py:442
  8.9 9.7 %collective-permute-start.1 = (bf16[32,2304]{1,0:T(8,128)(2,1)}, bf16[32,2304]{1,0:T(8,128)(2,1)S(1)}, u32[]{:S(2)}, u32[]{:S(2)}) collective-permute-start(bf16[32,2304]{1,0:T(8,128)(2,1)} %shard_map.68.c_ref), channel_id=1, source_target_pairs={{16,0},{32,16},{48,32},{64,48},{80,64},{96,80},{112,96},{128,112},... | collective-permute-start | bytes 442376 | tf_op jit(solution)/shard_map/ppermute | solution.py:442
  18.6 0.0 copy-start.1
  18.6 0.9 copy-done.1
  19.5 0.6 shard_map.69
  20.1 2.7 %collective-permute-done.l_ref = bf16[32,2304]{1,0:T(8,128)(2,1)S(1)} collective-permute-done((bf16[32,2304]{1,0:T(8,128)(2,1)}, bf16[32,2304]{1,0:T(8,128)(2,1)S(1)}, u32[]{:S(2)}, u32[]{:S(2)}) %collective-permute-start) | collective-permute-done | bytes 147488 | tf_op jit(solution)/shard_map/ppermute | solution.py:442
  22.8 0.0 collective-permute-done.1.r_ref
  22.8 1.0 shard_map.70
  23.8 0.3 all_to_all.28
  24.0 0.0 copy-start
  24.0 18.9 %all_to_all.44 = bf16[16,2,10496]{2,1,0:T(2,128)(2,1)S(1)} all-to-all(bf16[16,2,10496]{2,1,0:T(2,128)(2,1)S(1)} %all_to_all.28), channel_id=1, replica_groups=mesh['cells'=32,'bands'=16] {'bands'}, dimensions={0} | all-to-all | bytes 1343488 | tf_op jit(solution)/shard_map/all_to_all | solution.py:475
  42.9 0.3 all_to_all.30.got
  43.1 0.0 copy-done
  43.2 0.0 copy-start.2
  43.2 2.7 %shard_map.71 = (bf16[32,2048]{1,0:T(8,128)(2,1)S(1)}, f32[8,3,32,256]{3,2,1,0:T(8,128)S(1)}) custom-call(bf16[32,10496]{1,0:T(8,128)(2,1)S(1)} %all_to_all.30.got, bf16[2320,256]{1,0:T(8,128)(2,1)S(1)} %copy-done), custom_call_target="tpu_custom_call" | custom-call | tf_op jit(solution)/shard_map/pallas_call | solution.py:428
  45.9 4.7 %collective-permute-start.2 = (bf16[32,2048]{1,0:T(8,128)(2,1)S(1)}, bf16[32,2048]{1,0:T(8,128)(2,1)S(1)}, u32[]{:S(2)}, u32[]{:S(2)}) collective-permute-start(bf16[32,2048]{1,0:T(8,128)(2,1)S(1)} %get-tuple-element.14.c_ref), channel_id=1, source_target_pairs={{496,0},{0,16},{16,32},{32,48},{48,64},{64,80},{80,96},{96,112},{1... | collective-permute-start | bytes 393224 | tf_op jit(solution)/shard_map/ppermute | solution.py:442
  50.6 6.1 %collective-permute-start.3 = (bf16[32,2048]{1,0:T(8,128)(2,1)S(1)}, bf16[32,2048]{1,0:T(8,128)(2,1)S(1)}, u32[]{:S(2)}, u32[]{:S(2)}) collective-permute-start(bf16[32,2048]{1,0:T(8,128)(2,1)S(1)} %get-tuple-element.14.c_ref), channel_id=1, source_target_pairs={{16,0},{32,16},{48,32},{64,48},{80,64},{96,80},{112,96},{128,112},... | collective-permute-start | bytes 393224 | tf_op jit(solution)/shard_map/ppermute | solution.py:442
  56.7 0.0 copy-done.2
  56.7 0.2 copy.11
  56.9 0.3 copy.8
  57.2 0.1 copy.12
  57.2 2.8 %collective-permute-done.2.l_ref = bf16[32,2048]{1,0:T(8,128)(2,1)S(1)} collective-permute-done((bf16[32,2048]{1,0:T(8,128)(2,1)S(1)}, bf16[32,2048]{1,0:T(8,128)(2,1)S(1)}, u32[]{:S(2)}, u32[]{:S(2)}) %collective-permute-start.2) | collective-permute-done | bytes 131104 | tf_op jit(solution)/shard_map/ppermute | solution.py:442
  60.0 1.5 %collective-permute-done.3.r_ref = bf16[32,2048]{1,0:T(8,128)(2,1)S(1)} collective-permute-done((bf16[32,2048]{1,0:T(8,128)(2,1)S(1)}, bf16[32,2048]{1,0:T(8,128)(2,1)S(1)}, u32[]{:S(2)}, u32[]{:S(2)}) %collective-permute-start.3) | collective-permute-done | bytes 131104 | tf_op jit(solution)/shard_map/ppermute | solution.py:442
  61.5 2.3 %shard_map.72 = bf16[32,6144]{1,0:T(8,128)(2,1)S(1)} custom-call(bf16[32,2048]{1,0:T(8,128)(2,1)S(1)} %get-tuple-element.14.c_ref, bf16[32,2048]{1,0:T(8,128)(2,1)S(1)} %collective-permute-done.2.l_ref, bf16[32,2048]{1,0:T(8,128)(2,1)S(1)} %collective-permute-done.3.r_ref, f32[8,3,32,256]{3,2,1,0:T(8,128)S(1)} %get-tuple-element.15.g_ref, ...), custom_call_target="tpu_custom_call" | custom-call | tf_op jit(solution)/shard_map/pallas_call | solution.py:428
  63.9 0.3 all_to_all.31
  64.1 12.2 %all_to_all.45 = bf16[16,2,6144]{2,1,0:T(2,128)(2,1)S(1)} all-to-all(bf16[16,2,6144]{2,1,0:T(2,128)(2,1)S(1)} %all_to_all.31), channel_id=1, replica_groups=mesh['cells'=32,'bands'=16] {'bands'}, dimensions={0} | all-to-all | bytes 786432 | tf_op jit(solution)/shard_map/all_to_all | solution.py:495
  76.3 0.1 all_to_all.33.got
  76.5 1.0 shard_map.73
  77.4 15.6 %all_to_all.46 = f32[64,1,128]{2,1,0:T(1,128)S(1)} all-to-all(f32[64,1,128]{2,1,0:T(1,128)S(1)} %bitcast.20), channel_id=1, replica_groups={{0,1,2,3,4,5,6,7,8,9,10,11,12,13,14,15,16,17,18,19,20,21,22,23,24,25,26..., dimensions={0} | all-to-all | bytes 65536 | tf_op jit(solution)/shard_map/all_to_all | solution.py:504
  93.0 13.2 %all_to_all.47 = f32[8,1,128]{2,1,0:T(1,128)S(1)} all-to-all(f32[8,1,128]{2,1,0:T(1,128)S(1)} %bitcast.21), channel_id=1, replica_groups={{0,64,128,192,256,320,384,448},{16,80,144,208,272,336,400,464},{32,96,1..., dimensions={0} | all-to-all | bytes 8192 | tf_op jit(solution)/shard_map/all_to_all | solution.py:506
  106.2 0.6 shard_map.75
  (1 shorter events, 0.0 us)
Async XLA Ops:
  2.2 20.5 %collective-permute-start = (bf16[32,2304]{1,0:T(8,128)(2,1)}, bf16[32,2304]{1,0:T(8,128)(2,1)S(1)}, u32[]{:S(2)}, u32[]{:S(2)}) collective-permute-start(bf16[32,2304]{1,0:T(8,128)(2,1)} %shard_map.68.c_ref), channel_id=1, source_target_pairs={{496,0},{0,16},{16,32},{32,48},{48,64},{64,80},{80,96},{96,112},{1... | collective-permute-start | bytes 442376 | tf_op jit(solution)/shard_map/ppermute | solution.py:442
  8.9 13.9 %collective-permute-start.1 = (bf16[32,2304]{1,0:T(8,128)(2,1)}, bf16[32,2304]{1,0:T(8,128)(2,1)S(1)}, u32[]{:S(2)}, u32[]{:S(2)}) collective-permute-start(bf16[32,2304]{1,0:T(8,128)(2,1)} %shard_map.68.c_ref), channel_id=1, source_target_pairs={{16,0},{32,16},{48,32},{64,48},{80,64},{96,80},{112,96},{128,112},... | collective-permute-start | bytes 442376 | tf_op jit(solution)/shard_map/ppermute | solution.py:442
  18.6 0.9 copy-start.1
  24.0 19.1 %copy-start = (bf16[2320,256]{1,0:T(8,128)(2,1)S(1)}, bf16[2320,256]{1,0:T(8,128)(2,1)}, u32[]{:S(2)}) copy-start(bf16[2320,256]{1,0:T(8,128)(2,1)} %constant.2.clone.w_ref) | copy-start | bytes 3563524
  43.2 13.6 %copy-start.2 = (bf16[4,32768]{1,0:T(4,128)(2,1)S(1)}, bf16[4,32768]{1,0:T(4,128)(2,1)}, u32[]{:S(2)}) copy-start(bf16[4,32768]{1,0:T(4,128)(2,1)} %param.6) | copy-start | bytes 786436
  45.9 14.1 %collective-permute-start.2 = (bf16[32,2048]{1,0:T(8,128)(2,1)S(1)}, bf16[32,2048]{1,0:T(8,128)(2,1)S(1)}, u32[]{:S(2)}, u32[]{:S(2)}) collective-permute-start(bf16[32,2048]{1,0:T(8,128)(2,1)S(1)} %get-tuple-element.14.c_ref), channel_id=1, source_target_pairs={{496,0},{0,16},{16,32},{32,48},{48,64},{64,80},{80,96},{96,112},{1... | collective-permute-start | bytes 393224 | tf_op jit(solution)/shard_map/ppermute | solution.py:442
  50.6 10.9 %collective-permute-start.3 = (bf16[32,2048]{1,0:T(8,128)(2,1)S(1)}, bf16[32,2048]{1,0:T(8,128)(2,1)S(1)}, u32[]{:S(2)}, u32[]{:S(2)}) collective-permute-start(bf16[32,2048]{1,0:T(8,128)(2,1)S(1)} %get-tuple-element.14.c_ref), channel_id=1, source_target_pairs={{16,0},{32,16},{48,32},{64,48},{80,64},{96,80},{112,96},{128,112},... | collective-permute-start | bytes 393224 | tf_op jit(solution)/shard_map/ppermute | solution.py:442
